TPU v7x, 128 devices: a whole 4x4x4 slice. The times are simulated.
128 devices in a mesh: pipe: 8 (over z_hi, x), dp: 4 (over z_lo, core), tensor: 4 (over y).
Axes of the slice: x: 4, y: 4, z: 4 (z_hi: 2, z_lo: 2; z = z_hi * 2 + z_lo), core: 2. Of those that a mesh axis runs over, the one named last changes fastest.
Arguments:
- act_in: bfloat16 [8, 512, 4096], P('pipe', ('dp', 'tensor')), may hold values from -6 to 6
- act_first: bfloat16 [512, 4096], P(('dp', 'tensor')), may hold values from -6 to 6
- grad_in: bfloat16 [8, 512, 4096], P('pipe', ('dp', 'tensor')), may hold values from -1.5 to 1.5
- grad_last: bfloat16 [512, 4096], P(('dp', 'tensor')), may hold values from -1.5 to 1.5
- stash_local: bfloat16 [8, 2, 512, 4096], P('pipe', None, ('dp', 'tensor')), may hold values from -6 to 6
- stash_guest: bfloat16 [8, 2, 3, 512, 512], P('pipe', None, None, ('dp', 'tensor')), may hold values from -6 to 6
- plan: int32 [2, 2, 4, 4], replicated, may hold values from 0 to 7, as said below
- norm_gain: float32 [8, 4096], P('pipe'), may hold values from 0.25 to 1.75
- w_up: bfloat16 [8, 4096, 11264], P('pipe', 'dp', 'tensor'), may hold values from -0.09375 to 0.09375
- w_down: bfloat16 [8, 11264, 4096], P('pipe', 'tensor', 'dp'), may hold values from -0.0546875 to 0.0546875
Outputs:
- act_out: bfloat16 [8, 2, 512, 4096], P('pipe', None, ('dp', 'tensor'))
- grad_out: bfloat16 [8, 2, 512, 4096], P('pipe', None, ('dp', 'tensor'))
- keep_out: bfloat16 [8, 2, 512, 4096], P('pipe', None, ('dp', 'tensor'))
- guest_out: bfloat16 [8, 2, 3, 512, 512], P('pipe', None, None, ('dp', 'tensor'))
- grad_up: bfloat16 [8, 4096, 11264], P('pipe', 'dp', 'tensor')
- grad_down: bfloat16 [8, 11264, 4096], P('pipe', 'tensor', 'dp')
- grad_gain: float32 [8, 4096], P('pipe')
Inputs may be any that keep to these rules, and one draw needn't show every extreme that they name: For each first index o and tick m, plan[o, m, s, 0] over s = 0 .. 3 is a permutation of 0 .. 3, with plan[o, 0, 3, 0] = 0, and plan[o, m, s, 1 ..] are 3 distinct block ids below 8.
All inputs are finite; a program needn't handle non-finite values.
Results may differ from a plain program's by a relative error of at most 0.02.
Values may be sent and summed in bfloat16 or wider, within the bound.
No kernel may reach another device: no remote copies, remote signals or barrier semaphores. Data moves between devices by JAX's collectives and lax.ppermute only.
A program may use at most 192 MiB of HBM per device.

v0:
```python
import jax
import jax.numpy as jnp
from jax import lax
from jax.sharding import PartitionSpec as P

MICRO = 2


EPSILON = 1e-05


def in_blocks(shard, dim, devices):
    before, after = (shard.shape[:dim], shard.shape[dim + 1 :])
    return jnp.moveaxis(shard.reshape(*before, devices, -1, *after), dim, 0)


def sum_at_owner(shard, axis, dim):
    devices = lax.axis_size(axis)
    blocks = lax.all_to_all(in_blocks(shard, dim, devices), axis, 0, 0, tiled=True)
    return jnp.sum(blocks.astype(jnp.float32), axis=0)


def laid_out(blocks, dim):
    lengths = list(blocks.shape[1:])
    lengths[dim] *= blocks.shape[0]
    return jnp.moveaxis(blocks, 0, dim).reshape(lengths)


def from_everyone(shard, axis):
    copies = jnp.broadcast_to(shard, (lax.axis_size(axis), *shard.shape))
    return lax.all_to_all(copies, axis, split_axis=0, concat_axis=0, tiled=True)


def collect(shard, axis, dim):
    return laid_out(from_everyone(shard, axis), dim)


def side_by_side(arrays, axis, dim, along):
    both = jnp.concatenate(arrays, axis=along)
    filled, at, finished = (lax.all_gather(both, axis, axis=dim, tiled=True), 0, [])
    for a in arrays:
        finished.append(lax.slice_in_dim(filled, at, at + a.shape[along], axis=along))
        at += a.shape[along]
    return tuple(finished)


def passed_along(value, axis, steps):
    count = lax.axis_size(axis)
    first, last = (max(0, -steps), min(count, count - steps))
    return lax.ppermute(value, axis, [(source, source + steps) for source in range(first, last)])


def over_copies(shard, axis):
    everything = from_everyone(shard, axis)
    return jnp.sum(everything, axis=0)


def normalize(values, norm_scale):
    wide = values.astype(jnp.float32)
    inverse_rms = lax.rsqrt(jnp.mean(wide * wide, axis=-1, keepdims=True) + EPSILON)
    return (wide, inverse_rms, wide * inverse_rms * norm_scale)


def finish_norm(wide, inverse_rms, norm_scale, d_normed, cotangent):
    scaled = d_normed * norm_scale
    d_input = (
        cotangent.astype(jnp.float32)
        + inverse_rms * scaled
        - wide
        * (inverse_rms * inverse_rms * inverse_rms)
        * jnp.mean(scaled * wide, axis=-1, keepdims=True)
    )
    return (d_input.astype(jnp.bfloat16), jnp.sum(d_normed * wide * inverse_rms, axis=0))


def match_blocks(block_ids, block_count):
    return block_ids[:, None] == jnp.arange(block_count, dtype=jnp.int32)[None, :]


def pull_blocks(values, block_ids, block_width):
    row_total = values.shape[0]
    blocks = values.reshape(row_total, values.shape[1] // block_width, block_width)
    count = block_ids.shape[0]
    picked = [
        lax.dynamic_slice_in_dim(blocks, block_ids[e], 1, axis=1)[:, 0] for e in range(count)
    ]
    return jnp.stack(picked)


def clear_blocks(values, block_ids, block_width):
    row_total = values.shape[0]
    block_count = values.shape[1] // block_width
    covered = jnp.any(match_blocks(block_ids, block_count), axis=0)
    blocks = values.reshape(row_total, block_count, block_width)
    return jnp.where(covered[None, :, None], jnp.zeros((), values.dtype), blocks).reshape(
        values.shape
    )


def place_blocks(values, block_ids, fetched):
    row_total = values.shape[0]
    block_width = fetched.shape[2]
    block_count = values.shape[1] // block_width
    matched = match_blocks(block_ids, block_count)
    covered = jnp.any(matched, axis=0)
    fetched_cols = jnp.einsum(
        "eb,erw->rbw", matched.astype(jnp.float32), fetched.astype(jnp.float32)
    )
    blocks = values.reshape(row_total, block_count, block_width).astype(jnp.float32)
    return (
        jnp.where(covered[None, :, None], fetched_cols, blocks)
        .reshape(values.shape)
        .astype(values.dtype)
    )


def settle(partial_value, row_count):
    data_count = lax.axis_size("dp")
    tensor_count = lax.axis_size("tensor")
    shaped = partial_value.reshape(data_count, tensor_count, row_count, partial_value.shape[1])
    reduced = sum_at_owner(shaped.astype(jnp.bfloat16), "tensor", 1)
    placed = lax.all_to_all(
        reduced.astype(jnp.bfloat16), "dp", split_axis=0, concat_axis=3, tiled=True
    ).astype(reduced.dtype)
    return placed.reshape(row_count, placed.shape[3])


def forward_pass(values, norm_scale, up_matrix, down_matrix):
    wide, inverse_rms, normed = normalize(values, norm_scale)
    normed_low = normed.astype(jnp.bfloat16)
    replica_rows = collect(normed_low, "tensor", 0)
    row_block = lax.all_to_all(replica_rows, "dp", split_axis=1, concat_axis=0, tiled=True)
    hidden_pre = sum_at_owner(
        jnp.dot(row_block, up_matrix, preferred_element_type=jnp.float32).astype(jnp.bfloat16),
        "dp",
        0,
    )
    hidden = jax.nn.silu(hidden_pre).astype(jnp.bfloat16)
    partial_value = jnp.dot(
        lax.all_gather(hidden, "dp", axis=0, tiled=True),
        down_matrix,
        preferred_element_type=jnp.float32,
    )
    summed = settle(partial_value, values.shape[0])
    return (wide + summed).astype(jnp.bfloat16)


def backward_pass(values, cotangent, norm_scale, up_matrix, down_matrix, grad_pair):
    wide, inverse_rms, normed = normalize(values, norm_scale)
    normed_low = normed.astype(jnp.bfloat16)
    replica_normed, replica_cotan = side_by_side((normed_low, cotangent), "tensor", 0, 1)
    normed_block, cotan_block = (
        lax.all_to_all(replica_normed, "dp", split_axis=1, concat_axis=0, tiled=True),
        lax.all_to_all(replica_cotan, "dp", split_axis=1, concat_axis=0, tiled=True),
    )
    hidden_width = up_matrix.shape[1]
    pre_part = jnp.dot(normed_block, up_matrix, preferred_element_type=jnp.float32)
    back_part = lax.dot_general(
        cotan_block, down_matrix, (((1,), (1,)), ((), ())), preferred_element_type=jnp.float32
    )
    joined = lax.psum_scatter(
        jnp.concatenate([pre_part, back_part], axis=1).astype(jnp.bfloat16),
        "dp",
        scatter_dimension=0,
        tiled=True,
    ).astype(jnp.float32)
    hidden_pre = joined[:, :hidden_width]
    d_hidden = joined[:, hidden_width:]
    sigmoid_gate = jax.nn.sigmoid(hidden_pre)
    hidden = jax.nn.silu(hidden_pre).astype(jnp.bfloat16)
    d_pre = (d_hidden * sigmoid_gate * (1.0 + hidden_pre * (1.0 - sigmoid_gate))).astype(
        jnp.bfloat16
    )
    grad_up_acc = grad_pair[0]
    grad_down_acc = grad_pair[1]
    hidden_piece = lax.all_gather(hidden, "dp", axis=0, tiled=True)
    d_pre_piece = lax.all_gather(d_pre, "dp", axis=0, tiled=True)
    grad_up_acc = grad_up_acc + lax.dot_general(
        normed_block, d_pre_piece, (((0,), (0,)), ((), ())), preferred_element_type=jnp.float32
    )
    grad_down_acc = grad_down_acc + lax.dot_general(
        hidden_piece, cotan_block, (((0,), (0,)), ((), ())), preferred_element_type=jnp.float32
    )
    normed_part = lax.dot_general(
        d_pre_piece, up_matrix, (((1,), (1,)), ((), ())), preferred_element_type=jnp.float32
    )
    normed_grad = normed_part
    grad_up_acc, grad_down_acc, normed_grad = (grad_up_acc, grad_down_acc, normed_grad)
    d_normed = settle(normed_grad, values.shape[0])
    d_input, gain_part = finish_norm(wide, inverse_rms, norm_scale, d_normed, cotangent)
    return (d_input, gain_part, (grad_up_acc, grad_down_acc))


def local(
    act_in, act_first, grad_in, grad_last, stash_local, stash_guest, plan, norm_gain, w_up, w_down
):
    section_count = lax.axis_size("pipe")
    half_sections = section_count // 2
    section_index = lax.axis_index("pipe")
    is_early = section_index < half_sections
    plan_row = jnp.minimum(section_index, half_sections - 1)
    block_width = stash_guest.shape[-1]
    norm_scale = norm_gain[0]
    up_matrix = w_up[0]
    down_matrix = w_down[0]
    section_ids = jnp.arange(section_count, dtype=jnp.int32)
    clipped_ids = jnp.minimum(section_ids, half_sections - 1)
    section_early = section_ids < half_sections
    zero_low = jnp.zeros((), jnp.bfloat16)
    old_holder = plan[0, :, :, 0] + half_sections
    sends_back = section_early[:, None] & (
        jnp.transpose(old_holder[:, clipped_ids]) == section_index
    )
    outgoing = jnp.where(sends_back[:, :, None, None, None], stash_guest[0][None], zero_low)
    source_pick = section_ids[:, None] == old_holder[:, plan_row][None, :]
    arrived = lax.all_to_all(outgoing, "pipe", split_axis=0, concat_axis=0, tiled=True)
    fetched_all = jnp.sum(jnp.where(source_pick[:, :, None, None, None], arrived, zero_low), axis=0)
    fetched_list = [fetched_all[tick] for tick in range(MICRO)]
    stash_rows = []
    for tick in range(MICRO):
        own = stash_local[0, tick]
        merged = place_blocks(own, plan[0, tick, plan_row, 1:], fetched_list[tick])
        stash_rows.append(jnp.where(is_early, merged, own))
    front_zero = forward_pass(act_in[0], norm_scale, up_matrix, down_matrix)
    passed = passed_along(front_zero, "pipe", 1)
    input_one = jnp.where(section_index == 0, act_first, passed)
    front_one = forward_pass(input_one, norm_scale, up_matrix, down_matrix)
    empty_pair = (
        jnp.zeros(up_matrix.shape, jnp.float32),
        jnp.zeros(down_matrix.shape, jnp.float32),
    )
    back_zero = backward_pass(
        stash_rows[0], grad_in[0], norm_scale, up_matrix, down_matrix, empty_pair
    )
    returned = passed_along(back_zero[0], "pipe", -1)
    cot_one = jnp.where(section_index == section_count - 1, grad_last, returned)
    back_one = backward_pass(
        stash_rows[1], cot_one, norm_scale, up_matrix, down_matrix, back_zero[2]
    )
    gain_grad = over_copies(back_zero[1] + back_one[1], ("dp", "tensor"))
    new_inputs = [act_in[0], input_one]
    new_holder = plan[1, :, :, 0] + half_sections
    pulled = jnp.stack(
        [
            pull_blocks(new_inputs[tick], plan[1, tick, plan_row, 1:], block_width)
            for tick in range(MICRO)
        ]
    )
    heading = is_early & (section_ids[:, None] == new_holder[:, plan_row][None, :])
    parcels = jnp.where(heading[:, :, None, None, None], pulled[None], zero_low)
    landed = lax.all_to_all(parcels, "pipe", split_axis=0, concat_axis=0, tiled=True)
    coming = section_early[:, None] & (jnp.transpose(new_holder[:, clipped_ids]) == section_index)
    guest_new = jnp.sum(jnp.where(coming[:, :, None, None, None], landed, zero_low), axis=0)
    kept = jnp.stack(
        [
            jnp.where(
                is_early,
                clear_blocks(new_inputs[tick], plan[1, tick, plan_row, 1:], block_width),
                new_inputs[tick],
            )
            for tick in range(MICRO)
        ]
    )
    act_out = jnp.stack([front_zero, front_one])[None]
    grad_out = jnp.stack([back_zero[0], back_one[0]])[None]
    grad_up = back_one[2][0].astype(jnp.bfloat16)[None]
    grad_down = back_one[2][1].astype(jnp.bfloat16)[None]
    return (act_out, grad_out, kept[None], guest_new[None], grad_up, grad_down, gain_grad[None])


def solution(mesh):
    placed = (
        P("pipe", ("dp", "tensor"), None),
        P(("dp", "tensor"), None),
        P("pipe", ("dp", "tensor"), None),
        P(("dp", "tensor"), None),
        P("pipe", None, ("dp", "tensor"), None),
        P("pipe", None, None, ("dp", "tensor"), None),
        P(),
        P("pipe", None),
        P("pipe", "dp", "tensor"),
        P("pipe", "tensor", "dp"),
    )
    return jax.shard_map(
        local,
        mesh=mesh,
        in_specs=placed,
        out_specs=(
            P("pipe", None, ("dp", "tensor"), None),
            P("pipe", None, ("dp", "tensor"), None),
            P("pipe", None, ("dp", "tensor"), None),
            P("pipe", None, None, ("dp", "tensor"), None),
            P("pipe", "dp", "tensor"),
            P("pipe", "tensor", "dp"),
            P("pipe", None),
        ),
        check_vma=False,
    )
```

profile of v0, /device:TPU:64, one launch (start us, length us, event | category | flops | bytes accessed | tf_op | source)
XLA Modules:
  0.0 800.7 jit_solution(7578637422950112370)
XLA Ops:
  9.4 2.2 broadcast_select_fusion.1
  11.6 7.4 all-to-all-start.10
  21.3 17.6 %all-to-all-done.10 = bf16[8,2,3,32,512]{4,3,2,1,0:T(8,128)(2,1)S(1)} async-done(((bf16[8,2,3,32,512]{4,3,2,1,0:T(8,128)(2,1)}), bf16[8,2,3,32,512]{4,3,2,1,0:T(8,128)(2,1)S(1)}, u32[]{:S(2)}, u32[]{:S(2)}) %all-to-all-start.10) | async-done | bytes 1572896 | tf_op jit(solution)/shard_map/all_to_all | solution.py:216
  44.0 31.2 %all-gather.13.cloned.1.call-done = bf16[128,8192]{1,0:T(8,128)(2,1)} async-done(((bf16[32,8192]{1,0:T(8,128)(2,1)}), bf16[128,8192]{1,0:T(8,128)(2,1)}) %all-gather.13.cloned.1.call-update) | async-done | bytes 2097168 | tf_op jit(solution)/shard_map/all_gather | solution.py:40
  78.2 3.5 all-to-all-start.12
  83.1 13.1 %all-to-all-done.12 = bf16[128,4,1024]{0,2,1:T(8,128)(2,1)S(1)} async-done(((bf16[128,4,1024]{0,2,1:T(8,128)(2,1)}), bf16[128,4,1024]{0,2,1:T(8,128)(2,1)S(1)}, u32[]{:S(2)}, u32[]{:S(2)}) %all-to-all-start.12) | async-done | bytes 1048608 | tf_op jit(solution)/shard_map/all_to_all | solution.py:154
  96.2 3.5 all-to-all-start.11
  101.1 13.1 %all-to-all-done.11 = bf16[128,4,1024]{0,2,1:T(8,128)(2,1)S(1)} async-done(((bf16[128,4,1024]{0,2,1:T(8,128)(2,1)}), bf16[128,4,1024]{0,2,1:T(8,128)(2,1)S(1)}, u32[]{:S(2)}, u32[]{:S(2)}) %all-to-all-start.11) | async-done | bytes 1048608 | tf_op jit(solution)/shard_map/all_to_all | solution.py:153
  114.7 6.5 fusion.34
  121.2 6.0 fusion.28
  127.2 3.0 pad_maximum_fusion
  130.3 58.1 %reduce-scatter.3.cloned.1.call-done = bf16[128,5632]{1,0:T(8,128)(2,1)} async-done(((bf16[512,5632]{1,0:T(8,128)(2,1)}), bf16[128,5632]{1,0:T(8,128)(2,1)}) %reduce-scatter.3.cloned.1.call-update) | async-done | bytes 1441808 | tf_op jit(solution)/shard_map/reduce_scatter | solution.py:161
  191.7 36.5 %all-gather.15.cloned.1.call-done = bf16[512,2816]{1,0:T(8,128)(2,1)} async-done(((bf16[128,2816]{1,0:T(8,128)(2,1)}), bf16[512,2816]{1,0:T(8,128)(2,1)}) %all-gather.15.cloned.1.call-update) | async-done | bytes 2883600 | tf_op jit(solution)/shard_map/all_gather | solution.py:177
  228.2 6.7 fusion.59
  235.0 19.9 %all_to_all.206 = bf16[4,4,1,32,1024]{4,3,1,2,0:T(8,128)(2,1)S(1)} all-to-all(bf16[4,4,1,32,1024]{4,3,1,2,0:T(8,128)(2,1)S(1)} %copy.176), channel_id=1, replica_groups=mesh['pipe'=8,'dp'=4,'tensor'=4] {'tensor'}, dimensions={0} | all-to-all | bytes 2097152 | tf_op jit(solution)/shard_map/all_to_all | solution.py:19
  255.8 3.4 all-to-all-start.14
  261.2 4.1 all-to-all-done.14
  266.5 4.7 collective-permute-start.1
  271.2 5.3 collective-permute-done.1
  278.1 31.2 %all-gather.17.cloned.1.call-done = bf16[128,8192]{1,0:T(8,128)(2,1)} async-done(((bf16[32,8192]{1,0:T(8,128)(2,1)}), bf16[128,8192]{1,0:T(8,128)(2,1)}) %all-gather.17.cloned.1.call-update) | async-done | bytes 2097168 | tf_op jit(solution)/shard_map/all_gather | solution.py:40
  312.3 3.5 all-to-all-start.16
  317.2 13.1 %all-to-all-done.16 = bf16[128,4,1024]{0,2,1:T(8,128)(2,1)S(1)} async-done(((bf16[128,4,1024]{0,2,1:T(8,128)(2,1)}), bf16[128,4,1024]{0,2,1:T(8,128)(2,1)S(1)}, u32[]{:S(2)}, u32[]{:S(2)}) %all-to-all-start.16) | async-done | bytes 1048608 | tf_op jit(solution)/shard_map/all_to_all | solution.py:154
  330.3 3.5 all-to-all-start.15
  335.2 7.7 fusion.37
  342.9 5.3 all-to-all-done.15
  348.8 6.4 fusion.31
  355.2 3.0 pad_maximum_fusion.1
  359.2 17.7 %all_to_all.207 = bf16[4,32,4096]{2,1,0:T(8,128)(2,1)S(1)} all-to-all(bf16[4,32,4096]{2,1,0:T(8,128)(2,1)S(1)} %broadcast_in_dim.145), channel_id=1, replica_groups=mesh['pipe'=8,'dp'=4,'tensor'=4] {'tensor'}, dimensions={0} | all-to-all | bytes 2097152 | tf_op jit(solution)/shard_map/all_to_all | solution.py:31
  378.1 28.4 %all_to_all.208 = bf16[128,4,1024]{2,0,1:T(8,128)(2,1)S(1)} all-to-all(bf16[128,4,1024]{2,0,1:T(8,128)(2,1)S(1)} %copy.159), channel_id=1, replica_groups=mesh['pipe'=8,'dp'=4,'tensor'=4] {'dp'}, dimensions={1} | all-to-all | bytes 2097152 | tf_op jit(solution)/shard_map/all_to_all | solution.py:132
  406.5 6.0 fusion.22
  412.5 44.6 %all_to_all.209 = bf16[4,128,2816]{2,1,0:T(8,128)(2,1)S(1)} all-to-all(bf16[4,128,2816]{2,1,0:T(8,128)(2,1)S(1)} %bitcast.334), channel_id=1, replica_groups=mesh['pipe'=8,'dp'=4,'tensor'=4] {'dp'}, dimensions={0} | all-to-all | bytes 5767168 | tf_op jit(solution)/shard_map/all_to_all | solution.py:19
  462.4 32.9 %all-gather.9.cloned.1.call-done = bf16[512,2816]{1,0:T(8,128)(2,1)} async-done(((bf16[128,2816]{1,0:T(8,128)(2,1)}), bf16[512,2816]{1,0:T(8,128)(2,1)}) %all-gather.9.cloned.1.call-update) | async-done | bytes 2883600 | tf_op jit(solution)/shard_map/all_gather | solution.py:140
  495.3 6.6 fusion.65
  503.0 4.3 all-to-all-start.3
  507.4 15.7 %all-to-all-done.3 = bf16[4,4,1,32,1024]{4,3,1,2,0:T(8,128)(2,1)S(1)} async-done(((bf16[4,4,1,32,1024]{4,3,1,2,0:T(8,128)(2,1)}), bf16[4,4,1,32,1024]{4,3,1,2,0:T(8,128)(2,1)S(1)}, u32[]{:S(2)}, u32[]{:S(2)}) %all-to-all-start.3) | async-done | bytes 1048608 | tf_op jit(solution)/shard_map/all_to_all | solution.py:19
  524.1 3.4 all-to-all-start.4
  528.5 7.9 all-to-all-done.4
  537.8 3.4 collective-permute-start
  541.2 6.7 fusion.56
  549.0 3.5 all-to-all-start.17
  553.2 1.7 fusion.102
  555.1 12.4 %all-to-all-done.17 = bf16[4,4,1,32,1024]{4,3,1,2,0:T(8,128)(2,1)S(1)} async-done(((bf16[4,4,1,32,1024]{4,3,1,2,0:T(8,128)(2,1)}), bf16[4,4,1,32,1024]{4,3,1,2,0:T(8,128)(2,1)S(1)}, u32[]{:S(2)}, u32[]{:S(2)}) %all-to-all-start.17) | async-done | bytes 1048608 | tf_op jit(solution)/shard_map/all_to_all | solution.py:19
  568.4 3.5 all-to-all-start.18
  572.0 6.0 all-to-all-done.18
  580.1 17.6 %all_to_all.210 = bf16[4,32,4096]{2,1,0:T(8,128)(2,1)S(1)} all-to-all(bf16[4,32,4096]{2,1,0:T(8,128)(2,1)S(1)} %broadcast_in_dim.146), channel_id=1, replica_groups=mesh['pipe'=8,'dp'=4,'tensor'=4] {'tensor'}, dimensions={0} | all-to-all | bytes 2097152 | tf_op jit(solution)/shard_map/all_to_all | solution.py:31
  599.3 2.5 copy.165
  601.8 3.5 all-to-all-start.6
  606.1 13.6 %all-to-all-done.6 = bf16[128,4,1024]{2,0,1:T(8,128)(2,1)S(1)} async-done(((bf16[128,4,1024]{2,0,1:T(8,128)(2,1)}), bf16[128,4,1024]{2,0,1:T(8,128)(2,1)S(1)}, u32[]{:S(2)}, u32[]{:S(2)}) %all-to-all-start.6) | async-done | bytes 1048608 | tf_op jit(solution)/shard_map/all_to_all | solution.py:132
  619.7 6.0 fusion.25
  625.7 48.2 %all_to_all.211 = bf16[4,128,2816]{2,1,0:T(8,128)(2,1)S(1)} all-to-all(bf16[4,128,2816]{2,1,0:T(8,128)(2,1)S(1)} %bitcast.335), channel_id=1, replica_groups=mesh['pipe'=8,'dp'=4,'tensor'=4] {'dp'}, dimensions={0} | all-to-all | bytes 5767168 | tf_op jit(solution)/shard_map/all_to_all | solution.py:19
  692.3 7.2 all-to-all-start.19
  699.5 1.8 fusion.79
  701.3 1.9 maximum_bitcast_fusion.2
  703.2 18.7 %all-to-all-done.19 = bf16[8,2,3,32,512]{4,3,2,1,0:T(8,128)(2,1)S(1)} async-done(((bf16[8,2,3,32,512]{4,3,2,1,0:T(8,128)(2,1)}), bf16[8,2,3,32,512]{4,3,2,1,0:T(8,128)(2,1)S(1)}, u32[]{:S(2)}, u32[]{:S(2)}) %all-to-all-start.19) | async-done | bytes 1572896 | tf_op jit(solution)/shard_map/all_to_all | solution.py:251
  722.9 9.6 %fusion.126 = f32[1024,2816]{1,0:T(8,128)} fusion(bf16[512,1024]{1,0:T(8,128)(2,1)} %bitcast.354, bf16[512,2816]{1,0:T(8,128)(2,1)} %all-gather.15.cloned.1.call-done), kind=kOutput, calls=%fused_computation.202 | convolution fusion | flops 2952790016 | bytes 15466496 | tf_op jit(solution)/shard_map/dot_general | solution.py:178
  732.5 7.8 fusion.127
  741.0 7.1 fusion.62
  749.2 4.5 all-to-all-start.8
  753.7 11.4 %fusion.20 = bf16[1,1024,2816]{2,1,0:T(8,128)(2,1)} fusion(f32[1024,2816]{1,0:T(8,128)} %fusion.126, bf16[512,1024]{1,0:T(8,128)(2,1)} %bitcast.358, bf16[512,2816]{1,0:T(8,128)(2,1)} %all-gather.19.cloned.1.call-done), kind=kOutput, calls=%fused_computation.28 | convolution fusion | flops 2958557184 | bytes 21233664 | tf_op jit(solution)/shard_map/dot_general | solution.py:178
  765.2 3.1 all-to-all-done.8
  769.1 3.5 all-to-all-start.20
  772.7 8.5 %fusion.21 = bf16[1,2816,1024]{2,1,0:T(8,128)(2,1)} fusion(f32[2816,1024]{1,0:T(8,128)} %fusion.127, bf16[512,2816]{1,0:T(8,128)(2,1)} %all-gather.23.cloned.1.call-done, bf16[512,1024]{1,0:T(8,128)(2,1)S(1)} %bitcast.356), kind=kOutput, calls=%fused_computation.29 | convolution fusion | flops 2958557184 | bytes 21233664 | tf_op jit(solution)/shard_map/dot_general | solution.py:181
  782.2 3.5 all-to-all-start.9
  787.4 4.4 all-to-all-done.9
  (219 shorter events, 64.4 us)
Async XLA Ops:
  7.2 11.9 %copy-start.1 = (bf16[1,2,32,4096]{3,2,1,0:T(8,128)(2,1)S(1)}, bf16[1,2,32,4096]{3,2,1,0:T(8,128)(2,1)}, u32[]{:S(2)}) copy-start(bf16[1,2,32,4096]{3,2,1,0:T(8,128)(2,1)} %param.14) | copy-start | bytes 1572868
  11.6 9.4 %copy-start = (bf16[1,32,4096]{2,1,0:T(8,128)(2,1)S(1)}, bf16[1,32,4096]{2,1,0:T(8,128)(2,1)}, u32[]{:S(2)}) copy-start(bf16[1,32,4096]{2,1,0:T(8,128)(2,1)} %param.10) | copy-start | bytes 786436
  11.6 27.3 %all-to-all-start.10 = ((bf16[8,2,3,32,512]{4,3,2,1,0:T(8,128)(2,1)}), bf16[8,2,3,32,512]{4,3,2,1,0:T(8,128)(2,1)S(1)}, u32[]{:S(2)}, u32[]{:S(2)}) async-start(bf16[8,2,3,32,512]{4,3,2,1,0:T(8,128)(2,1)} %broadcast_select_fusion.1), calls=%async_computation.10 | async-start | bytes 3145728 | tf_op jit(solution)/shard_map/all_to_all | solution.py:216
  19.0 56.2 %all-gather.13.cloned.1.call-start = ((), (), s32[]{:S(2)}) async-start(), calls=%async_computation.25 | async-start | bytes 2621440 | tf_op jit(solution)/shard_map/all_gather | solution.py:40
  19.1 20.1 %copy-start.13 = (bf16[1,1,32,4096]{3,2,1,0:T(8,128)(2,1)}, bf16[1,1,32,4096]{3,2,1,0:T(8,128)(2,1)S(1)}, u32[]{:S(2)}) copy-start(bf16[1,1,32,4096]{3,2,1,0:T(8,128)(2,1)S(1)} %get-tuple-element.32) | copy-start | bytes 786436
  19.1 22.0 %copy-start.15 = (bf16[1,1,32,4096]{3,2,1,0:T(8,128)(2,1)}, bf16[1,1,32,4096]{3,2,1,0:T(8,128)(2,1)S(1)}, u32[]{:S(2)}) copy-start(bf16[1,1,32,4096]{3,2,1,0:T(8,128)(2,1)S(1)} %get-tuple-element.33) | copy-start | bytes 786436
  21.3 20.8 %copy-start.30 = (f32[1,4096]{1,0:T(1,128)S(1)}, f32[1,4096]{1,0:T(1,128)}, u32[]{:S(2)}) copy-start(f32[1,4096]{1,0:T(1,128)} %param.17) | copy-start | bytes 49156
  39.2 3.9 copy-start.10
  40.6 0.7 copy-start.7
  41.0 0.7 copy-start.24
  42.0 34.9 %copy-start.3 = (bf16[32,4096]{1,0:T(8,128)(2,1)}, bf16[32,4096]{1,0:T(8,128)(2,1)S(1)}, u32[]{:S(2)}) copy-start(bf16[32,4096]{1,0:T(8,128)(2,1)S(1)} %get-tuple-element.37) | copy-start | bytes 786436
  42.0 34.9 %copy-start.5 = (bf16[32,4096]{1,0:T(8,128)(2,1)}, bf16[32,4096]{1,0:T(8,128)(2,1)S(1)}, u32[]{:S(2)}) copy-start(bf16[32,4096]{1,0:T(8,128)(2,1)S(1)} %get-tuple-element.23) | copy-start | bytes 786436
  78.2 18.0 %all-to-all-start.12 = ((bf16[128,4,1024]{0,2,1:T(8,128)(2,1)}), bf16[128,4,1024]{0,2,1:T(8,128)(2,1)S(1)}, u32[]{:S(2)}, u32[]{:S(2)}) async-start(bf16[128,4,1024]{0,2,1:T(8,128)(2,1)} %bitcast.43), calls=%async_computation.12 | async-start | bytes 2097152 | tf_op jit(solution)/shard_map/all_to_all | solution.py:154
  96.2 18.0 %all-to-all-start.11 = ((bf16[128,4,1024]{0,2,1:T(8,128)(2,1)}), bf16[128,4,1024]{0,2,1:T(8,128)(2,1)S(1)}, u32[]{:S(2)}, u32[]{:S(2)}) async-start(bf16[128,4,1024]{0,2,1:T(8,128)(2,1)} %bitcast.40), calls=%async_computation.11 | async-start | bytes 2097152 | tf_op jit(solution)/shard_map/all_to_all | solution.py:153
  99.7 88.6 %reduce-scatter.3.cloned.1.call-start = ((), (), s32[]{:S(2)}) async-start(), calls=%async_computation.26 | async-start | bytes 7208960 | tf_op jit(solution)/shard_map/reduce_scatter | solution.py:161
  114.7 6.5 copy-start.21
  130.2 98.0 %all-gather.15.cloned.1.call-start = ((), (), s32[]{:S(2)}) async-start(), calls=%async_computation.27 | async-start | bytes 3604480 | tf_op jit(solution)/shard_map/all_gather | solution.py:177
  234.9 26.1 %copy-start.8 = (bf16[32,8,512]{2,1,0:T(8,128)(2,1)S(1)}, bf16[32,8,512]{2,1,0:T(8,128)(2,1)}, u32[]{:S(2)}) copy-start(bf16[32,8,512]{2,1,0:T(8,128)(2,1)} %copy-done.7) | copy-start | bytes 786436
  254.9 11.1 %copy-start.16 = (bf16[1,1,32,4096]{3,2,1,0:T(8,128)(2,1)S(1)}, bf16[1,1,32,4096]{3,2,1,0:T(8,128)(2,1)}, u32[]{:S(2)}) copy-start(bf16[1,1,32,4096]{3,2,1,0:T(8,128)(2,1)} %copy-done.15) | copy-start | bytes 786436
  254.9 11.4 %copy-start.6 = (bf16[32,4096]{1,0:T(8,128)(2,1)S(1)}, bf16[32,4096]{1,0:T(8,128)(2,1)}, u32[]{:S(2)}) copy-start(bf16[32,4096]{1,0:T(8,128)(2,1)} %copy-done.5) | copy-start | bytes 786436
  254.9 11.4 %copy-start.11 = (bf16[1,32,4096]{2,1,0:T(8,128)(2,1)S(1)}, bf16[1,32,4096]{2,1,0:T(8,128)(2,1)}, u32[]{:S(2)}) copy-start(bf16[1,32,4096]{2,1,0:T(8,128)(2,1)} %param.12) | copy-start | bytes 786436
  255.8 9.4 %all-to-all-start.14 = ((bf16[4,1,32,1024]{3,2,1,0:T(8,128)(2,1)}), bf16[4,1,32,1024]{3,2,1,0:T(8,128)(2,1)S(1)}, u32[]{:S(2)}, u32[]{:S(2)}) async-start(bf16[4,1,32,1024]{3,2,1,0:T(8,128)(2,1)} %bitcast.52), calls=%async_computation.15 | async-start | bytes 524288 | tf_op jit(solution)/shard_map/all_to_all | solution.py:122
  259.2 17.3 %copy-start.33 = (bf16[32,4096]{1,0:T(8,128)(2,1)S(1)}, bf16[32,4096]{1,0:T(8,128)(2,1)}, u32[]{:S(2)}) copy-start(bf16[32,4096]{1,0:T(8,128)(2,1)} %param.13) | copy-start | bytes 786436
  259.2 50.1 %all-gather.17.cloned.1.call-start = ((), (), s32[]{:S(2)}) async-start(), calls=%async_computation.28 | async-start | bytes 2621440 | tf_op jit(solution)/shard_map/all_gather | solution.py:40
  261.2 16.1 %copy-start.26 = (bf16[32,4096]{1,0:T(8,128)(2,1)S(1)}, bf16[32,4096]{1,0:T(8,128)(2,1)}, u32[]{:S(2)}) copy-start(bf16[32,4096]{1,0:T(8,128)(2,1)} %get-tuple-element.48) | copy-start | bytes 786436
  266.5 10.1 %collective-permute-start.1 = (bf16[32,4096]{1,0:T(8,128)(2,1)S(1)}, bf16[32,4096]{1,0:T(8,128)(2,1)S(1)}, u32[]{:S(2)}, u32[]{:S(2)}) collective-permute-start(bf16[32,4096]{1,0:T(8,128)(2,1)S(1)} %fusion.95), channel_id=1, source_target_pairs={{16,0},{32,16},{48,32},{64,48},{80,64},{96,80},{112,96},{17,1},{33... | collective-permute-start | bytes 786440 | tf_op jit(solution)/shard_map/ppermute | solution.py:50
  276.6 0.7 copy-start.17
  312.3 18.0 %all-to-all-start.16 = ((bf16[128,4,1024]{0,2,1:T(8,128)(2,1)}), bf16[128,4,1024]{0,2,1:T(8,128)(2,1)S(1)}, u32[]{:S(2)}, u32[]{:S(2)}) async-start(bf16[128,4,1024]{0,2,1:T(8,128)(2,1)} %bitcast.65), calls=%async_computation.17 | async-start | bytes 2097152 | tf_op jit(solution)/shard_map/all_to_all | solution.py:154
  330.3 18.0 %all-to-all-start.15 = ((bf16[128,4,1024]{0,2,1:T(8,128)(2,1)}), bf16[128,4,1024]{0,2,1:T(8,128)(2,1)S(1)}, u32[]{:S(2)}, u32[]{:S(2)}) async-start(bf16[128,4,1024]{0,2,1:T(8,128)(2,1)} %bitcast.62), calls=%async_computation.16 | async-start | bytes 2097152 | tf_op jit(solution)/shard_map/all_to_all | solution.py:153
  333.8 125.2 %reduce-scatter.5.cloned.1.call-start = ((), (), s32[]{:S(2)}) async-start(), calls=%async_computation.29 | async-start | bytes 7208960 | tf_op jit(solution)/shard_map/reduce_scatter | solution.py:161
  348.8 6.4 copy-start.23
  348.8 6.4 copy-start.2
  358.2 0.9 copy-start.19
  358.2 137.1 %all-gather.9.cloned.1.call-start = ((), (), s32[]{:S(2)}) async-start(), calls=%async_computation.23 | async-start | bytes 3604480 | tf_op jit(solution)/shard_map/all_gather | solution.py:140
  458.8 82.4 %all-gather.19.cloned.1.call-start = ((), (), s32[]{:S(2)}) async-start(), calls=%async_computation.30 | async-start | bytes 3604480 | tf_op jit(solution)/shard_map/all_gather | solution.py:177
  502.0 25.6 %copy-start.25 = (bf16[32,8,512]{2,1,0:T(8,128)(2,1)S(1)}, bf16[32,8,512]{2,1,0:T(8,128)(2,1)}, u32[]{:S(2)}) copy-start(bf16[32,8,512]{2,1,0:T(8,128)(2,1)} %copy-done.24) | copy-start | bytes 786436
  503.0 20.1 %all-to-all-start.3 = ((bf16[4,4,1,32,1024]{4,3,1,2,0:T(8,128)(2,1)}), bf16[4,4,1,32,1024]{4,3,1,2,0:T(8,128)(2,1)S(1)}, u32[]{:S(2)}, u32[]{:S(2)}) async-start(bf16[4,4,1,32,1024]{4,3,1,2,0:T(8,128)(2,1)} %copy.160), calls=%async_computation.3 | async-start | bytes 2097152 | tf_op jit(solution)/shard_map/all_to_all | solution.py:19
  524.1 12.3 %all-to-all-start.4 = ((bf16[4,1,32,1024]{3,2,1,0:T(8,128)(2,1)}), bf16[4,1,32,1024]{3,2,1,0:T(8,128)(2,1)S(1)}, u32[]{:S(2)}, u32[]{:S(2)}) async-start(bf16[4,1,32,1024]{3,2,1,0:T(8,128)(2,1)} %bitcast.13), calls=%async_computation.4 | async-start | bytes 524288 | tf_op jit(solution)/shard_map/all_to_all | solution.py:122
  537.8 14.7 %collective-permute-start = (bf16[32,4096]{1,0:T(8,128)(2,1)}, bf16[32,4096]{1,0:T(8,128)(2,1)S(1)}, u32[]{:S(2)}, u32[]{:S(2)}) collective-permute-start(bf16[32,4096]{1,0:T(8,128)(2,1)} %fusion.78), channel_id=1, source_target_pairs={{0,16},{16,32},{32,48},{48,64},{64,80},{80,96},{96,112},{1,17},{17... | collective-permute-start | bytes 786440 | tf_op jit(solution)/shard_map/ppermute | solution.py:50
  547.9 5.3 copy-start.31
  549.0 18.5 %all-to-all-start.17 = ((bf16[4,4,1,32,1024]{4,3,1,2,0:T(8,128)(2,1)}), bf16[4,4,1,32,1024]{4,3,1,2,0:T(8,128)(2,1)S(1)}, u32[]{:S(2)}, u32[]{:S(2)}) async-start(bf16[4,4,1,32,1024]{4,3,1,2,0:T(8,128)(2,1)} %copy.188), calls=%async_computation.19 | async-start | bytes 2097152 | tf_op jit(solution)/shard_map/all_to_all | solution.py:19
  552.5 0.7 copy-start.32
  555.0 24.1 %copy-start.4 = (bf16[32,4096]{1,0:T(8,128)(2,1)S(1)}, bf16[32,4096]{1,0:T(8,128)(2,1)}, u32[]{:S(2)}) copy-start(bf16[32,4096]{1,0:T(8,128)(2,1)} %copy-done.3) | copy-start | bytes 786436
  568.4 10.3 %copy-start.14 = (bf16[1,1,32,4096]{3,2,1,0:T(8,128)(2,1)S(1)}, bf16[1,1,32,4096]{3,2,1,0:T(8,128)(2,1)}, u32[]{:S(2)}) copy-start(bf16[1,1,32,4096]{3,2,1,0:T(8,128)(2,1)} %copy-done.13) | copy-start | bytes 786436
  568.4 10.3 %copy-start.27 = (bf16[1,1,32,4,1024]{4,3,2,1,0:T(4,128)(2,1)S(1)}, bf16[1,1,32,4,1024]{4,3,2,1,0:T(4,128)(2,1)}, u32[]{:S(2)}) copy-start(bf16[1,1,32,4,1024]{4,3,2,1,0:T(4,128)(2,1)} %convert_element_type.380) | copy-start | bytes 786436
  568.4 10.6 %copy-start.18 = (bf16[32,4096]{1,0:T(8,128)(2,1)S(1)}, bf16[32,4096]{1,0:T(8,128)(2,1)}, u32[]{:S(2)}) copy-start(bf16[32,4096]{1,0:T(8,128)(2,1)} %copy-done.17) | copy-start | bytes 786436
  568.4 9.5 %all-to-all-start.18 = ((bf16[4,1,32,1024]{3,2,1,0:T(8,128)(2,1)}), bf16[4,1,32,1024]{3,2,1,0:T(8,128)(2,1)S(1)}, u32[]{:S(2)}, u32[]{:S(2)}) async-start(bf16[4,1,32,1024]{3,2,1,0:T(8,128)(2,1)} %bitcast.349), calls=%async_computation.20 | async-start | bytes 524288 | tf_op jit(solution)/shard_map/all_to_all | solution.py:122
  601.8 18.0 %all-to-all-start.6 = ((bf16[128,4,1024]{2,0,1:T(8,128)(2,1)}), bf16[128,4,1024]{2,0,1:T(8,128)(2,1)S(1)}, u32[]{:S(2)}, u32[]{:S(2)}) async-start(bf16[128,4,1024]{2,0,1:T(8,128)(2,1)} %copy.165), calls=%async_computation.6 | async-start | bytes 2097152 | tf_op jit(solution)/shard_map/all_to_all | solution.py:132
  605.3 127.2 %all-gather.21.cloned.1.call-start = ((), (), s32[]{:S(2)}) async-start(), calls=%async_computation.31 | async-start | bytes 3604480 | tf_op jit(solution)/shard_map/all_gather | solution.py:176
  606.1 134.9 %all-gather.11.cloned.1.call-start = ((), (), s32[]{:S(2)}) async-start(), calls=%async_computation.24 | async-start | bytes 3604480 | tf_op jit(solution)/shard_map/all_gather | solution.py:140
  674.3 15.0 %copy-start.9 = (bf16[32,8,512]{2,1,0:T(8,128)(2,1)S(1)}, bf16[32,8,512]{2,1,0:T(8,128)(2,1)}, u32[]{:S(2)}) copy-start(bf16[32,8,512]{2,1,0:T(8,128)(2,1)} %copy-done.7) | copy-start | bytes 786436
  692.3 29.6 %all-to-all-start.19 = ((bf16[8,2,3,32,512]{4,3,2,1,0:T(8,128)(2,1)}), bf16[8,2,3,32,512]{4,3,2,1,0:T(8,128)(2,1)S(1)}, u32[]{:S(2)}, u32[]{:S(2)}) async-start(bf16[8,2,3,32,512]{4,3,2,1,0:T(8,128)(2,1)} %broadcast_select_fusion), calls=%async_computation.21 | async-start | bytes 3145728 | tf_op jit(solution)/shard_map/all_to_all | solution.py:251
  699.5 73.2 %all-gather.23.cloned.1.call-start = ((), (), s32[]{:S(2)}) async-start(), calls=%async_computation.32 | async-start | bytes 3604480 | tf_op jit(solution)/shard_map/all_gather | solution.py:176
  722.9 9.6 %copy-start.20 = (bf16[4,128,1024]{2,1,0:T(8,128)(2,1)S(1)}, bf16[4,128,1024]{2,1,0:T(8,128)(2,1)}, u32[]{:S(2)}) copy-start(bf16[4,128,1024]{2,1,0:T(8,128)(2,1)} %copy.175) | copy-start | bytes 3145732
  732.5 8.2 %copy-start.12 = (bf16[1,32,4096]{2,1,0:T(8,128)(2,1)S(1)}, bf16[1,32,4096]{2,1,0:T(8,128)(2,1)}, u32[]{:S(2)}) copy-start(bf16[1,32,4096]{2,1,0:T(8,128)(2,1)} %param.12) | copy-start | bytes 786436
  749.2 19.1 %all-to-all-start.8 = ((bf16[4,4,1,32,1024]{4,3,1,2,0:T(8,128)(2,1)}), bf16[4,4,1,32,1024]{4,3,1,2,0:T(8,128)(2,1)S(1)}, u32[]{:S(2)}, u32[]{:S(2)}) async-start(bf16[4,4,1,32,1024]{4,3,1,2,0:T(8,128)(2,1)} %copy.166), calls=%async_computation.8 | async-start | bytes 2097152 | tf_op jit(solution)/shard_map/all_to_all | solution.py:19
  753.7 19.0 %copy-start.22 = (bf16[4,128,1024]{2,1,0:T(8,128)(2,1)S(1)}, bf16[4,128,1024]{2,1,0:T(8,128)(2,1)}, u32[]{:S(2)}) copy-start(bf16[4,128,1024]{2,1,0:T(8,128)(2,1)} %copy.187) | copy-start | bytes 3145732
  769.1 13.1 %all-to-all-start.20 = ((f32[16,1,4096]{2,1,0:T(1,128)}), f32[16,1,4096]{2,1,0:T(1,128)S(1)}, u32[]{:S(2)}, u32[]{:S(2)}) async-start(f32[16,1,4096]{2,1,0:T(1,128)} %broadcast_in_dim.171), calls=%async_computation.22 | async-start | bytes 524288 | tf_op jit(solution)/shard_map/all_to_all | solution.py:31
  772.7 13.1 %copy-start.28 = (bf16[1,32,4096]{2,1,0:T(8,128)(2,1)S(1)}, bf16[1,32,4096]{2,1,0:T(8,128)(2,1)}, u32[]{:S(2)}) copy-start(bf16[1,32,4096]{2,1,0:T(8,128)(2,1)} %get-tuple-element.46) | copy-start | bytes 786436
  782.2 10.3 %copy-start.29 = (bf16[1,32,4096]{2,1,0:T(8,128)(2,1)S(1)}, bf16[1,32,4096]{2,1,0:T(8,128)(2,1)}, u32[]{:S(2)}) copy-start(bf16[1,32,4096]{2,1,0:T(8,128)(2,1)} %fusion.79) | copy-start | bytes 786436
  782.2 9.5 %all-to-all-start.9 = ((bf16[4,1,32,1024]{3,2,1,0:T(8,128)(2,1)}), bf16[4,1,32,1024]{3,2,1,0:T(8,128)(2,1)S(1)}, u32[]{:S(2)}, u32[]{:S(2)}) async-start(bf16[4,1,32,1024]{3,2,1,0:T(8,128)(2,1)} %bitcast.26), calls=%async_computation.9 | async-start | bytes 524288 | tf_op jit(solution)/shard_map/all_to_all | solution.py:122
Sparse Core Ops, SparseCore 0:
  44.1 31.0 all-gather.12
  130.3 57.9 reduce-scatter.2
  191.8 36.3 all-gather.14
  278.3 31.0 all-gather.16
  358.3 76.6 reduce-scatter.4
  458.9 36.3 all-gather.8
  497.0 38.9 all-gather.18
  607.8 45.9 all-gather.20
  675.7 53.2 all-gather.10
  730.5 36.5 all-gather.22
where the time goes:
time: 815 us; the launch traced here: 801 us
  waiting for transfers between devices  344 us (42%)
  blocking collectives  176 us (22%)
  matrix products  105 us (13%)
  starting transfers between devices  71 us (9%)
  other arithmetic  41.3 us (5%)
  local copies, waits for them, and re-layouts  35.6 us (4%)
  between operations  27.3 us (3%)
    all_to_all x3, blocking collectives, sum_at_owner(): lax.all_to_all(in_blocks(shard, dim, devices), axis, 0, 0, tiled=True)  113 us
    all_gather x2, waiting for transfers between devices, side_by_side(): lax.all_gather(both, axis, axis=dim, tiled=True)  62.5 us
    reduce_scatter x2, waiting for transfers between devices, backward_pass(): lax.psum_scatter(jnp.concatenate([pre_part, back_part], axis=1).astype(jn...  58.1 us
    all_gather x2, waiting for transfers between devices, backward_pass(): d_pre_piece = lax.all_gather(d_pre, 'dp', axis=0, tiled=True)  36.5 us
    all_to_all x2, blocking collectives, from_everyone(): return lax.all_to_all(copies, axis, split_axis=0, concat_axis=0, tiled=True)  35.3 us
    all_gather x2, waiting for transfers between devices, forward_pass(): lax.all_gather(hidden, 'dp', axis=0, tiled=True)  32.9 us
    all_to_all x3, waiting for transfers between devices, sum_at_owner(): lax.all_to_all(in_blocks(shard, dim, devices), axis, 0, 0, tiled=True)  31.2 us
    all_to_all x1, blocking collectives, forward_pass(): lax.all_to_all(replica_rows, 'dp', split_axis=1, concat_axis=0, tiled=True)  28.4 us
  transfers between devices with their start and end apart: 27, of which 20 were waited for; matrix products, arithmetic and copies ran while one was open for 14% of the time, Pallas kernels for 0%

commit v1 on v0

v1 whole, which is shorter than its diff:
```python
import jax
import jax.numpy as jnp
from jax import lax
from jax.sharding import PartitionSpec as P

MICRO = 2
EPSILON = 1e-05
LOW = jnp.bfloat16
WIDE = jnp.float32


def across_core(x):
    return lax.ppermute(x, "dp", [(d, d ^ 1) for d in range(4)])


def across_z(x):
    return lax.ppermute(x, "dp", [(d, d ^ 2) for d in range(4)])


def along_y(x, step):
    return lax.ppermute(x, "tensor", [(t, (t + step) % 4) for t in range(4)])


def round_x(x, step, first):
    return lax.ppermute(x, "pipe", [(first + i, first + (i + step) % 4) for i in range(4)])


def passed_along(value, steps):
    first, last = max(0, -steps), min(8, 8 - steps)
    return lax.ppermute(value, "pipe", [(s, s + steps) for s in range(first, last)])


def normalize(values, norm_scale):
    wide = values.astype(WIDE)
    inverse_rms = lax.rsqrt(jnp.mean(wide * wide, axis=-1, keepdims=True) + EPSILON)
    return wide, inverse_rms, (wide * inverse_rms * norm_scale).astype(LOW)


def finish_norm(wide, inverse_rms, norm_scale, d_normed, cotangent):
    scaled = d_normed * norm_scale
    d_input = (
        cotangent.astype(WIDE)
        + inverse_rms * scaled
        - wide
        * (inverse_rms * inverse_rms * inverse_rms)
        * jnp.mean(scaled * wide, axis=-1, keepdims=True)
    )
    return d_input.astype(LOW), jnp.sum(d_normed * wide * inverse_rms, axis=0)


def ordered(at_zero, own, other):
    return jnp.where(at_zero, own, other), jnp.where(at_zero, other, own)


class Place:
    def __init__(self):
        d = lax.axis_index("dp")
        self.z, self.core = d // 2, d % 2
        self.low_z, self.low_core = self.z == 0, self.core == 0


def gather_rows(x, place):
    rows, width = x.shape
    left, right = x[:, : width // 2], x[:, width // 2 :]
    keep = jnp.where(place.low_z, left, right)
    got = across_z(jnp.where(place.low_z, right, left))
    mine = jnp.stack(ordered(place.low_z, keep, got))
    before, after = along_y(mine, 1), along_y(mine, -1)
    far = jnp.stack([along_y(before[0], 1), along_y(after[1], -1)])
    ring = jnp.stack([mine, after, far, before])
    return jnp.concatenate([ring, across_core(ring)]).reshape(16 * rows, width // 2)


def settle(part, place):
    half, width = part.shape[0] // 2, part.shape[1]
    rows = half // 8
    got = across_core(part[half:].astype(LOW))
    summed = (part[:half] + got.astype(WIDE)).reshape(4, 2, rows, width)
    up = along_y(summed[2, 0].astype(LOW), 1).astype(WIDE)
    down = along_y(summed[2, 1].astype(LOW), -1).astype(WIDE)
    to_next = jnp.stack([summed[1, 0] + up, summed[1, 1]]).astype(LOW)
    to_last = jnp.stack([summed[3, 0], summed[3, 1] + down]).astype(LOW)
    mine = (
        summed[0] + along_y(to_next, 1).astype(WIDE) + along_y(to_last, -1).astype(WIDE)
    ).astype(LOW)
    keep = jnp.where(place.low_z, mine[0], mine[1])
    got = across_z(jnp.where(place.low_z, mine[1], mine[0]))
    return jnp.concatenate(ordered(place.low_z, keep, got), axis=1).astype(WIDE)


def summed_over_z(part):
    low = part.astype(LOW)
    return low.astype(WIDE) + across_z(low).astype(WIDE)


def whole_hidden(own, place):
    half = own.shape[0] // 2
    got = across_core(own)
    other = jnp.concatenate([got[half:], got[:half]])
    return jnp.concatenate(ordered(place.low_core, own, other), axis=1)


def my_features(x, place):
    half = x.shape[1] // 2
    return jnp.where(place.low_core, x[:, :half], x[:, half:])


def times_transposed(a, b):
    return lax.dot_general(a, b, (((1,), (1,)), ((), ())), preferred_element_type=WIDE)


def over_rows(a, b):
    return lax.dot_general(a, b, (((0,), (0,)), ((), ())), preferred_element_type=WIDE)


def match_blocks(block_ids, block_count):
    return block_ids[:, None] == jnp.arange(block_count, dtype=jnp.int32)[None, :]


def pull_blocks(values, block_ids, block_width):
    blocks = values.reshape(values.shape[0], -1, block_width)
    picked = [
        lax.dynamic_slice_in_dim(blocks, block_ids[e], 1, axis=1)[:, 0]
        for e in range(block_ids.shape[0])
    ]
    return jnp.stack(picked)


def clear_blocks(values, block_ids, block_width, active):
    blocks = values.reshape(values.shape[0], -1, block_width)
    covered = jnp.any(match_blocks(block_ids, blocks.shape[1]), axis=0) & active
    return jnp.where(covered[None, :, None], jnp.zeros((), values.dtype), blocks).reshape(
        values.shape
    )


def place_blocks(values, block_ids, fetched, active):
    block_width = fetched.shape[2]
    blocks = values.reshape(values.shape[0], -1, block_width)
    matched = match_blocks(block_ids, blocks.shape[1]) & active
    for e in range(fetched.shape[0]):
        blocks = jnp.where(matched[e][None, :, None], fetched[e][:, None, :], blocks)
    return blocks.reshape(values.shape)


def pick(options, wanted):
    total = jnp.where(wanted[0], options[0], jnp.zeros((), options[0].dtype))
    for option, want in zip(options[1:], wanted[1:]):
        total = jnp.where(want, option, total)
    return total


def guests_back(held, plan, section):
    column = section % 4
    around = [held, round_x(held, -1, 4), round_x(held, -2, 4), round_x(held, 1, 4)]
    found = []
    for tick in range(MICRO):
        holder = plan[0, tick, column, 0]
        found.append(
            pick(
                [a[tick] for a in around],
                [holder == (column + k) % 4 for k in range(4)],
            )
        )
    return lax.ppermute(jnp.stack(found), "pipe", [(4 + s, s) for s in range(4)])


def guests_out(pulled, plan_tick, section):
    column = section % 4
    landed = lax.ppermute(pulled, "pipe", [(s, 4 + s) for s in range(4)])
    around = [landed, round_x(landed, -1, 4), round_x(landed, -2, 4), round_x(landed, 1, 4)]
    late = section >= 4
    wanted = [late & (plan_tick[(column + k) % 4, 0] == column) for k in range(4)]
    return pick(around, wanted)


def over_copies(x):
    x = x + across_core(x)
    x = x + across_z(x)
    for bit in (1, 2):
        x = x + lax.ppermute(x, "tensor", [(t, t ^ bit) for t in range(4)])
    return x


def local(
    act_in, act_first, grad_in, grad_last, stash_local, stash_guest, plan, norm_gain, w_up, w_down
):
    place = Place()
    section = lax.axis_index("pipe")
    is_early = section < 4
    plan_row = jnp.minimum(section, 3)
    block_width = stash_guest.shape[-1]
    norm_scale = norm_gain[0]

    half = w_up.shape[2] // 2
    up_left, up_right = w_up[0][:, :half], w_up[0][:, half:]
    up_own = jnp.where(place.low_core, up_left, up_right)
    up_got = across_core(jnp.where(place.low_core, up_right, up_left))
    up = jnp.concatenate(ordered(place.low_core, up_own, up_got), axis=0)
    down_top, down_bottom = w_down[0][:half], w_down[0][half:]
    down_own = jnp.where(place.low_core, down_top, down_bottom)
    down_got = across_core(jnp.where(place.low_core, down_bottom, down_top))
    down = jnp.concatenate(ordered(place.low_core, down_own, down_got), axis=1)

    def forward_head(values):
        _, _, normed = normalize(values, norm_scale)
        rows = gather_rows(normed, place)
        return jnp.dot(rows, up, preferred_element_type=WIDE)

    def forward_tail(values, hidden_pre):
        hidden = jax.nn.silu(hidden_pre).astype(LOW)
        partial = jnp.dot(hidden, down, preferred_element_type=WIDE)
        return (values.astype(WIDE) + settle(partial, place)).astype(LOW)

    def backward_tail(values, inverse_rms, cotangent, hidden_pre, d_hidden):
        gate = jax.nn.sigmoid(hidden_pre)
        hidden = (hidden_pre * gate).astype(LOW)
        d_pre = (d_hidden * gate * (1.0 + hidden_pre * (1.0 - gate))).astype(LOW)
        d_normed = settle(times_transposed(d_pre, up), place)
        d_input, gain = finish_norm(
            values.astype(WIDE), inverse_rms, norm_scale, d_normed, cotangent
        )
        return d_input, gain, whole_hidden(hidden, place), whole_hidden(d_pre, place)

    guests = guests_back(stash_guest[0], plan, section)
    old = [
        place_blocks(stash_local[0, m], plan[0, m, plan_row, 1:], guests[m], is_early)
        for m in range(MICRO)
    ]
    stash_norm = [normalize(old[m], norm_scale) for m in range(MICRO)]

    cot_zero = grad_in[0]
    cot_rows_zero = gather_rows(cot_zero, place)
    d_hidden_zero = summed_over_z(times_transposed(cot_rows_zero, down))
    stash_rows = [gather_rows(stash_norm[m][2], place) for m in range(MICRO)]
    pre_zero = summed_over_z(jnp.dot(stash_rows[0], up, preferred_element_type=WIDE))

    front_pre_zero = summed_over_z(forward_head(act_in[0]))
    d_input_zero, gain_zero, hidden_zero, d_pre_zero = backward_tail(
        old[0], stash_norm[0][1], cot_zero, pre_zero, d_hidden_zero
    )
    pre_one = summed_over_z(jnp.dot(stash_rows[1], up, preferred_element_type=WIDE))
    front_zero = forward_tail(act_in[0], front_pre_zero)

    returned = passed_along(d_input_zero, -1)
    cot_one = jnp.where(section == 7, grad_last, returned)
    cot_rows_one = gather_rows(cot_one, place)
    d_hidden_one = summed_over_z(times_transposed(cot_rows_one, down))

    passed = passed_along(front_zero, 1)
    input_one = jnp.where(section == 0, act_first, passed)
    front_pre_one = summed_over_z(forward_head(input_one))

    d_input_one, gain_one, hidden_one, d_pre_one = backward_tail(
        old[1], stash_norm[1][1], cot_one, pre_one, d_hidden_one
    )
    front_one = forward_tail(input_one, front_pre_one)

    grad_up = (
        over_rows(my_features(stash_rows[0], place), d_pre_zero)
        + over_rows(my_features(stash_rows[1], place), d_pre_one)
    ).astype(LOW)
    grad_down = (
        over_rows(hidden_zero, my_features(cot_rows_zero, place))
        + over_rows(hidden_one, my_features(cot_rows_one, place))
    ).astype(LOW)
    gain_grad = over_copies((gain_zero + gain_one)[None])[0]

    new_inputs = [act_in[0], input_one]
    guest_new = []
    kept = []
    for m in range(MICRO):
        ids = plan[1, m, plan_row, 1:]
        guest_new.append(
            guests_out(pull_blocks(new_inputs[m], ids, block_width), plan[1, m], section)
        )
        kept.append(clear_blocks(new_inputs[m], ids, block_width, is_early))

    return (
        jnp.stack([front_zero, front_one])[None],
        jnp.stack([d_input_zero, d_input_one])[None],
        jnp.stack(kept)[None],
        jnp.stack(guest_new)[None],
        grad_up[None],
        grad_down[None],
        gain_grad[None],
    )


def solution(mesh):
    placed = (
        P("pipe", ("dp", "tensor"), None),
        P(("dp", "tensor"), None),
        P("pipe", ("dp", "tensor"), None),
        P(("dp", "tensor"), None),
        P("pipe", None, ("dp", "tensor"), None),
        P("pipe", None, None, ("dp", "tensor"), None),
        P(),
        P("pipe", None),
        P("pipe", "dp", "tensor"),
        P("pipe", "tensor", "dp"),
    )
    return jax.shard_map(
        local,
        mesh=mesh,
        in_specs=placed,
        out_specs=(
            P("pipe", None, ("dp", "tensor"), None),
            P("pipe", None, ("dp", "tensor"), None),
            P("pipe", None, ("dp", "tensor"), None),
            P("pipe", None, None, ("dp", "tensor"), None),
            P("pipe", "dp", "tensor"),
            P("pipe", "tensor", "dp"),
            P("pipe", None),
        ),
        check_vma=False,
    )
```

time: 815 us -> 541 us (0.66)
  blocking collectives: 176 us -> 0 us
  waiting for transfers between devices: 344 us -> 227 us
  starting transfers between devices: 71 us -> 127 us
  matrix products: 105 us -> 65.3 us
  other arithmetic: 41.3 us -> 59.2 us
    ppermute x2 -> x90, waiting for transfers between devices: 5.34 us -> 227 us  [the longest x17 157 us: across_z(): return lax.ppermute(x, 'dp', [(d, d ^ 2) for d in range(4)])]
    all_to_all x6 -> x0, blocking collectives: 176 us -> none  [the longest x3 113 us: sum_at_owner(): lax.all_to_all(in_blocks(shard, dim, devices), axis, 0, 0, tiled=True)]
    all_to_all x15 -> x0, waiting for transfers between devices: 148 us -> none  [the longest x3 31.2 us: sum_at_owner(): lax.all_to_all(in_blocks(shard, dim, devices), axis, 0, 0, tiled=True)]
    all_gather x8 -> x0, waiting for transfers between devices: 132 us -> none  [the longest x2 62.5 us: side_by_side(): lax.all_gather(both, axis, axis=dim, tiled=True)]
    ppermute x2 -> x90, starting transfers between devices: 8.07 us -> 127 us  [the longest x40 57.2 us: along_y(): return lax.ppermute(x, 'tensor', [(t, (t + step) % 4) for t in range(4)])]
    all_to_all x15 -> x0, starting transfers between devices: 61.9 us -> none  [the longest x4 13.9 us: settle(): lax.all_to_all(reduced.astype(jnp.bfloat16), 'dp', split_axis=0, concat_a...]
    reduce_scatter x2 -> x0, waiting for transfers between devices: 58.1 us -> none  [backward_pass(): lax.psum_scatter(jnp.concatenate([pre_part, back_part], axis=1).astype(jn...]
    dot_general x16 -> x14, matrix products: 105 us -> 65.3 us  [the longest x4 26.7 us: over_rows(): lax.dot_general(a, b, (((0,), (0,)), ((), ())), preferred_element_type=WIDE)]
  transfers between devices with their start and end apart: 27 -> 90, of which waited for: 20 -> 40; matrix products, arithmetic and copies ran while one was open for 14% -> 25% of each run, Pallas kernels for 0% -> 0%
where the time goes in v1:
time: 541 us; the launch traced here: 531 us
  waiting for transfers between devices  227 us (42%)
  starting transfers between devices  127 us (23%)
  matrix products  65.3 us (12%)
  other arithmetic  59.2 us (11%)
  local copies, waits for them, and re-layouts  28.1 us (5%)
  between operations  25.2 us (5%)
    ppermute x17, waiting for transfers between devices, across_z(): return lax.ppermute(x, 'dp', [(d, d ^ 2) for d in range(4)])  157 us
    ppermute x40, starting transfers between devices, along_y(): return lax.ppermute(x, 'tensor', [(t, (t + step) % 4) for t in range(4)])  57.2 us
    ppermute x40, waiting for transfers between devices, along_y(): return lax.ppermute(x, 'tensor', [(t, (t + step) % 4) for t in range(4)])  55 us
    ppermute x9, starting transfers between devices, round_x(): lax.ppermute(x, 'pipe', [(first + i, first + (i + step) % 4) for i in ran...  30 us
    dot_general x4, matrix products, over_rows(): lax.dot_general(a, b, (((0,), (0,)), ((), ())), preferred_element_type=WIDE)  26.7 us
    ppermute x17, starting transfers between devices, across_z(): return lax.ppermute(x, 'dp', [(d, d ^ 2) for d in range(4)])  16.8 us
    dot_general x4, matrix products, times_transposed(): lax.dot_general(a, b, (((1,), (1,)), ((), ())), preferred_element_type=WIDE)  13.8 us
    ppermute x17, starting transfers between devices, across_core(): return lax.ppermute(x, 'dp', [(d, d ^ 1) for d in range(4)])  12.3 us
  transfers between devices with their start and end apart: 90, of which 40 were waited for; matrix products, arithmetic and copies ran while one was open for 25% of the time, Pallas kernels for 0%

profile of v1, /device:TPU:64, one launch (start us, length us, event | category | flops | bytes accessed | tf_op | source)
XLA Modules:
  0.0 531.1 jit_solution(16055344964363482714)
XLA Ops:
  0.6 4.7 collective-permute-start.31
  5.3 2.7 collective-permute-start.30
  8.0 2.8 collective-permute-start.29
  26.2 4.7 broadcast_select_fusion.3
  52.8 3.7 collective-permute-start.75
  58.0 3.9 collective-permute-start.76
  62.0 2.6 collective-permute-start.77
  64.6 3.1 collective-permute-start.34
  70.7 2.6 collective-permute-done.34
  74.0 3.7 collective-permute-start.37
  83.7 2.6 fusion.50
  94.8 3.2 collective-permute-start.41
  102.9 3.3 collective-permute-start.44
  106.3 3.3 collective-permute-done.44
  109.6 3.7 collective-permute-start.62
  114.1 2.3 collective-permute-done.45
  116.6 2.9 broadcast_select_fusion.2
  119.6 3.4 convolution_convert_fusion.2
  126.9 3.5 convolution_convert_fusion.3
  133.9 3.1 collective-permute-done.65
  137.0 2.6 collective-permute-done.64
  139.9 17.6 %collective-permute-done.46 = bf16[512,1408]{1,0:T(8,128)(2,1)S(1)} collective-permute-done((bf16[512,1408]{1,0:T(8,128)(2,1)S(1)}, bf16[512,1408]{1,0:T(8,128)(2,1)S(1)}, u32[]{:S(2)}, u32[]{:S(2)}) %collective-permute-start.46) | collective-permute-done | bytes 1441824 | tf_op jit(solution)/shard_map/ppermute | solution.py:17
  157.5 30.1 %collective-permute-done.39 = bf16[512,1408]{1,0:T(8,128)(2,1)S(1)} collective-permute-done((bf16[512,1408]{1,0:T(8,128)(2,1)S(1)}, bf16[512,1408]{1,0:T(8,128)(2,1)S(1)}, u32[]{:S(2)}, u32[]{:S(2)}) %collective-permute-start.39) | collective-permute-done | bytes 1441824 | tf_op jit(solution)/shard_map/ppermute | solution.py:17
  189.3 3.4 fusion.113
  192.9 8.9 %collective-permute-start.47 = (bf16[256,2048]{1,0:T(8,128)(2,1)S(1)}, bf16[256,2048]{1,0:T(8,128)(2,1)S(1)}, u32[]{:S(2)}, u32[]{:S(2)}) collective-permute-start(bf16[256,2048]{1,0:T(8,128)(2,1)S(1)} %slice.920), channel_id=1, source_target_pairs={{0,4},{4,0},{8,12},{12,8},{1,5},{5,1},{9,13},{13,9},{2,6},{6,2},{1... | collective-permute-start | bytes 3145736 | tf_op jit(solution)/shard_map/ppermute | solution.py:13
  205.0 3.2 collective-permute-start.50
  208.2 4.6 convolution_convert_fusion
  216.9 6.5 %collective-permute-done.51 = bf16[2,32,2048]{2,1,0:T(8,128)(2,1)S(1)} collective-permute-done((bf16[2,32,2048]{2,1,0:T(8,128)(2,1)S(1)}, bf16[2,32,2048]{2,1,0:T(8,128)(2,1)S(1)}, u32[]{:S(2)}, u32[]{:S(2)}) %collective-permute-start.51) | collective-permute-done | bytes 262176 | tf_op jit(solution)/shard_map/ppermute | solution.py:21
  225.4 2.2 broadcast_select_fusion.12
  227.6 21.3 %collective-permute-done.52 = bf16[32,2048]{1,0:T(8,128)(2,1)S(1)} collective-permute-done((bf16[32,2048]{1,0:T(8,128)(2,1)S(1)}, bf16[32,2048]{1,0:T(8,128)(2,1)S(1)}, u32[]{:S(2)}, u32[]{:S(2)}) %collective-permute-start.52) | collective-permute-done | bytes 131104 | tf_op jit(solution)/shard_map/ppermute | solution.py:17
  261.2 4.4 collective-permute-done.53
  266.1 4.5 collective-permute-done.54
  275.1 3.5 collective-permute-done.4
  283.3 3.8 collective-permute-done.58
  291.1 3.4 convolution_convert_fusion.5
  295.1 3.5 convolution_convert_fusion.1
  302.4 26.7 %collective-permute-done.7 = bf16[512,1408]{1,0:T(8,128)(2,1)S(1)} collective-permute-done((bf16[512,1408]{1,0:T(8,128)(2,1)S(1)}, bf16[512,1408]{1,0:T(8,128)(2,1)S(1)}, u32[]{:S(2)}, u32[]{:S(2)}) %collective-permute-start.7) | collective-permute-done | bytes 1441824 | tf_op jit(solution)/shard_map/ppermute | solution.py:17
  329.1 3.6 fusion.16
  333.3 25.4 %collective-permute-done.60 = bf16[512,1408]{1,0:T(8,128)(2,1)S(1)} collective-permute-done((bf16[512,1408]{1,0:T(8,128)(2,1)S(1)}, bf16[512,1408]{1,0:T(8,128)(2,1)S(1)}, u32[]{:S(2)}, u32[]{:S(2)}) %collective-permute-start.60) | collective-permute-done | bytes 1441824 | tf_op jit(solution)/shard_map/ppermute | solution.py:17
  358.7 3.4 multiply_convert_fusion
  362.1 3.4 fusion.112
  366.7 3.0 collective-permute-start.12
  371.3 2.3 collective-permute-done.10
  373.7 3.0 collective-permute-start.13
  377.4 4.4 collective-permute-done.13
  381.8 3.7 collective-permute-start.71
  388.3 3.6 collective-permute-start.72
  392.8 3.3 collective-permute-start.15
  396.8 2.7 collective-permute-done.70
  415.9 4.0 collective-permute-done.16
  420.5 6.0 %fusion.12 = f32[2816,1024]{1,0:T(8,128)} fusion(bf16[512,1408]{1,0:T(8,128)(2,1)S(1)} %get-tuple-element.30, bf16[512,1408]{1,0:T(8,128)(2,1)S(1)} %get-tuple-element.29, bf16[512,2048]{1,0:T(8,128)(2,1)S(1)} %bitcast.577, pred[]{:T(512)S(6)} %eq.142), kind=kOutput, calls=%fused_computation.22 | convolution fusion | flops 2959081472 | bytes 16515073 | tf_op jit(solution)/shard_map/dot_general | solution.py:113
  429.9 5.1 collective-permute-done.18
  435.2 6.1 %collective-permute-done.19 = bf16[32,2048]{1,0:T(8,128)(2,1)S(1)} collective-permute-done((bf16[32,2048]{1,0:T(8,128)(2,1)S(1)}, bf16[32,2048]{1,0:T(8,128)(2,1)S(1)}, u32[]{:S(2)}, u32[]{:S(2)}) %collective-permute-start.19) | collective-permute-done | bytes 131104 | tf_op jit(solution)/shard_map/ppermute | solution.py:21
  441.7 2.6 collective-permute-done.21
  444.4 4.5 convolution_convert_fusion.4
  450.0 3.3 fusion.5
  453.3 8.7 %fusion = bf16[1,1024,2816]{2,1,0:T(8,128)(2,1)} fusion(f32[1024,2816]{1,0:T(8,128)S(1)} %fusion.5, bf16[512,1408]{1,0:T(8,128)(2,1)} %get-tuple-element.34, bf16[512,1408]{1,0:T(8,128)(2,1)} %get-tuple-element.33, bf16[512,2048]{1,0:T(8,128)(2,1)} %bitcast.575, pred[]{:T(512)S(6)} %eq.142), kind=kOutput, calls=%fused_computation.4 | convolution fusion | flops 2964848640 | bytes 22282240 | tf_op jit(solution)/shard_map/dot_general | solution.py:113
  462.0 21.0 %collective-permute-done.22 = bf16[512,1408]{1,0:T(8,128)(2,1)} collective-permute-done((bf16[512,1408]{1,0:T(8,128)(2,1)}, bf16[512,1408]{1,0:T(8,128)(2,1)}, u32[]{:S(2)}, u32[]{:S(2)}) %collective-permute-start.22) | collective-permute-done | bytes 1441824 | tf_op jit(solution)/shard_map/ppermute | solution.py:17
  483.0 5.4 %fusion.17 = f32[512,2048]{1,0:T(8,128)S(1)} fusion(bf16[512,1408]{1,0:T(8,128)(2,1)} %collective-permute-done.22, bf16[512,1408]{1,0:T(8,128)(2,1)} %convolution_convert_fusion.4, bf16[1408,1024]{1,0:T(8,128)(2,1)S(1)} %copy-done.9, bf16[1408,1024]{1,0:T(8,128)(2,1)S(1)} %copy-done.6), kind=kOutput, calls=%fused_computation.53 | convolution fusion | flops 2970091520 | bytes 12845056 | tf_op jit(solution)/shard_map/dot_general | solution.py:212
  488.7 8.6 %fusion.1 = bf16[1,2816,1024]{2,1,0:T(8,128)(2,1)} fusion(f32[2816,1024]{1,0:T(8,128)} %fusion.12, bf16[512,1408]{1,0:T(8,128)(2,1)S(1)} %copy-done.19, bf16[512,1408]{1,0:T(8,128)(2,1)S(1)} %copy-done.18, bf16[512,2048]{1,0:T(8,128)(2,1)} %bitcast.573, pred[]{:T(512)S(6)} %eq.142), kind=kOutput, calls=%fused_computation.5 | convolution fusion | flops 2964848640 | bytes 22282240 | tf_op jit(solution)/shard_map/dot_general | solution.py:113
  510.7 2.5 collective-permute-start.27
  514.8 2.9 collective-permute-start.79
  517.7 2.4 collective-permute-start.80
  520.1 4.3 collective-permute-start.81
  (500 shorter events, 140.7 us)
Async XLA Ops:
  0.6 57.4 %collective-permute-start.31 = (bf16[2,3,32,512]{3,2,1,0:T(8,128)(2,1)}, bf16[2,3,32,512]{3,2,1,0:T(8,128)(2,1)S(1)}, u32[]{:S(2)}, u32[]{:S(2)}) collective-permute-start(bf16[2,3,32,512]{3,2,1,0:T(8,128)(2,1)} %bitcast.546), channel_id=1, source_target_pairs={{64,112},{80,64},{96,80},{112,96},{65,113},{81,65},{97,81},{113,97... | collective-permute-start | bytes 589832 | tf_op jit(solution)/shard_map/ppermute | solution.py:25
  5.3 56.7 %collective-permute-start.30 = (bf16[2,3,32,512]{3,2,1,0:T(8,128)(2,1)}, bf16[2,3,32,512]{3,2,1,0:T(8,128)(2,1)S(1)}, u32[]{:S(2)}, u32[]{:S(2)}) collective-permute-start(bf16[2,3,32,512]{3,2,1,0:T(8,128)(2,1)} %bitcast.547), channel_id=1, source_target_pairs={{64,96},{80,112},{96,64},{112,80},{65,97},{81,113},{97,65},{113,81... | collective-permute-start | bytes 589832 | tf_op jit(solution)/shard_map/ppermute | solution.py:25
  8.0 56.5 %collective-permute-start.29 = (bf16[2,3,32,512]{3,2,1,0:T(8,128)(2,1)}, bf16[2,3,32,512]{3,2,1,0:T(8,128)(2,1)S(1)}, u32[]{:S(2)}, u32[]{:S(2)}) collective-permute-start(bf16[2,3,32,512]{3,2,1,0:T(8,128)(2,1)} %bitcast.548), channel_id=1, source_target_pairs={{64,80},{80,96},{96,112},{112,64},{65,81},{81,97},{97,113},{113,65... | collective-permute-start | bytes 589832 | tf_op jit(solution)/shard_map/ppermute | solution.py:25
  11.8 41.0 %collective-permute-start.33 = (bf16[32,2048]{1,0:T(8,128)(2,1)S(1)}, bf16[32,2048]{1,0:T(8,128)(2,1)S(1)}, u32[]{:S(2)}, u32[]{:S(2)}) collective-permute-start(bf16[32,2048]{1,0:T(8,128)(2,1)S(1)} %broadcast_select_fusion.26), channel_id=1, source_target_pairs={{0,8},{4,12},{8,0},{12,4},{1,9},{5,13},{9,1},{13,5},{2,10},{6,14},... | collective-permute-start | bytes 393224 | tf_op jit(solution)/shard_map/ppermute | solution.py:17
  22.2 30.5 %collective-permute-start.74 = (bf16[3,32,512]{2,1,0:T(8,128)(2,1)S(1)}, bf16[3,32,512]{2,1,0:T(8,128)(2,1)}, u32[]{:S(2)}, u32[]{:S(2)}) collective-permute-start(bf16[3,32,512]{2,1,0:T(8,128)(2,1)S(1)} %pad_maximum_fusion.27), channel_id=1, source_target_pairs={{0,64},{16,80},{32,96},{48,112},{1,65},{17,81},{33,97},{49,113},{2... | collective-permute-start | bytes 294920 | tf_op jit(solution)/shard_map/ppermute | solution.py:170
  52.7 63.8 %collective-permute-start.6 = (bf16[1024,1408]{1,0:T(8,128)(2,1)}, bf16[1024,1408]{1,0:T(8,128)(2,1)}, u32[]{:S(2)}, u32[]{:S(2)}) collective-permute-start(bf16[1024,1408]{1,0:T(8,128)(2,1)} %broadcast_select_fusion.3), channel_id=1, source_target_pairs={{0,4},{4,0},{8,12},{12,8},{1,5},{5,1},{9,13},{13,9},{2,6},{6,2},{1... | collective-permute-start | bytes 8650760 | tf_op jit(solution)/shard_map/ppermute | solution.py:13
  52.8 14.9 %collective-permute-start.75 = (bf16[3,32,512]{2,1,0:T(8,128)(2,1)}, bf16[3,32,512]{2,1,0:T(8,128)(2,1)S(1)}, u32[]{:S(2)}, u32[]{:S(2)}) collective-permute-start(bf16[3,32,512]{2,1,0:T(8,128)(2,1)} %collective-permute-done.74), channel_id=1, source_target_pairs={{64,80},{80,96},{96,112},{112,64},{65,81},{81,97},{97,113},{113,65... | collective-permute-start | bytes 294920 | tf_op jit(solution)/shard_map/ppermute | solution.py:25
  58.0 9.8 %collective-permute-start.76 = (bf16[3,32,512]{2,1,0:T(8,128)(2,1)}, bf16[3,32,512]{2,1,0:T(8,128)(2,1)S(1)}, u32[]{:S(2)}, u32[]{:S(2)}) collective-permute-start(bf16[3,32,512]{2,1,0:T(8,128)(2,1)} %collective-permute-done.74), channel_id=1, source_target_pairs={{64,96},{80,112},{96,64},{112,80},{65,97},{81,113},{97,65},{113,81... | collective-permute-start | bytes 294920 | tf_op jit(solution)/shard_map/ppermute | solution.py:25
  64.6 8.7 %collective-permute-start.34 = (bf16[2,32,2048]{2,1,0:T(8,128)(2,1)S(1)}, bf16[2,32,2048]{2,1,0:T(8,128)(2,1)S(1)}, u32[]{:S(2)}, u32[]{:S(2)}) collective-permute-start(bf16[2,32,2048]{2,1,0:T(8,128)(2,1)S(1)} %get-tuple-element.108), channel_id=1, source_target_pairs={{0,3},{1,0},{2,1},{3,2},{4,7},{5,4},{6,5},{7,6},{8,11},{9,8},{10,9... | collective-permute-start | bytes 786440 | tf_op jit(solution)/shard_map/ppermute | solution.py:21
  67.7 57.0 %collective-permute-start.8 = (bf16[1408,1024]{1,0:T(8,128)(2,1)}, bf16[1408,1024]{1,0:T(8,128)(2,1)}, u32[]{:S(2)}, u32[]{:S(2)}) collective-permute-start(bf16[1408,1024]{1,0:T(8,128)(2,1)} %select_bitcast_fusion), channel_id=1, source_target_pairs={{0,4},{4,0},{8,12},{12,8},{1,5},{5,1},{9,13},{13,9},{2,6},{6,2},{1... | collective-permute-start | bytes 8650760 | tf_op jit(solution)/shard_map/ppermute | solution.py:13
  67.9 9.9 %collective-permute-start.35 = (bf16[2,32,2048]{2,1,0:T(8,128)(2,1)S(1)}, bf16[2,32,2048]{2,1,0:T(8,128)(2,1)S(1)}, u32[]{:S(2)}, u32[]{:S(2)}) collective-permute-start(bf16[2,32,2048]{2,1,0:T(8,128)(2,1)S(1)} %get-tuple-element.108), channel_id=1, source_target_pairs={{0,1},{1,2},{2,3},{3,0},{4,5},{5,6},{6,7},{7,4},{8,9},{9,10},{10,1... | collective-permute-start | bytes 786440 | tf_op jit(solution)/shard_map/ppermute | solution.py:21
  68.7 10.5 %collective-permute-start.32 = (bf16[2,3,32,512]{3,2,1,0:T(8,128)(2,1)S(1)}, bf16[2,3,32,512]{3,2,1,0:T(8,128)(2,1)S(1)}, u32[]{:S(2)}, u32[]{:S(2)}) collective-permute-start(bf16[2,3,32,512]{3,2,1,0:T(8,128)(2,1)S(1)} %pad_maximum_fusion.26), channel_id=1, source_target_pairs={{64,0},{80,16},{96,32},{112,48},{65,1},{81,17},{97,33},{113,49},{6... | collective-permute-start | bytes 589832 | tf_op jit(solution)/shard_map/ppermute | solution.py:165
  74.0 20.8 %collective-permute-start.37 = (bf16[32,2048]{1,0:T(8,128)(2,1)}, bf16[32,2048]{1,0:T(8,128)(2,1)}, u32[]{:S(2)}, u32[]{:S(2)}) collective-permute-start(bf16[32,2048]{1,0:T(8,128)(2,1)} %slice_bitcast_fusion.22), channel_id=1, source_target_pairs={{0,3},{1,0},{2,1},{3,2},{4,7},{5,4},{6,5},{7,6},{8,11},{9,8},{10,9... | collective-permute-start | bytes 393224 | tf_op jit(solution)/shard_map/ppermute | solution.py:21
  78.4 19.6 %collective-permute-start.36 = (bf16[32,2048]{1,0:T(8,128)(2,1)}, bf16[32,2048]{1,0:T(8,128)(2,1)}, u32[]{:S(2)}, u32[]{:S(2)}) collective-permute-start(bf16[32,2048]{1,0:T(8,128)(2,1)} %slice_bitcast_fusion.23), channel_id=1, source_target_pairs={{0,1},{1,2},{2,3},{3,0},{4,5},{5,6},{6,7},{7,4},{8,9},{9,10},{10,1... | collective-permute-start | bytes 393224 | tf_op jit(solution)/shard_map/ppermute | solution.py:21
  94.3 8.4 %collective-permute-start.61 = (bf16[32,2048]{1,0:T(8,128)(2,1)S(1)}, bf16[32,2048]{1,0:T(8,128)(2,1)S(1)}, u32[]{:S(2)}, u32[]{:S(2)}) collective-permute-start(bf16[32,2048]{1,0:T(8,128)(2,1)S(1)} %broadcast_select_fusion.20), channel_id=1, source_target_pairs={{0,8},{4,12},{8,0},{12,4},{1,9},{5,13},{9,1},{13,5},{2,10},{6,14},... | collective-permute-start | bytes 393224 | tf_op jit(solution)/shard_map/ppermute | solution.py:17
  94.8 8.1 %collective-permute-start.41 = (bf16[2,32,2048]{2,1,0:T(8,128)(2,1)S(1)}, bf16[2,32,2048]{2,1,0:T(8,128)(2,1)S(1)}, u32[]{:S(2)}, u32[]{:S(2)}) collective-permute-start(bf16[2,32,2048]{2,1,0:T(8,128)(2,1)S(1)} %get-tuple-element.106), channel_id=1, source_target_pairs={{0,3},{1,0},{2,1},{3,2},{4,7},{5,4},{6,5},{7,6},{8,11},{9,8},{10,9... | collective-permute-start | bytes 786440 | tf_op jit(solution)/shard_map/ppermute | solution.py:21
  98.0 8.2 %collective-permute-start.42 = (bf16[2,32,2048]{2,1,0:T(8,128)(2,1)S(1)}, bf16[2,32,2048]{2,1,0:T(8,128)(2,1)S(1)}, u32[]{:S(2)}, u32[]{:S(2)}) collective-permute-start(bf16[2,32,2048]{2,1,0:T(8,128)(2,1)S(1)} %get-tuple-element.106), channel_id=1, source_target_pairs={{0,1},{1,2},{2,3},{3,0},{4,5},{5,6},{6,7},{7,4},{8,9},{9,10},{10,1... | collective-permute-start | bytes 786440 | tf_op jit(solution)/shard_map/ppermute | solution.py:21
  102.7 11.2 %collective-permute-start.38 = (bf16[4,2,32,2048]{3,2,1,0:T(8,128)(2,1)S(1)}, bf16[4,2,32,2048]{3,2,1,0:T(8,128)(2,1)S(1)}, u32[]{:S(2)}, u32[]{:S(2)}) collective-permute-start(bf16[4,2,32,2048]{3,2,1,0:T(8,128)(2,1)S(1)} %pad_maximum_fusion.8), channel_id=1, source_target_pairs={{0,4},{4,0},{8,12},{12,8},{1,5},{5,1},{9,13},{13,9},{2,6},{6,2},{1... | collective-permute-start | bytes 3145736 | tf_op jit(solution)/shard_map/ppermute | solution.py:13
  106.2 7.1 %collective-permute-start.43 = (bf16[32,2048]{1,0:T(8,128)(2,1)S(1)}, bf16[32,2048]{1,0:T(8,128)(2,1)S(1)}, u32[]{:S(2)}, u32[]{:S(2)}) collective-permute-start(bf16[32,2048]{1,0:T(8,128)(2,1)S(1)} %slice_bitcast_fusion.21), channel_id=1, source_target_pairs={{0,1},{1,2},{2,3},{3,0},{4,5},{5,6},{6,7},{7,4},{8,9},{9,10},{10,1... | collective-permute-start | bytes 393224 | tf_op jit(solution)/shard_map/ppermute | solution.py:21
  109.6 22.1 %collective-permute-start.62 = (bf16[2,32,2048]{2,1,0:T(8,128)(2,1)S(1)}, bf16[2,32,2048]{2,1,0:T(8,128)(2,1)S(1)}, u32[]{:S(2)}, u32[]{:S(2)}) collective-permute-start(bf16[2,32,2048]{2,1,0:T(8,128)(2,1)S(1)} %get-tuple-element.102), channel_id=1, source_target_pairs={{0,3},{1,0},{2,1},{3,2},{4,7},{5,4},{6,5},{7,6},{8,11},{9,8},{10,9... | collective-permute-start | bytes 786440 | tf_op jit(solution)/shard_map/ppermute | solution.py:21
  113.9 19.4 %collective-permute-start.63 = (bf16[2,32,2048]{2,1,0:T(8,128)(2,1)S(1)}, bf16[2,32,2048]{2,1,0:T(8,128)(2,1)S(1)}, u32[]{:S(2)}, u32[]{:S(2)}) collective-permute-start(bf16[2,32,2048]{2,1,0:T(8,128)(2,1)S(1)} %get-tuple-element.102), channel_id=1, source_target_pairs={{0,1},{1,2},{2,3},{3,0},{4,5},{5,6},{6,7},{7,4},{8,9},{9,10},{10,1... | collective-permute-start | bytes 786440 | tf_op jit(solution)/shard_map/ppermute | solution.py:21
  123.0 34.5 %collective-permute-start.46 = (bf16[512,1408]{1,0:T(8,128)(2,1)S(1)}, bf16[512,1408]{1,0:T(8,128)(2,1)S(1)}, u32[]{:S(2)}, u32[]{:S(2)}) collective-permute-start(bf16[512,1408]{1,0:T(8,128)(2,1)S(1)} %convolution_convert_fusion.2), channel_id=1, source_target_pairs={{0,8},{4,12},{8,0},{12,4},{1,9},{5,13},{9,1},{13,5},{2,10},{6,14},... | collective-permute-start | bytes 4325384 | tf_op jit(solution)/shard_map/ppermute | solution.py:17
  130.4 57.2 %collective-permute-start.39 = (bf16[512,1408]{1,0:T(8,128)(2,1)S(1)}, bf16[512,1408]{1,0:T(8,128)(2,1)S(1)}, u32[]{:S(2)}, u32[]{:S(2)}) collective-permute-start(bf16[512,1408]{1,0:T(8,128)(2,1)S(1)} %convolution_convert_fusion.3), channel_id=1, source_target_pairs={{0,8},{4,12},{8,0},{12,4},{1,9},{5,13},{9,1},{13,5},{2,10},{6,14},... | collective-permute-start | bytes 4325384 | tf_op jit(solution)/shard_map/ppermute | solution.py:17
  139.8 62.0 %collective-permute-start.66 = (bf16[4,2,32,2048]{3,2,1,0:T(8,128)(2,1)S(1)}, bf16[4,2,32,2048]{3,2,1,0:T(8,128)(2,1)S(1)}, u32[]{:S(2)}, u32[]{:S(2)}) collective-permute-start(bf16[4,2,32,2048]{3,2,1,0:T(8,128)(2,1)S(1)} %pad_maximum_fusion.11), channel_id=1, source_target_pairs={{0,4},{4,0},{8,12},{12,8},{1,5},{5,1},{9,13},{13,9},{2,6},{6,2},{1... | collective-permute-start | bytes 3145736 | tf_op jit(solution)/shard_map/ppermute | solution.py:13
  192.9 11.5 %collective-permute-start.47 = (bf16[256,2048]{1,0:T(8,128)(2,1)S(1)}, bf16[256,2048]{1,0:T(8,128)(2,1)S(1)}, u32[]{:S(2)}, u32[]{:S(2)}) collective-permute-start(bf16[256,2048]{1,0:T(8,128)(2,1)S(1)} %slice.920), channel_id=1, source_target_pairs={{0,4},{4,0},{8,12},{12,8},{1,5},{5,1},{9,13},{13,9},{2,6},{6,2},{1... | collective-permute-start | bytes 3145736 | tf_op jit(solution)/shard_map/ppermute | solution.py:13
  202.0 14.8 %collective-permute-start.82 = (bf16[512,1408]{1,0:T(8,128)(2,1)S(1)}, bf16[512,1408]{1,0:T(8,128)(2,1)S(1)}, u32[]{:S(2)}, u32[]{:S(2)}) collective-permute-start(bf16[512,1408]{1,0:T(8,128)(2,1)S(1)} %get-tuple-element.28), channel_id=1, source_target_pairs={{0,4},{4,0},{8,12},{12,8},{1,5},{5,1},{9,13},{13,9},{2,6},{6,2},{1... | collective-permute-start | bytes 4325384 | tf_op jit(solution)/shard_map/ppermute | solution.py:13
  204.9 9.5 %collective-permute-start.48 = (bf16[32,2048]{1,0:T(8,128)(2,1)S(1)}, bf16[32,2048]{1,0:T(8,128)(2,1)S(1)}, u32[]{:S(2)}, u32[]{:S(2)}) collective-permute-start(bf16[32,2048]{1,0:T(8,128)(2,1)S(1)} %get-tuple-element.57), channel_id=1, source_target_pairs={{0,1},{1,2},{2,3},{3,0},{4,5},{5,6},{6,7},{7,4},{8,9},{9,10},{10,1... | collective-permute-start | bytes 393224 | tf_op jit(solution)/shard_map/ppermute | solution.py:21
  205.0 9.5 %collective-permute-start.50 = (bf16[32,2048]{1,0:T(8,128)(2,1)S(1)}, bf16[32,2048]{1,0:T(8,128)(2,1)S(1)}, u32[]{:S(2)}, u32[]{:S(2)}) collective-permute-start(bf16[32,2048]{1,0:T(8,128)(2,1)S(1)} %get-tuple-element.58), channel_id=1, source_target_pairs={{0,3},{1,0},{2,1},{3,2},{4,7},{5,4},{6,5},{7,6},{8,11},{9,8},{10,9... | collective-permute-start | bytes 393224 | tf_op jit(solution)/shard_map/ppermute | solution.py:21
  212.8 120.5 %collective-permute-start.67 = (bf16[512,1408]{1,0:T(8,128)(2,1)}, bf16[512,1408]{1,0:T(8,128)(2,1)}, u32[]{:S(2)}, u32[]{:S(2)}) collective-permute-start(bf16[512,1408]{1,0:T(8,128)(2,1)} %convolution_convert_fusion), channel_id=1, source_target_pairs={{0,8},{4,12},{8,0},{12,4},{1,9},{5,13},{9,1},{13,5},{2,10},{6,14},... | collective-permute-start | bytes 4325384 | tf_op jit(solution)/shard_map/ppermute | solution.py:17
  214.4 41.1 %collective-permute-start.84 = (bf16[512,1408]{1,0:T(8,128)(2,1)S(1)}, bf16[512,1408]{1,0:T(8,128)(2,1)}, u32[]{:S(2)}, u32[]{:S(2)}) collective-permute-start(bf16[512,1408]{1,0:T(8,128)(2,1)S(1)} %get-tuple-element.27), channel_id=1, source_target_pairs={{0,4},{4,0},{8,12},{12,8},{1,5},{5,1},{9,13},{13,9},{2,6},{6,2},{1... | collective-permute-start | bytes 4325384 | tf_op jit(solution)/shard_map/ppermute | solution.py:13
  214.6 8.8 %collective-permute-start.51 = (bf16[2,32,2048]{2,1,0:T(8,128)(2,1)S(1)}, bf16[2,32,2048]{2,1,0:T(8,128)(2,1)S(1)}, u32[]{:S(2)}, u32[]{:S(2)}) collective-permute-start(bf16[2,32,2048]{2,1,0:T(8,128)(2,1)S(1)} %pad_maximum_fusion.21), channel_id=1, source_target_pairs={{0,3},{1,0},{2,1},{3,2},{4,7},{5,4},{6,5},{7,6},{8,11},{9,8},{10,9... | collective-permute-start | bytes 786440 | tf_op jit(solution)/shard_map/ppermute | solution.py:21
  215.1 9.7 %collective-permute-start.49 = (bf16[2,32,2048]{2,1,0:T(8,128)(2,1)S(1)}, bf16[2,32,2048]{2,1,0:T(8,128)(2,1)S(1)}, u32[]{:S(2)}, u32[]{:S(2)}) collective-permute-start(bf16[2,32,2048]{2,1,0:T(8,128)(2,1)S(1)} %pad_maximum_fusion.20), channel_id=1, source_target_pairs={{0,1},{1,2},{2,3},{3,0},{4,5},{5,6},{6,7},{7,4},{8,9},{9,10},{10,1... | collective-permute-start | bytes 786440 | tf_op jit(solution)/shard_map/ppermute | solution.py:21
  224.9 24.0 %collective-permute-start.52 = (bf16[32,2048]{1,0:T(8,128)(2,1)S(1)}, bf16[32,2048]{1,0:T(8,128)(2,1)S(1)}, u32[]{:S(2)}, u32[]{:S(2)}) collective-permute-start(bf16[32,2048]{1,0:T(8,128)(2,1)S(1)} %select_bitcast_fusion.7), channel_id=1, source_target_pairs={{0,8},{4,12},{8,0},{12,4},{1,9},{5,13},{9,1},{13,5},{2,10},{6,14},... | collective-permute-start | bytes 393224 | tf_op jit(solution)/shard_map/ppermute | solution.py:17
  256.9 8.6 %collective-permute-start.53 = (bf16[32,4096]{1,0:T(8,128)(2,1)S(1)}, bf16[32,4096]{1,0:T(8,128)(2,1)S(1)}, u32[]{:S(2)}, u32[]{:S(2)}) collective-permute-start(bf16[32,4096]{1,0:T(8,128)(2,1)S(1)} %get-tuple-element.121), channel_id=1, source_target_pairs={{16,0},{32,16},{48,32},{64,48},{80,64},{96,80},{112,96},{17,1},{33... | collective-permute-start | bytes 786440 | tf_op jit(solution)/shard_map/ppermute | solution.py:30
  259.1 13.7 %collective-permute-start.1 = (bf16[2,32,2048]{2,1,0:T(8,128)(2,1)S(1)}, bf16[2,32,2048]{2,1,0:T(8,128)(2,1)S(1)}, u32[]{:S(2)}, u32[]{:S(2)}) collective-permute-start(bf16[2,32,2048]{2,1,0:T(8,128)(2,1)S(1)} %get-tuple-element.112), channel_id=1, source_target_pairs={{0,3},{1,0},{2,1},{3,2},{4,7},{5,4},{6,5},{7,6},{8,11},{9,8},{10,9... | collective-permute-start | bytes 786440 | tf_op jit(solution)/shard_map/ppermute | solution.py:21
  259.5 15.0 %collective-permute-start.2 = (bf16[2,32,2048]{2,1,0:T(8,128)(2,1)S(1)}, bf16[2,32,2048]{2,1,0:T(8,128)(2,1)S(1)}, u32[]{:S(2)}, u32[]{:S(2)}) collective-permute-start(bf16[2,32,2048]{2,1,0:T(8,128)(2,1)S(1)} %get-tuple-element.112), channel_id=1, source_target_pairs={{0,1},{1,2},{2,3},{3,0},{4,5},{5,6},{6,7},{7,4},{8,9},{9,10},{10,1... | collective-permute-start | bytes 786440 | tf_op jit(solution)/shard_map/ppermute | solution.py:21
  270.7 10.4 %collective-permute-start.55 = (bf16[2,32,2048]{2,1,0:T(8,128)(2,1)S(1)}, bf16[2,32,2048]{2,1,0:T(8,128)(2,1)S(1)}, u32[]{:S(2)}, u32[]{:S(2)}) collective-permute-start(bf16[2,32,2048]{2,1,0:T(8,128)(2,1)S(1)} %get-tuple-element.104), channel_id=1, source_target_pairs={{0,3},{1,0},{2,1},{3,2},{4,7},{5,4},{6,5},{7,6},{8,11},{9,8},{10,9... | collective-permute-start | bytes 786440 | tf_op jit(solution)/shard_map/ppermute | solution.py:21
  271.2 10.0 %collective-permute-start.56 = (bf16[2,32,2048]{2,1,0:T(8,128)(2,1)S(1)}, bf16[2,32,2048]{2,1,0:T(8,128)(2,1)S(1)}, u32[]{:S(2)}, u32[]{:S(2)}) collective-permute-start(bf16[2,32,2048]{2,1,0:T(8,128)(2,1)S(1)} %get-tuple-element.104), channel_id=1, source_target_pairs={{0,1},{1,2},{2,3},{3,0},{4,5},{5,6},{6,7},{7,4},{8,9},{9,10},{10,1... | collective-permute-start | bytes 786440 | tf_op jit(solution)/shard_map/ppermute | solution.py:21
  281.0 8.0 %collective-permute-start.5 = (bf16[4,2,32,2048]{3,2,1,0:T(8,128)(2,1)S(1)}, bf16[4,2,32,2048]{3,2,1,0:T(8,128)(2,1)S(1)}, u32[]{:S(2)}, u32[]{:S(2)}) collective-permute-start(bf16[4,2,32,2048]{3,2,1,0:T(8,128)(2,1)S(1)} %pad_maximum_fusion.6), channel_id=1, source_target_pairs={{0,4},{4,0},{8,12},{12,8},{1,5},{5,1},{9,13},{13,9},{2,6},{6,2},{1... | collective-permute-start | bytes 3145736 | tf_op jit(solution)/shard_map/ppermute | solution.py:13
  281.2 7.2 %collective-permute-start.57 = (bf16[32,2048]{1,0:T(8,128)(2,1)S(1)}, bf16[32,2048]{1,0:T(8,128)(2,1)S(1)}, u32[]{:S(2)}, u32[]{:S(2)}) collective-permute-start(bf16[32,2048]{1,0:T(8,128)(2,1)S(1)} %slice_bitcast_fusion.15), channel_id=1, source_target_pairs={{0,1},{1,2},{2,3},{3,0},{4,5},{5,6},{6,7},{7,4},{8,9},{9,10},{10,1... | collective-permute-start | bytes 393224 | tf_op jit(solution)/shard_map/ppermute | solution.py:21
  294.5 34.6 %collective-permute-start.7 = (bf16[512,1408]{1,0:T(8,128)(2,1)S(1)}, bf16[512,1408]{1,0:T(8,128)(2,1)S(1)}, u32[]{:S(2)}, u32[]{:S(2)}) collective-permute-start(bf16[512,1408]{1,0:T(8,128)(2,1)S(1)} %convolution_convert_fusion.5), channel_id=1, source_target_pairs={{0,8},{4,12},{8,0},{12,4},{1,9},{5,13},{9,1},{13,5},{2,10},{6,14},... | collective-permute-start | bytes 4325384 | tf_op jit(solution)/shard_map/ppermute | solution.py:17
  298.6 60.1 %collective-permute-start.60 = (bf16[512,1408]{1,0:T(8,128)(2,1)S(1)}, bf16[512,1408]{1,0:T(8,128)(2,1)S(1)}, u32[]{:S(2)}, u32[]{:S(2)}) collective-permute-start(bf16[512,1408]{1,0:T(8,128)(2,1)S(1)} %convolution_convert_fusion.1), channel_id=1, source_target_pairs={{0,8},{4,12},{8,0},{12,4},{1,9},{5,13},{9,1},{13,5},{2,10},{6,14},... | collective-permute-start | bytes 4325384 | tf_op jit(solution)/shard_map/ppermute | solution.py:17
  332.8 33.0 %collective-permute-start.9 = (bf16[256,2048]{1,0:T(8,128)(2,1)S(1)}, bf16[256,2048]{1,0:T(8,128)(2,1)S(1)}, u32[]{:S(2)}, u32[]{:S(2)}) collective-permute-start(bf16[256,2048]{1,0:T(8,128)(2,1)S(1)} %slice.922), channel_id=1, source_target_pairs={{0,4},{4,0},{8,12},{12,8},{1,5},{5,1},{9,13},{13,9},{2,6},{6,2},{1... | collective-permute-start | bytes 3145736 | tf_op jit(solution)/shard_map/ppermute | solution.py:13
  365.7 11.1 %collective-permute-start.68 = (bf16[256,2048]{1,0:T(8,128)(2,1)S(1)}, bf16[256,2048]{1,0:T(8,128)(2,1)S(1)}, u32[]{:S(2)}, u32[]{:S(2)}) collective-permute-start(bf16[256,2048]{1,0:T(8,128)(2,1)S(1)} %slice.919), channel_id=1, source_target_pairs={{0,4},{4,0},{8,12},{12,8},{1,5},{5,1},{9,13},{13,9},{2,6},{6,2},{1... | collective-permute-start | bytes 3145736 | tf_op jit(solution)/shard_map/ppermute | solution.py:13
  366.4 7.2 %collective-permute-start.10 = (bf16[32,2048]{1,0:T(8,128)(2,1)S(1)}, bf16[32,2048]{1,0:T(8,128)(2,1)S(1)}, u32[]{:S(2)}, u32[]{:S(2)}) collective-permute-start(bf16[32,2048]{1,0:T(8,128)(2,1)S(1)} %get-tuple-element.65), channel_id=1, source_target_pairs={{0,1},{1,2},{2,3},{3,0},{4,5},{5,6},{6,7},{7,4},{8,9},{9,10},{10,1... | collective-permute-start | bytes 393224 | tf_op jit(solution)/shard_map/ppermute | solution.py:21
  370.8 29.6 %collective-permute-start.83 = (bf16[512,1408]{1,0:T(8,128)(2,1)S(1)}, bf16[512,1408]{1,0:T(8,128)(2,1)S(1)}, u32[]{:S(2)}, u32[]{:S(2)}) collective-permute-start(bf16[512,1408]{1,0:T(8,128)(2,1)S(1)} %get-tuple-element.32), channel_id=1, source_target_pairs={{0,4},{4,0},{8,12},{12,8},{1,5},{5,1},{9,13},{13,9},{2,6},{6,2},{1... | collective-permute-start | bytes 4325384 | tf_op jit(solution)/shard_map/ppermute | solution.py:13
  370.8 31.3 %collective-permute-start.85 = (bf16[512,1408]{1,0:T(8,128)(2,1)S(1)}, bf16[512,1408]{1,0:T(8,128)(2,1)S(1)}, u32[]{:S(2)}, u32[]{:S(2)}) collective-permute-start(bf16[512,1408]{1,0:T(8,128)(2,1)S(1)} %get-tuple-element.31), channel_id=1, source_target_pairs={{0,4},{4,0},{8,12},{12,8},{1,5},{5,1},{9,13},{13,9},{2,6},{6,2},{1... | collective-permute-start | bytes 4325384 | tf_op jit(solution)/shard_map/ppermute | solution.py:13
  373.7 8.1 %collective-permute-start.13 = (bf16[2,32,2048]{2,1,0:T(8,128)(2,1)S(1)}, bf16[2,32,2048]{2,1,0:T(8,128)(2,1)S(1)}, u32[]{:S(2)}, u32[]{:S(2)}) collective-permute-start(bf16[2,32,2048]{2,1,0:T(8,128)(2,1)S(1)} %pad_maximum_fusion.14), channel_id=1, source_target_pairs={{0,3},{1,0},{2,1},{3,2},{4,7},{5,4},{6,5},{7,6},{8,11},{9,8},{10,9... | collective-permute-start | bytes 786440 | tf_op jit(solution)/shard_map/ppermute | solution.py:21
  376.7 10.0 %collective-permute-start.11 = (bf16[2,32,2048]{2,1,0:T(8,128)(2,1)S(1)}, bf16[2,32,2048]{2,1,0:T(8,128)(2,1)S(1)}, u32[]{:S(2)}, u32[]{:S(2)}) collective-permute-start(bf16[2,32,2048]{2,1,0:T(8,128)(2,1)S(1)} %pad_maximum_fusion.13), channel_id=1, source_target_pairs={{0,1},{1,2},{2,3},{3,0},{4,5},{5,6},{6,7},{7,4},{8,9},{9,10},{10,1... | collective-permute-start | bytes 786440 | tf_op jit(solution)/shard_map/ppermute | solution.py:21
  377.4 10.8 %collective-permute-start.69 = (bf16[32,2048]{1,0:T(8,128)(2,1)S(1)}, bf16[32,2048]{1,0:T(8,128)(2,1)S(1)}, u32[]{:S(2)}, u32[]{:S(2)}) collective-permute-start(bf16[32,2048]{1,0:T(8,128)(2,1)S(1)} %get-tuple-element.53), channel_id=1, source_target_pairs={{0,1},{1,2},{2,3},{3,0},{4,5},{5,6},{6,7},{7,4},{8,9},{9,10},{10,1... | collective-permute-start | bytes 393224 | tf_op jit(solution)/shard_map/ppermute | solution.py:21
  388.3 8.6 %collective-permute-start.72 = (bf16[2,32,2048]{2,1,0:T(8,128)(2,1)S(1)}, bf16[2,32,2048]{2,1,0:T(8,128)(2,1)S(1)}, u32[]{:S(2)}, u32[]{:S(2)}) collective-permute-start(bf16[2,32,2048]{2,1,0:T(8,128)(2,1)S(1)} %pad_maximum_fusion.25), channel_id=1, source_target_pairs={{0,3},{1,0},{2,1},{3,2},{4,7},{5,4},{6,5},{7,6},{8,11},{9,8},{10,9... | collective-permute-start | bytes 786440 | tf_op jit(solution)/shard_map/ppermute | solution.py:21
  391.9 7.7 %collective-permute-start.70 = (bf16[2,32,2048]{2,1,0:T(8,128)(2,1)S(1)}, bf16[2,32,2048]{2,1,0:T(8,128)(2,1)S(1)}, u32[]{:S(2)}, u32[]{:S(2)}) collective-permute-start(bf16[2,32,2048]{2,1,0:T(8,128)(2,1)S(1)} %pad_maximum_fusion.24), channel_id=1, source_target_pairs={{0,1},{1,2},{2,3},{3,0},{4,5},{5,6},{6,7},{7,4},{8,9},{9,10},{10,1... | collective-permute-start | bytes 786440 | tf_op jit(solution)/shard_map/ppermute | solution.py:21
  392.8 18.2 %collective-permute-start.15 = (bf16[32,4096]{1,0:T(8,128)(2,1)}, bf16[32,4096]{1,0:T(8,128)(2,1)}, u32[]{:S(2)}, u32[]{:S(2)}) collective-permute-start(bf16[32,4096]{1,0:T(8,128)(2,1)} %fusion.34), channel_id=1, source_target_pairs={{0,16},{16,32},{32,48},{48,64},{64,80},{80,96},{96,112},{1,17},{17... | collective-permute-start | bytes 786440 | tf_op jit(solution)/shard_map/ppermute | solution.py:30
  420.0 8.2 %collective-permute-start.17 = (bf16[2,32,2048]{2,1,0:T(8,128)(2,1)S(1)}, bf16[2,32,2048]{2,1,0:T(8,128)(2,1)S(1)}, u32[]{:S(2)}, u32[]{:S(2)}) collective-permute-start(bf16[2,32,2048]{2,1,0:T(8,128)(2,1)S(1)} %get-tuple-element.110), channel_id=1, source_target_pairs={{0,3},{1,0},{2,1},{3,2},{4,7},{5,4},{6,5},{7,6},{8,11},{9,8},{10,9... | collective-permute-start | bytes 786440 | tf_op jit(solution)/shard_map/ppermute | solution.py:21
  426.6 8.4 %collective-permute-start.18 = (bf16[2,32,2048]{2,1,0:T(8,128)(2,1)S(1)}, bf16[2,32,2048]{2,1,0:T(8,128)(2,1)S(1)}, u32[]{:S(2)}, u32[]{:S(2)}) collective-permute-start(bf16[2,32,2048]{2,1,0:T(8,128)(2,1)S(1)} %get-tuple-element.110), channel_id=1, source_target_pairs={{0,1},{1,2},{2,3},{3,0},{4,5},{5,6},{6,7},{7,4},{8,9},{9,10},{10,1... | collective-permute-start | bytes 786440 | tf_op jit(solution)/shard_map/ppermute | solution.py:21
  428.2 7.0 %collective-permute-start.20 = (bf16[32,2048]{1,0:T(8,128)(2,1)S(1)}, bf16[32,2048]{1,0:T(8,128)(2,1)S(1)}, u32[]{:S(2)}, u32[]{:S(2)}) collective-permute-start(bf16[32,2048]{1,0:T(8,128)(2,1)S(1)} %slice_bitcast_fusion.28), channel_id=1, source_target_pairs={{0,3},{1,0},{2,1},{3,2},{4,7},{5,4},{6,5},{7,6},{8,11},{9,8},{10,9... | collective-permute-start | bytes 393224 | tf_op jit(solution)/shard_map/ppermute | solution.py:21
  448.9 34.1 %collective-permute-start.22 = (bf16[512,1408]{1,0:T(8,128)(2,1)}, bf16[512,1408]{1,0:T(8,128)(2,1)}, u32[]{:S(2)}, u32[]{:S(2)}) collective-permute-start(bf16[512,1408]{1,0:T(8,128)(2,1)} %convolution_convert_fusion.4), channel_id=1, source_target_pairs={{0,8},{4,12},{8,0},{12,4},{1,9},{5,13},{9,1},{13,5},{2,10},{6,14},... | collective-permute-start | bytes 4325384 | tf_op jit(solution)/shard_map/ppermute | solution.py:17
  488.5 14.5 %collective-permute-start.23 = (bf16[256,2048]{1,0:T(8,128)(2,1)S(1)}, bf16[256,2048]{1,0:T(8,128)(2,1)S(1)}, u32[]{:S(2)}, u32[]{:S(2)}) collective-permute-start(bf16[256,2048]{1,0:T(8,128)(2,1)S(1)} %slice.921), channel_id=1, source_target_pairs={{0,4},{4,0},{8,12},{12,8},{1,5},{5,1},{9,13},{13,9},{2,6},{6,2},{1... | collective-permute-start | bytes 3145736 | tf_op jit(solution)/shard_map/ppermute | solution.py:13
  500.1 14.8 %collective-permute-start.78 = (bf16[3,32,512]{2,1,0:T(8,128)(2,1)S(1)}, bf16[3,32,512]{2,1,0:T(8,128)(2,1)S(1)}, u32[]{:S(2)}, u32[]{:S(2)}) collective-permute-start(bf16[3,32,512]{2,1,0:T(8,128)(2,1)S(1)} %pad_maximum_fusion.28), channel_id=1, source_target_pairs={{0,64},{16,80},{32,96},{48,112},{1,65},{17,81},{33,97},{49,113},{2... | collective-permute-start | bytes 294920 | tf_op jit(solution)/shard_map/ppermute | solution.py:170
  510.7 13.8 %collective-permute-start.27 = (bf16[2,32,2048]{2,1,0:T(8,128)(2,1)S(1)}, bf16[2,32,2048]{2,1,0:T(8,128)(2,1)S(1)}, u32[]{:S(2)}, u32[]{:S(2)}) collective-permute-start(bf16[2,32,2048]{2,1,0:T(8,128)(2,1)S(1)} %pad_maximum_fusion.17), channel_id=1, source_target_pairs={{0,3},{1,0},{2,1},{3,2},{4,7},{5,4},{6,5},{7,6},{8,11},{9,8},{10,9... | collective-permute-start | bytes 786440 | tf_op jit(solution)/shard_map/ppermute | solution.py:21
  513.3 11.3 %collective-permute-start.25 = (bf16[2,32,2048]{2,1,0:T(8,128)(2,1)S(1)}, bf16[2,32,2048]{2,1,0:T(8,128)(2,1)S(1)}, u32[]{:S(2)}, u32[]{:S(2)}) collective-permute-start(bf16[2,32,2048]{2,1,0:T(8,128)(2,1)S(1)} %pad_maximum_fusion.16), channel_id=1, source_target_pairs={{0,1},{1,2},{2,3},{3,0},{4,5},{5,6},{6,7},{7,4},{8,9},{9,10},{10,1... | collective-permute-start | bytes 786440 | tf_op jit(solution)/shard_map/ppermute | solution.py:21
  514.8 10.6 %collective-permute-start.79 = (bf16[3,32,512]{2,1,0:T(8,128)(2,1)S(1)}, bf16[3,32,512]{2,1,0:T(8,128)(2,1)S(1)}, u32[]{:S(2)}, u32[]{:S(2)}) collective-permute-start(bf16[3,32,512]{2,1,0:T(8,128)(2,1)S(1)} %collective-permute-done.78), channel_id=1, source_target_pairs={{64,80},{80,96},{96,112},{112,64},{65,81},{81,97},{97,113},{113,65... | collective-permute-start | bytes 294920 | tf_op jit(solution)/shard_map/ppermute | solution.py:25
  517.7 8.0 %collective-permute-start.80 = (bf16[3,32,512]{2,1,0:T(8,128)(2,1)S(1)}, bf16[3,32,512]{2,1,0:T(8,128)(2,1)S(1)}, u32[]{:S(2)}, u32[]{:S(2)}) collective-permute-start(bf16[3,32,512]{2,1,0:T(8,128)(2,1)S(1)} %collective-permute-done.78), channel_id=1, source_target_pairs={{64,96},{80,112},{96,64},{112,80},{65,97},{81,113},{97,65},{113,81... | collective-permute-start | bytes 294920 | tf_op jit(solution)/shard_map/ppermute | solution.py:25
  520.1 7.1 %collective-permute-start.81 = (bf16[3,32,512]{2,1,0:T(8,128)(2,1)S(1)}, bf16[3,32,512]{2,1,0:T(8,128)(2,1)S(1)}, u32[]{:S(2)}, u32[]{:S(2)}) collective-permute-start(bf16[3,32,512]{2,1,0:T(8,128)(2,1)S(1)} %collective-permute-done.78), channel_id=1, source_target_pairs={{64,112},{80,64},{96,80},{112,96},{65,113},{81,65},{97,81},{113,97... | collective-permute-start | bytes 294920 | tf_op jit(solution)/shard_map/ppermute | solution.py:25
  (93 other events, 1003.5 us)

commit v2 on v1

v2 whole, which is shorter than its diff:
```python
import functools

import jax
import jax.numpy as jnp
from jax import lax
from jax.experimental import pallas as pl
from jax.experimental.pallas import tpu as pltpu
from jax.sharding import PartitionSpec as P

MICRO = 2
EVICT = 3
EPSILON = 1e-05
LOW = jnp.bfloat16
WIDE = jnp.float32

TO_CORE = ("dp", [(d, d ^ 1) for d in range(4)])
TO_Z = ("dp", [(d, d ^ 2) for d in range(4)])
UP_Y = ("tensor", [(t, (t + 1) % 4) for t in range(4)])
DOWN_Y = ("tensor", [(t, (t - 1) % 4) for t in range(4)])
TO_EARLY = ("pipe", [(4 + s, s) for s in range(4)])
TO_LATE = ("pipe", [(s, 4 + s) for s in range(4)])
NEXT = ("pipe", [(s, s + 1) for s in range(7)])
LAST = ("pipe", [(s, s - 1) for s in range(1, 8)])


def round_x(step):
    return ("pipe", [(4 + i, 4 + (i + step) % 4) for i in range(4)])


class Order:
    def __init__(self):
        self.held, self.bulks = None, []

    def send(self, x, route):
        (x,) = self.take(x)
        self.held = x
        return lax.ppermute(x, *route)

    def take(self, *xs):
        if self.held is None:
            return xs
        return lax.optimization_barrier((*xs, self.held))[: len(xs)]

    def send_z(self, x):
        ahead = [(b, i) for b in self.bulks for i in range(b.taken, len(b.landed))]
        return self.send(x, TO_Z), ahead

    def take_z(self, sent):
        x, ahead = sent
        ahead = [(b, i) for b, i in ahead if i >= b.taken]
        values = lax.optimization_barrier((x, self.held, *(b.landed[i] for b, i in ahead)))
        for (b, i), value in zip(ahead, values[2:]):
            b.landed[i], b.taken = value, i + 1
        return values[0]

    def done(self, x):
        (self.held,) = self.take(x)
        return self.held


def call(body, outs, in_smem, *args):
    specs = [pl.BlockSpec(memory_space=pltpu.SMEM)] * in_smem
    specs += [pl.BlockSpec(memory_space=pltpu.VMEM)] * (len(args) - in_smem)
    return pl.pallas_call(
        body,
        out_shape=[jax.ShapeDtypeStruct(*o) for o in outs],
        in_specs=specs,
        out_specs=[pl.BlockSpec(memory_space=pltpu.VMEM)] * len(outs),
        compiler_params=pltpu.CompilerParams(vmem_limit_bytes=32 * 2**20),
    )(*args)


def plan_at(plan_ref, which, tick, row, field):
    return plan_ref[((which * MICRO + tick) * 4 + row) * 4 + field]


def norm_of(values, gain):
    wide = values.astype(WIDE)
    inverse_rms = lax.rsqrt(jnp.mean(wide * wide, axis=-1, keepdims=True) + EPSILON)
    return (wide * inverse_rms * gain).astype(LOW)


def store_split(where_ref, index, values, keep_ref, send_ref):
    half = values.shape[1] // 2
    left, right = values[:, :half], values[:, half:]

    @pl.when(where_ref[1] == 0)
    def _():
        keep_ref[index] = left
        send_ref[index] = right

    @pl.when(where_ref[1] == 1)
    def _():
        keep_ref[index] = right
        send_ref[index] = left


def heads_body(normed, where_ref, gain_ref, *refs):
    *ins, keep_ref, send_ref = refs
    for k, (x, wanted) in enumerate(zip(ins, normed)):
        values = norm_of(x[...], gain_ref[...]) if wanted else x[...]
        store_split(where_ref, k, values, keep_ref, send_ref)


def heads(where, gain, arrays, normed):
    rows, width = arrays[0].shape
    out = ((len(arrays), rows, width // 2), LOW)
    return call(functools.partial(heads_body, normed), [out, out], 1, where, gain, *arrays)


def pick_back_body(where_ref, plan_ref, *refs):
    *around, out = refs
    column = where_ref[0] % 4
    for tick in range(MICRO):
        distance = (plan_at(plan_ref, 0, tick, column, 0) - column + 4) % 4
        for k in range(4):

            @pl.when(distance == k)
            def _(k=k, tick=tick):
                out[tick] = around[k][tick]


def pick_out_body(where_ref, plan_ref, *refs):
    *around, out = refs
    column = where_ref[0] % 4
    out[...] = jnp.zeros_like(out)
    for tick in range(MICRO):
        for k in range(4):
            heading = plan_at(plan_ref, 1, tick, (column + k) % 4, 0) == column

            @pl.when(heading & (where_ref[0] >= 4))
            def _(k=k, tick=tick):
                out[tick] = around[k][tick]


def columns_of(plan_ref, which, tick, row, e, width):
    start = plan_at(plan_ref, which, tick, row, 1 + e) * width
    return pl.ds(pl.multiple_of(start, width), width)


def stash_body(where_ref, plan_ref, gain_ref, own, fetched, old, keep_ref, send_ref):
    width = fetched.shape[-1]
    row = jnp.minimum(where_ref[0], 3)
    for tick in range(MICRO):
        old[tick] = own[tick]

        @pl.when(where_ref[0] < 4)
        def _(tick=tick):
            for e in range(EVICT):
                old[tick, :, columns_of(plan_ref, 0, tick, row, e, width)] = fetched[tick, e]

        store_split(where_ref, tick, norm_of(old[tick], gain_ref[...]), keep_ref, send_ref)


def leave_body(where_ref, plan_ref, first, second, pulled, kept):
    width = pulled.shape[-1]
    row = jnp.minimum(where_ref[0], 3)
    for tick, x in enumerate((first, second)):
        kept[tick] = x[...]
        for e in range(EVICT):
            columns = columns_of(plan_ref, 1, tick, row, e, width)
            pulled[tick, e] = x[:, columns]

            @pl.when(where_ref[0] < 4)
            def _(tick=tick, columns=columns):
                kept[tick, :, columns] = jnp.zeros((kept.shape[1], width), kept.dtype)


def sides(where_ref, keep, got):
    low_z = where_ref[1] == 0
    a, b = keep[...].astype(WIDE), got[...].astype(WIDE)
    return jnp.where(low_z, a, b), jnp.where(low_z, b, a)


def add_body(where_ref, values, keep, got, out):
    half = keep.shape[1]
    left, right = sides(where_ref, keep, got)
    out[:, :half] = (values[:, :half].astype(WIDE) + left).astype(LOW)
    out[:, half:] = (values[:, half:].astype(WIDE) + right).astype(LOW)


def finish_body(where_ref, gain_ref, values, cotangent, keep, got, out, part):
    half = keep.shape[1]
    width = 2 * half
    wide = values[...].astype(WIDE)
    inverse_rms = lax.rsqrt(jnp.mean(wide * wide, axis=-1, keepdims=True) + EPSILON)
    cubed = inverse_rms * inverse_rms * inverse_rms
    pieces = []
    for at, d_normed in zip((0, half), sides(where_ref, keep, got)):
        columns = slice(at, at + half)
        v = values[:, columns].astype(WIDE)
        part[:, columns] = jnp.sum(d_normed * v * inverse_rms, axis=0, keepdims=True)
        scaled = d_normed * gain_ref[:, columns]
        pieces.append((columns, v, scaled, jnp.sum(scaled * v, axis=-1, keepdims=True)))
    mean = (pieces[0][3] + pieces[1][3]) / width
    for columns, v, scaled, _ in pieces:
        g = cotangent[:, columns].astype(WIDE)
        out[:, columns] = (g + inverse_rms * scaled - v * cubed * mean).astype(LOW)


def ordered(at_zero, own, other):
    return jnp.where(at_zero, own, other), jnp.where(at_zero, other, own)


class Gather:
    def __init__(self, order, low_z, keep, send):
        self.order, self.low_z, self.keep, self.outgoing = order, low_z, keep, send

    def z(self):
        self.got = self.order.send_z(self.outgoing)

    def y(self):
        self.got = self.order.take_z(self.got)
        self.mine = jnp.stack(ordered(self.low_z, self.keep, self.got))
        self.before = self.order.send(self.mine, UP_Y)
        self.behind = self.order.send(self.mine, DOWN_Y)

    def far(self):
        self.before, self.behind = self.order.take(self.before, self.behind)
        self.far_low = self.order.send(self.before[0], UP_Y)
        self.far_high = self.order.send(self.behind[1], DOWN_Y)

    def core(self):
        self.far_low, self.far_high = self.order.take(self.far_low, self.far_high)
        self.ring = [
            jnp.stack(
                [
                    self.mine[:, k],
                    self.behind[:, k],
                    jnp.stack([self.far_low[k], self.far_high[k]]),
                    self.before[:, k],
                ]
            )
            for k in range(self.keep.shape[0])
        ]
        self.swapped = [self.order.send(r, TO_CORE) for r in self.ring]

    def rows(self):
        half = self.keep.shape[-1]
        self.swapped = self.order.take(*self.swapped)
        return [
            jnp.concatenate([r, s]).reshape(-1, half) for r, s in zip(self.ring, self.swapped)
        ]


class Settle:
    def __init__(self, order, low_z):
        self.order, self.low_z = order, low_z

    def core(self, part):
        half = part.shape[0] // 2
        self.kept = part[:half]
        self.got = self.order.send(part[half:].astype(LOW), TO_CORE)

    def far(self):
        half, width = self.kept.shape
        (self.got,) = self.order.take(self.got)
        self.summed = (self.kept + self.got.astype(WIDE)).reshape(4, 2, half // 8, width)
        self.low = self.order.send(self.summed[2, 0].astype(LOW), UP_Y)
        self.high = self.order.send(self.summed[2, 1].astype(LOW), DOWN_Y)

    def y(self):
        s = self.summed
        self.low, self.high = self.order.take(self.low, self.high)
        up = jnp.stack([s[1, 0] + self.low.astype(WIDE), s[1, 1]]).astype(LOW)
        down = jnp.stack([s[3, 0], s[3, 1] + self.high.astype(WIDE)]).astype(LOW)
        self.first = self.order.send(up, UP_Y)
        self.second = self.order.send(down, DOWN_Y)

    def z(self):
        self.first, self.second = self.order.take(self.first, self.second)
        mine = self.summed[0] + self.first.astype(WIDE) + self.second.astype(WIDE)
        mine = mine.astype(LOW)
        self.keep = jnp.where(self.low_z, mine[0], mine[1])
        self.got = self.order.send_z(jnp.where(self.low_z, mine[1], mine[0]))

    def end(self):
        self.got = self.order.take_z(self.got)
        return self.keep, self.got


class Bulk:
    def __init__(self, order, part, chunks):
        self.order, self.own = order, part.astype(LOW)
        self.size = part.shape[0] // chunks
        self.landed, self.taken = [], 0
        order.bulks.append(self)

    def z(self):
        at = len(self.landed) * self.size
        self.landed.append(self.order.send(self.own[at : at + self.size], TO_Z))

    def take(self):
        i = self.taken
        (self.landed[i],) = self.order.take(self.landed[i])
        self.taken = i + 1

    def total(self):
        self.landed = list(self.order.take(*self.landed))
        self.taken = len(self.landed)
        got = self.landed[0] if len(self.landed) == 1 else jnp.concatenate(self.landed)
        return self.own.astype(WIDE) + got.astype(WIDE)


def times(a, b):
    return jnp.dot(a, b, preferred_element_type=WIDE)


def times_transposed(a, b):
    return lax.dot_general(a, b, (((1,), (1,)), ((), ())), preferred_element_type=WIDE)


def over_rows(a, b):
    return lax.dot_general(a, b, (((0,), (0,)), ((), ())), preferred_element_type=WIDE)


def activations(hidden_pre, d_hidden):
    gate = jax.nn.sigmoid(hidden_pre)
    hidden = (hidden_pre * gate).astype(LOW)
    return hidden, (d_hidden * gate * (1.0 + hidden_pre * (1.0 - gate))).astype(LOW)


def local(
    act_in, act_first, grad_in, grad_last, stash_local, stash_guest, plan, norm_gain, w_up, w_down
):
    order = Order()
    section, d = lax.axis_index("pipe"), lax.axis_index("dp")
    z, core = d // 2, d % 2
    low_z, low_core = z == 0, core == 0
    where = jnp.stack([section, z]).astype(jnp.int32)
    plan = plan.reshape(-1)
    rows, width = act_in.shape[1:]
    whole = ((rows, width), LOW)
    parcel = (stash_guest.shape[1:], LOW)

    def gather(keep, send):
        return Gather(order, low_z, keep, send)

    def swap_hidden(*owns):
        return [(own, order.send(own, TO_CORE)) for own in owns]

    def whole_hidden(*pairs):
        wholes = []
        for own, got in pairs:
            (got,) = order.take(got)
            half = own.shape[0] // 2
            other = jnp.concatenate([got[half:], got[:half]])
            wholes.append(order.done(jnp.concatenate(ordered(low_core, own, other), axis=1)))
        return wholes

    def my_features(x):
        half = x.shape[1] // 2
        return jnp.where(low_core, x[:, :half], x[:, half:])

    def finished(values, cotangent, settled):
        outs = [whole, ((1, width), WIDE)]
        args = (where, norm_gain, values, cotangent, *settled.end())
        return call(finish_body, outs, 1, *args)

    held = stash_guest[0]
    around = [held] + [order.send(held, round_x(step)) for step in (-1, -2, 1)]
    first = gather(*heads(where, norm_gain, [grad_in[0], act_in[0]], (False, True)))
    first.z()

    w_up, w_down = order.take(w_up, w_down)
    half = w_up.shape[2] // 2
    here, there = core * half, (1 - core) * half
    down_got = order.send(lax.dynamic_slice_in_dim(w_down[0], there, half, 0), TO_CORE)
    (found,) = call(pick_back_body, [parcel], 2, where, plan, *order.take(*around))
    guests = order.send(found, TO_EARLY)
    first.y()
    up_got = order.send(lax.dynamic_slice_in_dim(w_up[0], there, half, 1), TO_CORE)
    (down_got,) = order.take(down_got)
    down_own = lax.dynamic_slice_in_dim(w_down[0], here, half, 0)
    down = order.done(jnp.concatenate(ordered(low_core, down_own, down_got), axis=1))
    first.far()
    (up_got,) = order.take(up_got)
    up_own = lax.dynamic_slice_in_dim(w_up[0], here, half, 1)
    up = order.done(jnp.concatenate(ordered(low_core, up_own, up_got), axis=0))

    pair = ((MICRO, rows, width // 2), LOW)
    old, *split = call(
        stash_body,
        [((MICRO, rows, width), LOW), pair, pair],
        2,
        where,
        plan,
        norm_gain,
        stash_local[0],
        *order.take(guests),
    )
    stash = gather(*split)
    stash.z()
    first.core()
    cot_rows_zero, front_rows_zero = first.rows()
    stash.y()
    d_hidden_zero = Bulk(order, times_transposed(cot_rows_zero, down), 1)
    d_hidden_zero.z()
    stash.far()
    stash.core()
    stash_rows = stash.rows()
    pre_zero = Bulk(order, times(stash_rows[0], up), 1)
    pre_zero.z()
    front_pre_zero = Bulk(order, times(front_rows_zero, up), 2)
    front_pre_zero.z()
    pre_one = Bulk(order, order.done(times(stash_rows[1], up).astype(LOW)), 2)

    hidden_zero, d_pre_zero = activations(pre_zero.total(), d_hidden_zero.total())
    back = Settle(order, low_z)
    back.core(times_transposed(d_pre_zero, up))
    front_pre_zero.z()
    front_pre_zero.take()
    back.far()
    back.y()
    back.z()
    pre_one.z()
    hidden_zero, d_pre_zero = swap_hidden(hidden_zero, d_pre_zero)
    d_input_zero, gain_zero = finished(old[0], grad_in[0], back)
    returned = order.send(d_input_zero, LAST)

    front = Settle(order, low_z)
    front_hidden = jax.nn.silu(front_pre_zero.total()).astype(LOW)
    front.core(times(front_hidden, down))
    cot_one = jnp.where(section == 7, grad_last, order.take(returned)[0])
    second = gather(*heads(where, norm_gain, [cot_one], (False,)))
    second.z()
    pre_one.z()
    front.far()
    second.y()
    front.y()
    second.far()
    front.z()
    second.core()
    (cot_rows_one,) = second.rows()
    d_hidden_one = Bulk(order, times_transposed(cot_rows_one, down), 2)
    d_hidden_one.z()
    (front_zero,) = call(add_body, [whole], 1, where, act_in[0], *front.end())
    passed = order.send(front_zero, NEXT)
    hidden_zero, d_pre_zero = whole_hidden(hidden_zero, d_pre_zero)
    grad_up = order.done(over_rows(my_features(stash_rows[0]), d_pre_zero))
    input_one = jnp.where(section == 0, act_first, order.take(passed)[0])
    third = gather(*heads(where, norm_gain, [input_one], (True,)))
    third.z()
    d_hidden_one.z()
    pulled, kept = call(
        leave_body,
        [parcel, ((MICRO, rows, width), LOW)],
        2,
        where,
        plan,
        act_in[0],
        input_one,
    )
    third.y()
    landed = order.send(pulled, TO_LATE)
    grad_down = order.done(over_rows(hidden_zero, my_features(cot_rows_zero)))
    third.far()
    third.core()
    (front_rows_one,) = third.rows()
    (landed,) = order.take(landed)
    front_pre_one = Bulk(order, order.done(times(front_rows_one, up).astype(LOW)), 1)
    front_pre_one.z()

    hidden_one, d_pre_one = activations(pre_one.total(), d_hidden_one.total())
    back = Settle(order, low_z)
    back.core(times_transposed(d_pre_one, up))
    hidden_one, d_pre_one = swap_hidden(hidden_one, d_pre_one)
    back.far()
    around = [landed] + [order.send(landed, round_x(step)) for step in (-1, -2, 1)]
    back.y()
    hidden_one, d_pre_one = whole_hidden(hidden_one, d_pre_one)
    back.z()
    (guest_new,) = call(pick_out_body, [parcel], 2, where, plan, *order.take(*around))
    more = over_rows(my_features(stash_rows[1]), d_pre_one)
    grad_up = order.done((grad_up + more).astype(LOW))
    more = over_rows(hidden_one, my_features(cot_rows_one))
    grad_down = order.done((grad_down + more).astype(LOW))

    front = Settle(order, low_z)
    front_hidden = jax.nn.silu(front_pre_one.total()).astype(LOW)
    front.core(times(front_hidden, down))
    d_input_one, gain_one = finished(old[1], cot_one, back)
    gain = gain_zero + gain_one
    gain = gain + order.send(gain, TO_CORE)
    front.far()
    gain = gain + order.send(gain, TO_Z)
    front.y()
    gain = gain + order.send(gain, ("tensor", [(t, t ^ 1) for t in range(4)]))
    front.z()
    gain = gain + order.send(gain, ("tensor", [(t, t ^ 2) for t in range(4)]))
    (front_one,) = call(add_body, [whole], 1, where, input_one, *front.end())

    return (
        jnp.stack([front_zero, front_one])[None],
        jnp.stack([d_input_zero, d_input_one])[None],
        kept[None],
        guest_new[None],
        grad_up[None],
        grad_down[None],
        gain,
    )


def solution(mesh):
    placed = (
        P("pipe", ("dp", "tensor"), None),
        P(("dp", "tensor"), None),
        P("pipe", ("dp", "tensor"), None),
        P(("dp", "tensor"), None),
        P("pipe", None, ("dp", "tensor"), None),
        P("pipe", None, None, ("dp", "tensor"), None),
        P(),
        P("pipe", None),
        P("pipe", "dp", "tensor"),
        P("pipe", "tensor", "dp"),
    )
    return jax.shard_map(
        local,
        mesh=mesh,
        in_specs=placed,
        out_specs=(
            P("pipe", None, ("dp", "tensor"), None),
            P("pipe", None, ("dp", "tensor"), None),
            P("pipe", None, ("dp", "tensor"), None),
            P("pipe", None, None, ("dp", "tensor"), None),
            P("pipe", "dp", "tensor"),
            P("pipe", "tensor", "dp"),
            P("pipe", None),
        ),
        check_vma=False,
    )
```

time: 541 us -> 434 us (0.80)
  waiting for transfers between devices: 227 us -> 186 us
  other arithmetic: 59.2 us -> 30.7 us
  starting transfers between devices: 127 us -> 101 us
  between operations: 25.2 us -> 2.67 us
  Pallas kernels: 0 us -> 9.68 us
    ppermute x90 -> x79, waiting for transfers between devices: 227 us -> 186 us  [send(): return lax.ppermute(x, *route)]
    ppermute x90 -> x79, starting transfers between devices: 127 us -> 101 us  [send(): return lax.ppermute(x, *route)]
    pallas_call x0 -> x11, Pallas kernels: none -> 9.68 us  [call(): pl.pallas_call(body, out_shape=[jax.ShapeDtypeStruct(*o) for o in outs],...]
    select_n x16 -> x6, other arithmetic: 10.2 us -> 1.11 us  [the longest x1 0.98 us: local(): cot_one = jnp.where(section == 7, grad_last, order.take(returned)[0])]
    reduce_sum x5 -> x0, other arithmetic: 7.03 us -> none  [the longest x3 3.83 us: normalize(): jnp.mean(wide * wide, axis=-1, keepdims=True) + EPSILON]
    broadcast_in_dim x18 -> x0, local copies, waits for them, and re-layouts: 6.94 us -> none  [place_blocks(): jnp.where(matched[e][None, :, None], fetched[e][:, None, :], blocks)]
    convert_element_type x13 -> x6, other arithmetic: 12.8 us -> 5.92 us  [the longest x1 2.82 us: activations(): (d_hidden * gate * (1.0 + hidden_pre * (1.0 - gate))).astype(LOW)]
    unnamed x176 -> x76, local copies, waits for them, and re-layouts: 7.02 us -> 11 us
  transfers between devices with their start and end apart: 90 -> 79, of which waited for: 40 -> 44; matrix products, arithmetic and copies ran while one was open for 25% -> 22% of each run, Pallas kernels for 0% -> 2%
where the time goes in v2:
time: 434 us; the launch traced here: 425 us
  waiting for transfers between devices  186 us (43%)
  starting transfers between devices  101 us (23%)
  matrix products  65.9 us (15%)
  other arithmetic  30.7 us (7%)
  local copies, waits for them, and re-layouts  28.4 us (7%)
  Pallas kernels  9.68 us (2%)
    ppermute x79, waiting for transfers between devices, send(): return lax.ppermute(x, *route)  186 us
    ppermute x79, starting transfers between devices, send(): return lax.ppermute(x, *route)  101 us
    dot_general x4, matrix products, over_rows(): lax.dot_general(a, b, (((0,), (0,)), ((), ())), preferred_element_type=WIDE)  28.4 us
    dot_general x6, matrix products, times(): return jnp.dot(a, b, preferred_element_type=WIDE)  23.6 us
    dot_general x4, matrix products, times_transposed(): lax.dot_general(a, b, (((1,), (1,)), ((), ())), preferred_element_type=WIDE)  13.8 us
    unnamed x76, local copies, waits for them, and re-layouts  11 us
    pallas_call x11, Pallas kernels, call(): pl.pallas_call(body, out_shape=[jax.ShapeDtypeStruct(*o) for o in outs],...  9.68 us
    select_n x6, other arithmetic, ordered(): return (jnp.where(at_zero, own, other), jnp.where(at_zero, other, own))  9.41 us
  transfers between devices with their start and end apart: 79, of which 44 were waited for; matrix products, arithmetic and copies ran while one was open for 22% of the time, Pallas kernels for 2%

profile of v2, /device:TPU:64, one launch (start us, length us, event | category | flops | bytes accessed | tf_op | source)
XLA Modules:
  0.0 425.0 jit_solution(9322973652833687657)
XLA Ops:
  4.2 3.7 dynamic-slice_bitcast_fusion.1
  7.9 3.4 collective-permute-start.3
  11.3 4.6 %collective-permute-start.2 = (bf16[2,3,32,512]{3,2,1,0:T(8,128)(2,1)S(1)}, bf16[2,3,32,512]{3,2,1,0:T(8,128)(2,1)S(1)}, u32[]{:S(2)}, u32[]{:S(2)}) collective-permute-start(bf16[2,3,32,512]{3,2,1,0:T(8,128)(2,1)S(1)} %bitcast.331), channel_id=1, source_target_pairs={{64,96},{80,112},{96,64},{112,80},{65,97},{81,113},{97,65},{113,81... | collective-permute-start | bytes 589832 | tf_op jit(solution)/shard_map/ppermute | solution.py:37
  15.9 3.3 collective-permute-start.1
  21.1 3.6 dynamic-slice_bitcast_fusion
  30.0 3.0 collective-permute-start.5
  33.9 4.3 %bitcast_select_fusion.3 = (bf16[1408,1024]{1,0:T(8,128)(2,1)S(1)}, bf16[1408,1024]{1,0:T(8,128)(2,1)S(1)}) fusion(bf16[1408,1024]{1,0:T(8,128)(2,1)} %collective-permute-done.6, pred[]{:T(512)S(6)} %eq.15, bf16[1,2816,1024]{2,1,0:T(8,128)(2,1)} %param.19, s32[]{:T(128)S(6)} %select_n.215), kind=kLoop, calls=%fused_computation.17 | loop fusion | flops 2883584 | bytes 11534341 | tf_op jit(solution)/shard_map/jit(_where)/select_n | solution.py:202
  39.0 8.2 %collective-permute-done.4 = bf16[2,2,32,2048]{3,2,0,1:T(8,128)(2,1)S(1)} collective-permute-done((bf16[2,2,32,2048]{3,2,0,1:T(8,128)(2,1)}, bf16[2,2,32,2048]{3,2,0,1:T(8,128)(2,1)S(1)}, u32[]{:S(2)}, u32[]{:S(2)}) %collective-permute-start.4) | collective-permute-done | bytes 524320 | tf_op jit(solution)/shard_map/ppermute | solution.py:37
  48.8 3.2 collective-permute-start.8
  53.6 3.0 bitcast_select_fusion.1
  56.7 3.0 pad_maximum_fusion.1
  69.8 3.5 convolution_convert_fusion.4
  73.3 6.2 %collective-permute-done.15 = bf16[2,2,32,2048]{3,2,1,0:T(8,128)(2,1)S(1)} collective-permute-done((bf16[2,2,32,2048]{3,2,1,0:T(8,128)(2,1)S(1)}, bf16[2,2,32,2048]{3,2,1,0:T(8,128)(2,1)S(1)}, u32[]{:S(2)}, u32[]{:S(2)}) %collective-permute-start.15) | collective-permute-done | bytes 524320 | tf_op jit(solution)/shard_map/ppermute | solution.py:37
  82.1 2.8 collective-permute-start.17
  85.1 3.4 convolution_convert_fusion.5
  90.5 3.3 collective-permute-done.19
  93.8 3.4 convolution_convert_fusion.3
  99.4 3.4 convolution_convert_fusion.2
  102.9 12.8 %collective-permute-done.21 = bf16[512,1408]{1,0:T(8,128)(2,1)S(1)} collective-permute-done((bf16[512,1408]{1,0:T(8,128)(2,1)S(1)}, bf16[512,1408]{1,0:T(8,128)(2,1)S(1)}, u32[]{:S(2)}, u32[]{:S(2)}) %collective-permute-start.21) | collective-permute-done | bytes 1441824 | tf_op jit(solution)/shard_map/ppermute | solution.py:37
  115.7 27.3 %collective-permute-done.22 = bf16[512,1408]{1,0:T(8,128)(2,1)S(1)} collective-permute-done((bf16[512,1408]{1,0:T(8,128)(2,1)S(1)}, bf16[512,1408]{1,0:T(8,128)(2,1)S(1)}, u32[]{:S(2)}, u32[]{:S(2)}) %collective-permute-start.22) | collective-permute-done | bytes 1441824 | tf_op jit(solution)/shard_map/ppermute | solution.py:37
  143.0 2.8 multiply_convert_fusion.4
  145.8 3.4 fusion.69
  149.5 2.6 collective-permute-done.23
  154.8 3.5 collective-permute-done.25
  160.2 2.9 collective-permute-start.27
  170.0 12.3 %collective-permute-done.20 = bf16[256,1408]{1,0:T(8,128)(2,1)S(1)} collective-permute-done((bf16[256,1408]{1,0:T(8,128)(2,1)S(1)}, bf16[256,1408]{1,0:T(8,128)(2,1)S(1)}, u32[]{:S(2)}, u32[]{:S(2)}) %collective-permute-start.20) | collective-permute-done | bytes 720928 | tf_op jit(solution)/shard_map/ppermute | solution.py:37
  182.3 14.3 %collective-permute-done.29 = bf16[256,1408]{1,0:T(8,128)(2,1)S(1)} collective-permute-done((bf16[256,1408]{1,0:T(8,128)(2,1)S(1)}, bf16[256,1408]{1,0:T(8,128)(2,1)S(1)}, u32[]{:S(2)}, u32[]{:S(2)}) %collective-permute-start.29) | collective-permute-done | bytes 720928 | tf_op jit(solution)/shard_map/ppermute | solution.py:37
  201.4 3.5 fusion
  215.0 15.1 %collective-permute-done.34 = bf16[1,32,2048]{2,1,0:T(8,128)(2,1)S(1)} collective-permute-done((bf16[1,32,2048]{2,1,0:T(8,128)(2,1)S(1)}, bf16[1,32,2048]{2,1,0:T(8,128)(2,1)S(1)}, u32[]{:S(2)}, u32[]{:S(2)}) %collective-permute-start.34) | collective-permute-done | bytes 131104 | tf_op jit(solution)/shard_map/ppermute | solution.py:37
  230.1 3.2 collective-permute-start.33
  233.4 2.4 collective-permute-done.33
  235.8 3.7 collective-permute-start.39
  239.6 3.8 collective-permute-done.39
  243.4 6.2 %collective-permute-done.38 = bf16[2,1,32,2048]{3,2,0,1:T(8,128)(2,1)S(1)} collective-permute-done((bf16[2,1,32,2048]{3,2,0,1:T(8,128)(2,1)S(1)}, bf16[2,1,32,2048]{3,2,0,1:T(8,128)(2,1)S(1)}, u32[]{:S(2)}, u32[]{:S(2)}) %collective-permute-start.38) | collective-permute-done | bytes 262176 | tf_op jit(solution)/shard_map/ppermute | solution.py:37
  249.6 7.6 %collective-permute-done.37 = bf16[2,32,2048]{2,1,0:T(8,128)(2,1)S(1)} collective-permute-done((bf16[2,32,2048]{2,1,0:T(8,128)(2,1)S(1)}, bf16[2,32,2048]{2,1,0:T(8,128)(2,1)S(1)}, u32[]{:S(2)}, u32[]{:S(2)}) %collective-permute-start.37) | collective-permute-done | bytes 262176 | tf_op jit(solution)/shard_map/ppermute | solution.py:37
  257.1 3.2 collective-permute-start.42
  260.5 2.4 collective-permute-done.42
  267.8 3.4 convolution_convert_fusion.1
  272.8 4.7 %collective-permute-start.45 = (bf16[32,4096]{1,0:T(8,128)(2,1)S(1)}, bf16[32,4096]{1,0:T(8,128)(2,1)S(1)}, u32[]{:S(2)}, u32[]{:S(2)}) collective-permute-start(bf16[32,4096]{1,0:T(8,128)(2,1)S(1)} %shard_map.158), channel_id=1, source_target_pairs={{0,16},{16,32},{32,48},{48,64},{64,80},{80,96},{96,112},{1,17},{17... | collective-permute-start | bytes 786440 | tf_op jit(solution)/shard_map/ppermute | solution.py:37
  280.6 6.1 %fusion.11 = f32[1024,2816]{1,0:T(8,128)} fusion(bf16[512,2816]{1,0:T(8,128)(2,1)S(1)} %pad_maximum_fusion.3, bf16[512,2048]{1,0:T(8,128)(2,1)S(1)} %bitcast.365, pred[]{:T(512)S(6)} %eq.15), kind=kOutput, calls=%fused_computation.66 | convolution fusion | flops 2953314304 | bytes 16515073 | tf_op jit(solution)/shard_map/dot_general | solution.py:314
  289.0 3.8 collective-permute-done.48
  292.9 3.3 collective-permute-start.51
  296.2 6.0 %fusion.9 = f32[2816,1024]{1,0:T(8,128)} fusion(bf16[512,2816]{1,0:T(8,128)(2,1)S(1)} %pad_maximum_fusion.2, bf16[512,2048]{1,0:T(8,128)(2,1)S(1)} %bitcast.370, pred[]{:T(512)S(6)} %eq.15), kind=kOutput, calls=%fused_computation.63 | convolution fusion | flops 2953314304 | bytes 16515073 | tf_op jit(solution)/shard_map/dot_general | solution.py:314
  304.9 3.3 collective-permute-start.53
  308.2 2.5 collective-permute-done.53
  311.6 2.6 collective-permute-done.54
  314.3 4.5 %convolution_convert_fusion = bf16[512,1408]{1,0:T(8,128)(2,1)} fusion(bf16[512,2048]{1,0:T(8,128)(2,1)S(1)} %bitcast.363, bf16[2048,1408]{1,0:T(8,128)(2,1)S(1)} %bitcast.349), kind=kOutput, calls=%fused_computation.4 | convolution fusion | flops 2953510912 | bytes 9306112 | tf_op jit(solution)/shard_map/dot_general | solution.py:306
  320.2 2.8 multiply_convert_fusion.1
  323.1 3.4 fusion.70
  329.8 3.0 collective-permute-start.60
  332.9 4.6 %collective-permute-done.61.refs_0_ = bf16[2,3,32,512]{3,2,1,0:T(8,128)(2,1)S(1)} collective-permute-done((bf16[2,3,32,512]{3,2,1,0:T(8,128)(2,1)S(1)}, bf16[2,3,32,512]{3,2,1,0:T(8,128)(2,1)S(1)}, u32[]{:S(2)}, u32[]{:S(2)}) %collective-permute-start.61) | collective-permute-done | bytes 196640 | tf_op jit(solution)/shard_map/ppermute | solution.py:37
  339.5 3.5 collective-permute-start.64
  344.8 8.7 %add_convert_fusion = bf16[1024,2816]{1,0:T(8,128)(2,1)} fusion(f32[1024,2816]{1,0:T(8,128)} %fusion.11, bf16[512,2816]{1,0:T(8,128)(2,1)S(1)} %pad_maximum_fusion.5, bf16[512,2048]{1,0:T(8,128)(2,1)} %bitcast.368, pred[]{:T(512)S(6)} %eq.15), kind=kOutput, calls=%fused_computation | convolution fusion | flops 2959081472 | bytes 22282240 | tf_op jit(solution)/shard_map/dot_general | solution.py:314
  353.6 7.6 %add_convert_fusion.1 = bf16[2816,1024]{1,0:T(8,128)(2,1)} fusion(f32[2816,1024]{1,0:T(8,128)} %fusion.9, bf16[512,2816]{1,0:T(8,128)(2,1)S(1)} %pad_maximum_fusion.4, bf16[512,2048]{1,0:T(8,128)(2,1)S(1)} %bitcast.362, pred[]{:T(512)S(6)} %eq.15), kind=kOutput, calls=%fused_computation.1 | convolution fusion | flops 2959081472 | bytes 22282240 | tf_op jit(solution)/shard_map/dot_general | solution.py:314
  361.3 10.5 %collective-permute-done.55 = bf16[512,1408]{1,0:T(8,128)(2,1)} collective-permute-done((bf16[512,1408]{1,0:T(8,128)(2,1)}, bf16[512,1408]{1,0:T(8,128)(2,1)}, u32[]{:S(2)}, u32[]{:S(2)}) %collective-permute-start.55) | collective-permute-done | bytes 1441824 | tf_op jit(solution)/shard_map/ppermute | solution.py:37
  371.7 5.3 %fusion.1 = f32[512,2048]{1,0:T(8,128)S(1)} fusion(bf16[1408,2048]{1,0:T(8,128)(2,1)S(1)} %bitcast.345, bf16[512,1408]{1,0:T(8,128)(2,1)} %collective-permute-done.55, bf16[512,1408]{1,0:T(8,128)(2,1)} %convolution_convert_fusion), kind=kOutput, calls=%fused_computation.39 | convolution fusion | flops 2958557184 | bytes 12845056 | tf_op jit(solution)/shard_map/dot_general | solution.py:306
  378.1 5.1 %collective-permute-done.66.got = bf16[32,2048]{1,0:T(8,128)(2,1)S(1)} collective-permute-done((bf16[32,2048]{1,0:T(8,128)(2,1)S(1)}, bf16[32,2048]{1,0:T(8,128)(2,1)S(1)}, u32[]{:S(2)}, u32[]{:S(2)}) %collective-permute-start.66) | collective-permute-done | bytes 131104 | tf_op jit(solution)/shard_map/ppermute | solution.py:37
  384.8 3.0 collective-permute-start.68
  390.4 3.6 collective-permute-done.67
  397.0 4.7 %collective-permute-start.77 = (bf16[2,3,32,512]{3,2,1,0:T(8,128)(2,1)S(1)}, bf16[2,3,32,512]{3,2,1,0:T(8,128)(2,1)S(1)}, u32[]{:S(2)}, u32[]{:S(2)}) collective-permute-start(bf16[2,3,32,512]{3,2,1,0:T(8,128)(2,1)S(1)} %collective-permute-done.61.refs_0_), channel_id=1, source_target_pairs={{64,80},{80,96},{96,112},{112,64},{65,81},{81,97},{97,113},{113,65... | collective-permute-start | bytes 589832 | tf_op jit(solution)/shard_map/ppermute | solution.py:37
  401.6 4.6 %collective-permute-start.76 = (bf16[2,3,32,512]{3,2,1,0:T(8,128)(2,1)S(1)}, bf16[2,3,32,512]{3,2,1,0:T(8,128)(2,1)S(1)}, u32[]{:S(2)}, u32[]{:S(2)}) collective-permute-start(bf16[2,3,32,512]{3,2,1,0:T(8,128)(2,1)S(1)} %collective-permute-done.61.refs_0_), channel_id=1, source_target_pairs={{64,96},{80,112},{96,64},{112,80},{65,97},{81,113},{97,65},{113,81... | collective-permute-start | bytes 589832 | tf_op jit(solution)/shard_map/ppermute | solution.py:37
  406.3 3.8 collective-permute-start.75
  411.1 2.7 collective-permute-done.75.refs_1_
  418.0 4.4 %collective-permute-done.78 = f32[1,4096]{1,0:T(1,128)S(1)} collective-permute-done((f32[1,4096]{1,0:T(1,128)S(1)}, f32[1,4096]{1,0:T(1,128)S(1)}, u32[]{:S(2)}, u32[]{:S(2)}) %collective-permute-start.78) | collective-permute-done | bytes 16416 | tf_op jit(solution)/shard_map/ppermute | solution.py:37
  (326 shorter events, 98.3 us)
Async XLA Ops:
  7.9 26.1 %collective-permute-start.6 = (bf16[1408,1024]{1,0:T(8,128)(2,1)}, bf16[1408,1024]{1,0:T(8,128)(2,1)}, u32[]{:S(2)}, u32[]{:S(2)}) collective-permute-start(bf16[1408,1024]{1,0:T(8,128)(2,1)} %dynamic-slice_bitcast_fusion.1), channel_id=1, source_target_pairs={{0,4},{4,0},{8,12},{12,8},{1,5},{5,1},{9,13},{13,9},{2,6},{6,2},{1... | collective-permute-start | bytes 8650760 | tf_op jit(solution)/shard_map/ppermute | solution.py:37
  7.9 16.8 %collective-permute-start.3 = (bf16[2,3,32,512]{3,2,1,0:T(8,128)(2,1)S(1)}, bf16[2,3,32,512]{3,2,1,0:T(8,128)(2,1)S(1)}, u32[]{:S(2)}, u32[]{:S(2)}) collective-permute-start(bf16[2,3,32,512]{3,2,1,0:T(8,128)(2,1)S(1)} %bitcast.330), channel_id=1, source_target_pairs={{64,80},{80,96},{96,112},{112,64},{65,81},{81,97},{97,113},{113,65... | collective-permute-start | bytes 589832 | tf_op jit(solution)/shard_map/ppermute | solution.py:37
  11.3 13.4 %collective-permute-start.2 = (bf16[2,3,32,512]{3,2,1,0:T(8,128)(2,1)S(1)}, bf16[2,3,32,512]{3,2,1,0:T(8,128)(2,1)S(1)}, u32[]{:S(2)}, u32[]{:S(2)}) collective-permute-start(bf16[2,3,32,512]{3,2,1,0:T(8,128)(2,1)S(1)} %bitcast.331), channel_id=1, source_target_pairs={{64,96},{80,112},{96,64},{112,80},{65,97},{81,113},{97,65},{113,81... | collective-permute-start | bytes 589832 | tf_op jit(solution)/shard_map/ppermute | solution.py:37
  15.9 9.1 %collective-permute-start.1 = (bf16[2,3,32,512]{3,2,1,0:T(8,128)(2,1)S(1)}, bf16[2,3,32,512]{3,2,1,0:T(8,128)(2,1)S(1)}, u32[]{:S(2)}, u32[]{:S(2)}) collective-permute-start(bf16[2,3,32,512]{3,2,1,0:T(8,128)(2,1)S(1)} %bitcast.332), channel_id=1, source_target_pairs={{64,112},{80,64},{96,80},{112,96},{65,113},{81,65},{97,81},{113,97... | collective-permute-start | bytes 589832 | tf_op jit(solution)/shard_map/ppermute | solution.py:37
  19.3 8.0 %collective-permute-start = (bf16[2,32,2048]{2,1,0:T(8,128)(2,1)S(1)}, bf16[2,32,2048]{2,1,0:T(8,128)(2,1)S(1)}, u32[]{:S(2)}, u32[]{:S(2)}) collective-permute-start(bf16[2,32,2048]{2,1,0:T(8,128)(2,1)S(1)} %get-tuple-element.200), channel_id=1, source_target_pairs={{0,8},{4,12},{8,0},{12,4},{1,9},{5,13},{9,1},{13,5},{2,10},{6,14},... | collective-permute-start | bytes 786440 | tf_op jit(solution)/shard_map/ppermute | solution.py:37
  25.6 34.0 %collective-permute-start.9 = (bf16[2,3,32,512]{3,2,1,0:T(8,128)(2,1)S(1)}, bf16[2,3,32,512]{3,2,1,0:T(8,128)(2,1)S(1)}, u32[]{:S(2)}, u32[]{:S(2)}) collective-permute-start(bf16[2,3,32,512]{3,2,1,0:T(8,128)(2,1)S(1)} %shard_map.154), channel_id=1, source_target_pairs={{64,0},{80,16},{96,32},{112,48},{65,1},{81,17},{97,33},{113,49},{6... | collective-permute-start | bytes 589832 | tf_op jit(solution)/shard_map/ppermute | solution.py:37
  30.0 17.2 %collective-permute-start.5 = (bf16[2,2,32,2048]{3,2,1,0:T(8,128)(2,1)}, bf16[2,2,32,2048]{3,2,1,0:T(8,128)(2,1)S(1)}, u32[]{:S(2)}, u32[]{:S(2)}) collective-permute-start(bf16[2,2,32,2048]{3,2,1,0:T(8,128)(2,1)} %pad_maximum_fusion.17), channel_id=1, source_target_pairs={{0,3},{1,0},{2,1},{3,2},{4,7},{5,4},{6,5},{7,6},{8,11},{9,8},{10,9... | collective-permute-start | bytes 1572872 | tf_op jit(solution)/shard_map/ppermute | solution.py:37
  33.0 14.2 %collective-permute-start.4 = (bf16[2,2,32,2048]{3,2,0,1:T(8,128)(2,1)}, bf16[2,2,32,2048]{3,2,0,1:T(8,128)(2,1)S(1)}, u32[]{:S(2)}, u32[]{:S(2)}) collective-permute-start(bf16[2,2,32,2048]{3,2,0,1:T(8,128)(2,1)} %copy.18), channel_id=1, source_target_pairs={{0,1},{1,2},{2,3},{3,0},{4,5},{5,6},{6,7},{7,4},{8,9},{9,10},{10,1... | collective-permute-start | bytes 1572872 | tf_op jit(solution)/shard_map/ppermute | solution.py:37
  33.0 20.6 %collective-permute-start.10 = (bf16[1024,1408]{1,0:T(8,128)(2,1)}, bf16[1024,1408]{1,0:T(8,128)(2,1)S(1)}, u32[]{:S(2)}, u32[]{:S(2)}) collective-permute-start(bf16[1024,1408]{1,0:T(8,128)(2,1)} %dynamic-slice_bitcast_fusion), channel_id=1, source_target_pairs={{0,4},{4,0},{8,12},{12,8},{1,5},{5,1},{9,13},{13,9},{2,6},{6,2},{1... | collective-permute-start | bytes 8650760 | tf_op jit(solution)/shard_map/ppermute | solution.py:37
  47.9 14.4 %collective-permute-start.7 = (bf16[2,32,2048]{2,1,0:T(8,128)(2,1)}, bf16[2,32,2048]{2,1,0:T(8,128)(2,1)}, u32[]{:S(2)}, u32[]{:S(2)}) collective-permute-start(bf16[2,32,2048]{2,1,0:T(8,128)(2,1)} %slice_bitcast_fusion.10), channel_id=1, source_target_pairs={{0,1},{1,2},{2,3},{3,0},{4,5},{5,6},{6,7},{7,4},{8,9},{9,10},{10,1... | collective-permute-start | bytes 786440 | tf_op jit(solution)/shard_map/ppermute | solution.py:37
  48.8 13.6 %collective-permute-start.8 = (bf16[2,32,2048]{2,1,0:T(8,128)(2,1)}, bf16[2,32,2048]{2,1,0:T(8,128)(2,1)}, u32[]{:S(2)}, u32[]{:S(2)}) collective-permute-start(bf16[2,32,2048]{2,1,0:T(8,128)(2,1)} %get-tuple-element.218), channel_id=1, source_target_pairs={{0,3},{1,0},{2,1},{3,2},{4,7},{5,4},{6,5},{7,6},{8,11},{9,8},{10,9... | collective-permute-start | bytes 786440 | tf_op jit(solution)/shard_map/ppermute | solution.py:37
  60.6 6.5 %collective-permute-start.13 = (bf16[2,32,2048]{2,1,0:T(8,128)(2,1)S(1)}, bf16[2,32,2048]{2,1,0:T(8,128)(2,1)S(1)}, u32[]{:S(2)}, u32[]{:S(2)}) collective-permute-start(bf16[2,32,2048]{2,1,0:T(8,128)(2,1)S(1)} %get-tuple-element.223), channel_id=1, source_target_pairs={{0,8},{4,12},{8,0},{12,4},{1,9},{5,13},{9,1},{13,5},{2,10},{6,14},... | collective-permute-start | bytes 786440 | tf_op jit(solution)/shard_map/ppermute | solution.py:37
  67.2 12.3 %collective-permute-start.15 = (bf16[2,2,32,2048]{3,2,1,0:T(8,128)(2,1)S(1)}, bf16[2,2,32,2048]{3,2,1,0:T(8,128)(2,1)S(1)}, u32[]{:S(2)}, u32[]{:S(2)}) collective-permute-start(bf16[2,2,32,2048]{3,2,1,0:T(8,128)(2,1)S(1)} %pad_maximum_fusion.18), channel_id=1, source_target_pairs={{0,3},{1,0},{2,1},{3,2},{4,7},{5,4},{6,5},{7,6},{8,11},{9,8},{10,9... | collective-permute-start | bytes 1572872 | tf_op jit(solution)/shard_map/ppermute | solution.py:37
  67.3 13.7 %collective-permute-start.14 = (bf16[2,2,32,2048]{3,2,0,1:T(8,128)(2,1)S(1)}, bf16[2,2,32,2048]{3,2,0,1:T(8,128)(2,1)S(1)}, u32[]{:S(2)}, u32[]{:S(2)}) collective-permute-start(bf16[2,2,32,2048]{3,2,0,1:T(8,128)(2,1)S(1)} %copy.23), channel_id=1, source_target_pairs={{0,1},{1,2},{2,3},{3,0},{4,5},{5,6},{6,7},{7,4},{8,9},{9,10},{10,1... | collective-permute-start | bytes 1572872 | tf_op jit(solution)/shard_map/ppermute | solution.py:37
  81.1 34.6 %collective-permute-start.21 = (bf16[512,1408]{1,0:T(8,128)(2,1)S(1)}, bf16[512,1408]{1,0:T(8,128)(2,1)S(1)}, u32[]{:S(2)}, u32[]{:S(2)}) collective-permute-start(bf16[512,1408]{1,0:T(8,128)(2,1)S(1)} %convolution_convert_fusion.4), channel_id=1, source_target_pairs={{0,8},{4,12},{8,0},{12,4},{1,9},{5,13},{9,1},{13,5},{2,10},{6,14},... | collective-permute-start | bytes 4325384 | tf_op jit(solution)/shard_map/ppermute | solution.py:37
  81.6 7.7 %collective-permute-start.16 = (bf16[2,32,2048]{2,1,0:T(8,128)(2,1)S(1)}, bf16[2,32,2048]{2,1,0:T(8,128)(2,1)S(1)}, u32[]{:S(2)}, u32[]{:S(2)}) collective-permute-start(bf16[2,32,2048]{2,1,0:T(8,128)(2,1)S(1)} %slice_bitcast_fusion.8), channel_id=1, source_target_pairs={{0,1},{1,2},{2,3},{3,0},{4,5},{5,6},{6,7},{7,4},{8,9},{9,10},{10,1... | collective-permute-start | bytes 786440 | tf_op jit(solution)/shard_map/ppermute | solution.py:37
  82.1 6.7 %collective-permute-start.17 = (bf16[2,32,2048]{2,1,0:T(8,128)(2,1)S(1)}, bf16[2,32,2048]{2,1,0:T(8,128)(2,1)S(1)}, u32[]{:S(2)}, u32[]{:S(2)}) collective-permute-start(bf16[2,32,2048]{2,1,0:T(8,128)(2,1)S(1)} %get-tuple-element.238), channel_id=1, source_target_pairs={{0,3},{1,0},{2,1},{3,2},{4,7},{5,4},{6,5},{7,6},{8,11},{9,8},{10,9... | collective-permute-start | bytes 786440 | tf_op jit(solution)/shard_map/ppermute | solution.py:37
  97.3 45.7 %collective-permute-start.22 = (bf16[512,1408]{1,0:T(8,128)(2,1)S(1)}, bf16[512,1408]{1,0:T(8,128)(2,1)S(1)}, u32[]{:S(2)}, u32[]{:S(2)}) collective-permute-start(bf16[512,1408]{1,0:T(8,128)(2,1)S(1)} %convolution_convert_fusion.3), channel_id=1, source_target_pairs={{0,8},{4,12},{8,0},{12,4},{1,9},{5,13},{9,1},{13,5},{2,10},{6,14},... | collective-permute-start | bytes 4325384 | tf_op jit(solution)/shard_map/ppermute | solution.py:37
  153.1 6.5 %collective-permute-start.24 = (bf16[32,2048]{1,0:T(8,128)(2,1)S(1)}, bf16[32,2048]{1,0:T(8,128)(2,1)S(1)}, u32[]{:S(2)}, u32[]{:S(2)}) collective-permute-start(bf16[32,2048]{1,0:T(8,128)(2,1)S(1)} %get-tuple-element.254), channel_id=1, source_target_pairs={{0,1},{1,2},{2,3},{3,0},{4,5},{5,6},{6,7},{7,4},{8,9},{9,10},{10,1... | collective-permute-start | bytes 393224 | tf_op jit(solution)/shard_map/ppermute | solution.py:37
  159.7 8.5 %collective-permute-start.26 = (bf16[2,32,2048]{2,1,0:T(8,128)(2,1)S(1)}, bf16[2,32,2048]{2,1,0:T(8,128)(2,1)S(1)}, u32[]{:S(2)}, u32[]{:S(2)}) collective-permute-start(bf16[2,32,2048]{2,1,0:T(8,128)(2,1)S(1)} %pad_maximum_fusion.19), channel_id=1, source_target_pairs={{0,1},{1,2},{2,3},{3,0},{4,5},{5,6},{6,7},{7,4},{8,9},{9,10},{10,1... | collective-permute-start | bytes 786440 | tf_op jit(solution)/shard_map/ppermute | solution.py:37
  160.2 7.3 %collective-permute-start.27 = (bf16[2,32,2048]{2,1,0:T(8,128)(2,1)S(1)}, bf16[2,32,2048]{2,1,0:T(8,128)(2,1)S(1)}, u32[]{:S(2)}, u32[]{:S(2)}) collective-permute-start(bf16[2,32,2048]{2,1,0:T(8,128)(2,1)S(1)} %pad_maximum_fusion.20), channel_id=1, source_target_pairs={{0,3},{1,0},{2,1},{3,2},{4,7},{5,4},{6,5},{7,6},{8,11},{9,8},{10,9... | collective-permute-start | bytes 786440 | tf_op jit(solution)/shard_map/ppermute | solution.py:37
  163.1 19.2 %collective-permute-start.20 = (bf16[256,1408]{1,0:T(8,128)(2,1)S(1)}, bf16[256,1408]{1,0:T(8,128)(2,1)S(1)}, u32[]{:S(2)}, u32[]{:S(2)}) collective-permute-start(bf16[256,1408]{1,0:T(8,128)(2,1)S(1)} %get-tuple-element.245), channel_id=1, source_target_pairs={{0,8},{4,12},{8,0},{12,4},{1,9},{5,13},{9,1},{13,5},{2,10},{6,14},... | collective-permute-start | bytes 2162696 | tf_op jit(solution)/shard_map/ppermute | solution.py:37
  163.5 33.1 %collective-permute-start.29 = (bf16[256,1408]{1,0:T(8,128)(2,1)S(1)}, bf16[256,1408]{1,0:T(8,128)(2,1)S(1)}, u32[]{:S(2)}, u32[]{:S(2)}) collective-permute-start(bf16[256,1408]{1,0:T(8,128)(2,1)S(1)} %get-tuple-element.251), channel_id=1, source_target_pairs={{0,8},{4,12},{8,0},{12,4},{1,9},{5,13},{9,1},{13,5},{2,10},{6,14},... | collective-permute-start | bytes 2162696 | tf_op jit(solution)/shard_map/ppermute | solution.py:37
  168.4 29.6 %collective-permute-start.28 = (bf16[32,2048]{1,0:T(8,128)(2,1)S(1)}, bf16[32,2048]{1,0:T(8,128)(2,1)S(1)}, u32[]{:S(2)}, u32[]{:S(2)}) collective-permute-start(bf16[32,2048]{1,0:T(8,128)(2,1)S(1)} %get-tuple-element.262), channel_id=1, source_target_pairs={{0,8},{4,12},{8,0},{12,4},{1,9},{5,13},{9,1},{13,5},{2,10},{6,14},... | collective-permute-start | bytes 393224 | tf_op jit(solution)/shard_map/ppermute | solution.py:37
  199.0 9.9 %collective-permute-start.31 = (bf16[32,4096]{1,0:T(8,128)(2,1)S(1)}, bf16[32,4096]{1,0:T(8,128)(2,1)}, u32[]{:S(2)}, u32[]{:S(2)}) collective-permute-start(bf16[32,4096]{1,0:T(8,128)(2,1)S(1)} %get-tuple-element.270), channel_id=1, source_target_pairs={{16,0},{32,16},{48,32},{64,48},{80,64},{96,80},{112,96},{17,1},{33... | collective-permute-start | bytes 786440 | tf_op jit(solution)/shard_map/ppermute | solution.py:37
  208.1 22.0 %collective-permute-start.35 = (bf16[256,1408]{1,0:T(8,128)(2,1)}, bf16[256,1408]{1,0:T(8,128)(2,1)S(1)}, u32[]{:S(2)}, u32[]{:S(2)}) collective-permute-start(bf16[256,1408]{1,0:T(8,128)(2,1)} %get-tuple-element.263), channel_id=1, source_target_pairs={{0,8},{4,12},{8,0},{12,4},{1,9},{5,13},{9,1},{13,5},{2,10},{6,14},... | collective-permute-start | bytes 2162696 | tf_op jit(solution)/shard_map/ppermute | solution.py:37
  208.4 69.1 %collective-permute-start.47 = (bf16[512,1408]{1,0:T(8,128)(2,1)}, bf16[512,1408]{1,0:T(8,128)(2,1)S(1)}, u32[]{:S(2)}, u32[]{:S(2)}) collective-permute-start(bf16[512,1408]{1,0:T(8,128)(2,1)} %get-tuple-element.264), channel_id=1, source_target_pairs={{0,4},{4,0},{8,12},{12,8},{1,5},{5,1},{9,13},{13,9},{2,6},{6,2},{1... | collective-permute-start | bytes 4325384 | tf_op jit(solution)/shard_map/ppermute | solution.py:37
  208.6 69.7 %collective-permute-start.46 = (bf16[512,1408]{1,0:T(8,128)(2,1)S(1)}, bf16[512,1408]{1,0:T(8,128)(2,1)S(1)}, u32[]{:S(2)}, u32[]{:S(2)}) collective-permute-start(bf16[512,1408]{1,0:T(8,128)(2,1)S(1)} %get-tuple-element.265), channel_id=1, source_target_pairs={{0,4},{4,0},{8,12},{12,8},{1,5},{5,1},{9,13},{13,9},{2,6},{6,2},{1... | collective-permute-start | bytes 4325384 | tf_op jit(solution)/shard_map/ppermute | solution.py:37
  210.5 19.6 %collective-permute-start.34 = (bf16[1,32,2048]{2,1,0:T(8,128)(2,1)S(1)}, bf16[1,32,2048]{2,1,0:T(8,128)(2,1)S(1)}, u32[]{:S(2)}, u32[]{:S(2)}) collective-permute-start(bf16[1,32,2048]{2,1,0:T(8,128)(2,1)S(1)} %get-tuple-element.276), channel_id=1, source_target_pairs={{0,8},{4,12},{8,0},{12,4},{1,9},{5,13},{9,1},{13,5},{2,10},{6,14},... | collective-permute-start | bytes 393224 | tf_op jit(solution)/shard_map/ppermute | solution.py:37
  212.3 59.6 %collective-permute-start.44 = (bf16[256,1408]{1,0:T(8,128)(2,1)}, bf16[256,1408]{1,0:T(8,128)(2,1)S(1)}, u32[]{:S(2)}, u32[]{:S(2)}) collective-permute-start(bf16[256,1408]{1,0:T(8,128)(2,1)} %get-tuple-element.277), channel_id=1, source_target_pairs={{0,8},{4,12},{8,0},{12,4},{1,9},{5,13},{9,1},{13,5},{2,10},{6,14},... | collective-permute-start | bytes 2162696 | tf_op jit(solution)/shard_map/ppermute | solution.py:37
  230.1 9.4 %collective-permute-start.32 = (bf16[32,2048]{1,0:T(8,128)(2,1)S(1)}, bf16[32,2048]{1,0:T(8,128)(2,1)S(1)}, u32[]{:S(2)}, u32[]{:S(2)}) collective-permute-start(bf16[32,2048]{1,0:T(8,128)(2,1)S(1)} %get-tuple-element.279), channel_id=1, source_target_pairs={{0,1},{1,2},{2,3},{3,0},{4,5},{5,6},{6,7},{7,4},{8,9},{9,10},{10,1... | collective-permute-start | bytes 393224 | tf_op jit(solution)/shard_map/ppermute | solution.py:37
  230.1 5.8 %collective-permute-start.33 = (bf16[32,2048]{1,0:T(8,128)(2,1)S(1)}, bf16[32,2048]{1,0:T(8,128)(2,1)S(1)}, u32[]{:S(2)}, u32[]{:S(2)}) collective-permute-start(bf16[32,2048]{1,0:T(8,128)(2,1)S(1)} %get-tuple-element.280), channel_id=1, source_target_pairs={{0,3},{1,0},{2,1},{3,2},{4,7},{5,4},{6,5},{7,6},{8,11},{9,8},{10,9... | collective-permute-start | bytes 393224 | tf_op jit(solution)/shard_map/ppermute | solution.py:37
  235.8 7.5 %collective-permute-start.39 = (bf16[2,1,32,2048]{3,2,1,0:T(8,128)(2,1)S(1)}, bf16[2,1,32,2048]{3,2,1,0:T(8,128)(2,1)S(1)}, u32[]{:S(2)}, u32[]{:S(2)}) collective-permute-start(bf16[2,1,32,2048]{3,2,1,0:T(8,128)(2,1)S(1)} %get-tuple-element.284), channel_id=1, source_target_pairs={{0,3},{1,0},{2,1},{3,2},{4,7},{5,4},{6,5},{7,6},{8,11},{9,8},{10,9... | collective-permute-start | bytes 786440 | tf_op jit(solution)/shard_map/ppermute | solution.py:37
  239.5 10.1 %collective-permute-start.38 = (bf16[2,1,32,2048]{3,2,0,1:T(8,128)(2,1)S(1)}, bf16[2,1,32,2048]{3,2,0,1:T(8,128)(2,1)S(1)}, u32[]{:S(2)}, u32[]{:S(2)}) collective-permute-start(bf16[2,1,32,2048]{3,2,0,1:T(8,128)(2,1)S(1)} %bitcast.358), channel_id=1, source_target_pairs={{0,1},{1,2},{2,3},{3,0},{4,5},{5,6},{6,7},{7,4},{8,9},{9,10},{10,1... | collective-permute-start | bytes 786440 | tf_op jit(solution)/shard_map/ppermute | solution.py:37
  243.4 13.8 %collective-permute-start.36 = (bf16[2,32,2048]{2,1,0:T(8,128)(2,1)S(1)}, bf16[2,32,2048]{2,1,0:T(8,128)(2,1)S(1)}, u32[]{:S(2)}, u32[]{:S(2)}) collective-permute-start(bf16[2,32,2048]{2,1,0:T(8,128)(2,1)S(1)} %pad_maximum_fusion.22), channel_id=1, source_target_pairs={{0,1},{1,2},{2,3},{3,0},{4,5},{5,6},{6,7},{7,4},{8,9},{9,10},{10,1... | collective-permute-start | bytes 786440 | tf_op jit(solution)/shard_map/ppermute | solution.py:37
  249.5 7.6 %collective-permute-start.37 = (bf16[2,32,2048]{2,1,0:T(8,128)(2,1)S(1)}, bf16[2,32,2048]{2,1,0:T(8,128)(2,1)S(1)}, u32[]{:S(2)}, u32[]{:S(2)}) collective-permute-start(bf16[2,32,2048]{2,1,0:T(8,128)(2,1)S(1)} %pad_maximum_fusion.23), channel_id=1, source_target_pairs={{0,3},{1,0},{2,1},{3,2},{4,7},{5,4},{6,5},{7,6},{8,11},{9,8},{10,9... | collective-permute-start | bytes 786440 | tf_op jit(solution)/shard_map/ppermute | solution.py:37
  257.1 6.2 %collective-permute-start.41 = (bf16[1,32,2048]{2,1,0:T(8,128)(2,1)S(1)}, bf16[1,32,2048]{2,1,0:T(8,128)(2,1)S(1)}, u32[]{:S(2)}, u32[]{:S(2)}) collective-permute-start(bf16[1,32,2048]{2,1,0:T(8,128)(2,1)S(1)} %slice_bitcast_fusion.40), channel_id=1, source_target_pairs={{0,1},{1,2},{2,3},{3,0},{4,5},{5,6},{6,7},{7,4},{8,9},{9,10},{10,1... | collective-permute-start | bytes 393224 | tf_op jit(solution)/shard_map/ppermute | solution.py:37
  257.1 5.8 %collective-permute-start.42 = (bf16[1,32,2048]{2,1,0:T(8,128)(2,1)S(1)}, bf16[1,32,2048]{2,1,0:T(8,128)(2,1)S(1)}, u32[]{:S(2)}, u32[]{:S(2)}) collective-permute-start(bf16[1,32,2048]{2,1,0:T(8,128)(2,1)S(1)} %slice_bitcast_fusion.41), channel_id=1, source_target_pairs={{0,3},{1,0},{2,1},{3,2},{4,7},{5,4},{6,5},{7,6},{8,11},{9,8},{10,9... | collective-permute-start | bytes 393224 | tf_op jit(solution)/shard_map/ppermute | solution.py:37
  263.6 8.3 %collective-permute-start.40 = (bf16[32,2048]{1,0:T(8,128)(2,1)S(1)}, bf16[32,2048]{1,0:T(8,128)(2,1)S(1)}, u32[]{:S(2)}, u32[]{:S(2)}) collective-permute-start(bf16[32,2048]{1,0:T(8,128)(2,1)S(1)} %get-tuple-element.295), channel_id=1, source_target_pairs={{0,8},{4,12},{8,0},{12,4},{1,9},{5,13},{9,1},{13,5},{2,10},{6,14},... | collective-permute-start | bytes 393224 | tf_op jit(solution)/shard_map/ppermute | solution.py:37
  271.3 21.4 %collective-permute-start.49 = (bf16[256,1408]{1,0:T(8,128)(2,1)S(1)}, bf16[256,1408]{1,0:T(8,128)(2,1)S(1)}, u32[]{:S(2)}, u32[]{:S(2)}) collective-permute-start(bf16[256,1408]{1,0:T(8,128)(2,1)S(1)} %get-tuple-element.300), channel_id=1, source_target_pairs={{0,8},{4,12},{8,0},{12,4},{1,9},{5,13},{9,1},{13,5},{2,10},{6,14},... | collective-permute-start | bytes 2162696 | tf_op jit(solution)/shard_map/ppermute | solution.py:37
  272.8 14.0 %collective-permute-start.45 = (bf16[32,4096]{1,0:T(8,128)(2,1)S(1)}, bf16[32,4096]{1,0:T(8,128)(2,1)S(1)}, u32[]{:S(2)}, u32[]{:S(2)}) collective-permute-start(bf16[32,4096]{1,0:T(8,128)(2,1)S(1)} %shard_map.158), channel_id=1, source_target_pairs={{0,16},{16,32},{32,48},{48,64},{64,80},{80,96},{96,112},{1,17},{17... | collective-permute-start | bytes 786440 | tf_op jit(solution)/shard_map/ppermute | solution.py:37
  292.9 11.9 %collective-permute-start.51 = (bf16[2,1,32,2048]{3,2,1,0:T(8,128)(2,1)S(1)}, bf16[2,1,32,2048]{3,2,1,0:T(8,128)(2,1)S(1)}, u32[]{:S(2)}, u32[]{:S(2)}) collective-permute-start(bf16[2,1,32,2048]{3,2,1,0:T(8,128)(2,1)S(1)} %get-tuple-element.315), channel_id=1, source_target_pairs={{0,3},{1,0},{2,1},{3,2},{4,7},{5,4},{6,5},{7,6},{8,11},{9,8},{10,9... | collective-permute-start | bytes 786440 | tf_op jit(solution)/shard_map/ppermute | solution.py:37
  296.2 8.6 %collective-permute-start.50 = (bf16[2,1,32,2048]{3,2,0,1:T(8,128)(2,1)S(1)}, bf16[2,1,32,2048]{3,2,0,1:T(8,128)(2,1)S(1)}, u32[]{:S(2)}, u32[]{:S(2)}) collective-permute-start(bf16[2,1,32,2048]{3,2,0,1:T(8,128)(2,1)S(1)} %bitcast.359), channel_id=1, source_target_pairs={{0,1},{1,2},{2,3},{3,0},{4,5},{5,6},{6,7},{7,4},{8,9},{9,10},{10,1... | collective-permute-start | bytes 786440 | tf_op jit(solution)/shard_map/ppermute | solution.py:37
  303.6 16.6 %collective-permute-start.56 = (bf16[256,1408]{1,0:T(8,128)(2,1)S(1)}, bf16[256,1408]{1,0:T(8,128)(2,1)S(1)}, u32[]{:S(2)}, u32[]{:S(2)}) collective-permute-start(bf16[256,1408]{1,0:T(8,128)(2,1)S(1)} %get-tuple-element.312), channel_id=1, source_target_pairs={{0,8},{4,12},{8,0},{12,4},{1,9},{5,13},{9,1},{13,5},{2,10},{6,14},... | collective-permute-start | bytes 2162696 | tf_op jit(solution)/shard_map/ppermute | solution.py:37
  304.8 6.2 %collective-permute-start.52 = (bf16[1,32,2048]{2,1,0:T(8,128)(2,1)S(1)}, bf16[1,32,2048]{2,1,0:T(8,128)(2,1)S(1)}, u32[]{:S(2)}, u32[]{:S(2)}) collective-permute-start(bf16[1,32,2048]{2,1,0:T(8,128)(2,1)S(1)} %slice_bitcast_fusion.39), channel_id=1, source_target_pairs={{0,1},{1,2},{2,3},{3,0},{4,5},{5,6},{6,7},{7,4},{8,9},{9,10},{10,1... | collective-permute-start | bytes 393224 | tf_op jit(solution)/shard_map/ppermute | solution.py:37
  304.9 5.8 %collective-permute-start.53 = (bf16[1,32,2048]{2,1,0:T(8,128)(2,1)S(1)}, bf16[1,32,2048]{2,1,0:T(8,128)(2,1)S(1)}, u32[]{:S(2)}, u32[]{:S(2)}) collective-permute-start(bf16[1,32,2048]{2,1,0:T(8,128)(2,1)S(1)} %slice_bitcast_fusion.38), channel_id=1, source_target_pairs={{0,3},{1,0},{2,1},{3,2},{4,7},{5,4},{6,5},{7,6},{8,11},{9,8},{10,9... | collective-permute-start | bytes 393224 | tf_op jit(solution)/shard_map/ppermute | solution.py:37
  326.7 10.7 %collective-permute-start.61 = (bf16[2,3,32,512]{3,2,1,0:T(8,128)(2,1)S(1)}, bf16[2,3,32,512]{3,2,1,0:T(8,128)(2,1)S(1)}, u32[]{:S(2)}, u32[]{:S(2)}) collective-permute-start(bf16[2,3,32,512]{3,2,1,0:T(8,128)(2,1)S(1)} %get-tuple-element.317), channel_id=1, source_target_pairs={{0,64},{16,80},{32,96},{48,112},{1,65},{17,81},{33,97},{49,113},{2... | collective-permute-start | bytes 589832 | tf_op jit(solution)/shard_map/ppermute | solution.py:37
  328.0 15.0 %collective-permute-start.57 = (bf16[512,1408]{1,0:T(8,128)(2,1)S(1)}, bf16[512,1408]{1,0:T(8,128)(2,1)S(1)}, u32[]{:S(2)}, u32[]{:S(2)}) collective-permute-start(bf16[512,1408]{1,0:T(8,128)(2,1)S(1)} %get-tuple-element.337), channel_id=1, source_target_pairs={{0,4},{4,0},{8,12},{12,8},{1,5},{5,1},{9,13},{13,9},{2,6},{6,2},{1... | collective-permute-start | bytes 4325384 | tf_op jit(solution)/shard_map/ppermute | solution.py:37
  329.8 8.4 %collective-permute-start.60 = (bf16[32,2048]{1,0:T(8,128)(2,1)S(1)}, bf16[32,2048]{1,0:T(8,128)(2,1)S(1)}, u32[]{:S(2)}, u32[]{:S(2)}) collective-permute-start(bf16[32,2048]{1,0:T(8,128)(2,1)S(1)} %get-tuple-element.341), channel_id=1, source_target_pairs={{0,3},{1,0},{2,1},{3,2},{4,7},{5,4},{6,5},{7,6},{8,11},{9,8},{10,9... | collective-permute-start | bytes 393224 | tf_op jit(solution)/shard_map/ppermute | solution.py:37
  332.9 6.5 %collective-permute-start.59 = (bf16[32,2048]{1,0:T(8,128)(2,1)S(1)}, bf16[32,2048]{1,0:T(8,128)(2,1)S(1)}, u32[]{:S(2)}, u32[]{:S(2)}) collective-permute-start(bf16[32,2048]{1,0:T(8,128)(2,1)S(1)} %get-tuple-element.340), channel_id=1, source_target_pairs={{0,1},{1,2},{2,3},{3,0},{4,5},{5,6},{6,7},{7,4},{8,9},{9,10},{10,1... | collective-permute-start | bytes 393224 | tf_op jit(solution)/shard_map/ppermute | solution.py:37
  337.4 6.5 %collective-permute-start.62 = (bf16[512,1408]{1,0:T(8,128)(2,1)S(1)}, bf16[512,1408]{1,0:T(8,128)(2,1)S(1)}, u32[]{:S(2)}, u32[]{:S(2)}) collective-permute-start(bf16[512,1408]{1,0:T(8,128)(2,1)S(1)} %get-tuple-element.401), channel_id=1, source_target_pairs={{0,4},{4,0},{8,12},{12,8},{1,5},{5,1},{9,13},{13,9},{2,6},{6,2},{1... | collective-permute-start | bytes 4325384 | tf_op jit(solution)/shard_map/ppermute | solution.py:37
  337.4 34.3 %collective-permute-start.55 = (bf16[512,1408]{1,0:T(8,128)(2,1)}, bf16[512,1408]{1,0:T(8,128)(2,1)}, u32[]{:S(2)}, u32[]{:S(2)}) collective-permute-start(bf16[512,1408]{1,0:T(8,128)(2,1)} %convolution_convert_fusion), channel_id=1, source_target_pairs={{0,8},{4,12},{8,0},{12,4},{1,9},{5,13},{9,1},{13,5},{2,10},{6,14},... | collective-permute-start | bytes 4325384 | tf_op jit(solution)/shard_map/ppermute | solution.py:37
  339.4 14.1 %collective-permute-start.63 = (bf16[2,32,2048]{2,1,0:T(8,128)(2,1)S(1)}, bf16[2,32,2048]{2,1,0:T(8,128)(2,1)S(1)}, u32[]{:S(2)}, u32[]{:S(2)}) collective-permute-start(bf16[2,32,2048]{2,1,0:T(8,128)(2,1)S(1)} %pad_maximum_fusion.26), channel_id=1, source_target_pairs={{0,1},{1,2},{2,3},{3,0},{4,5},{5,6},{6,7},{7,4},{8,9},{9,10},{10,1... | collective-permute-start | bytes 786440 | tf_op jit(solution)/shard_map/ppermute | solution.py:37
  339.5 14.0 %collective-permute-start.64 = (bf16[2,32,2048]{2,1,0:T(8,128)(2,1)S(1)}, bf16[2,32,2048]{2,1,0:T(8,128)(2,1)S(1)}, u32[]{:S(2)}, u32[]{:S(2)}) collective-permute-start(bf16[2,32,2048]{2,1,0:T(8,128)(2,1)S(1)} %pad_maximum_fusion.25), channel_id=1, source_target_pairs={{0,3},{1,0},{2,1},{3,2},{4,7},{5,4},{6,5},{7,6},{8,11},{9,8},{10,9... | collective-permute-start | bytes 786440 | tf_op jit(solution)/shard_map/ppermute | solution.py:37
  377.2 7.0 %collective-permute-start.65 = (bf16[256,2048]{1,0:T(8,128)(2,1)S(1)}, bf16[256,2048]{1,0:T(8,128)(2,1)S(1)}, u32[]{:S(2)}, u32[]{:S(2)}) collective-permute-start(bf16[256,2048]{1,0:T(8,128)(2,1)S(1)} %slice.670), channel_id=1, source_target_pairs={{0,4},{4,0},{8,12},{12,8},{1,5},{5,1},{9,13},{13,9},{2,6},{6,2},{1... | collective-permute-start | bytes 3145736 | tf_op jit(solution)/shard_map/ppermute | solution.py:37
  377.3 5.9 %collective-permute-start.66 = (bf16[32,2048]{1,0:T(8,128)(2,1)S(1)}, bf16[32,2048]{1,0:T(8,128)(2,1)S(1)}, u32[]{:S(2)}, u32[]{:S(2)}) collective-permute-start(bf16[32,2048]{1,0:T(8,128)(2,1)S(1)} %get-tuple-element.356), channel_id=1, source_target_pairs={{0,8},{4,12},{8,0},{12,4},{1,9},{5,13},{9,1},{13,5},{2,10},{6,14},... | collective-permute-start | bytes 393224 | tf_op jit(solution)/shard_map/ppermute | solution.py:37
  387.8 6.2 %collective-permute-start.67 = (bf16[32,2048]{1,0:T(8,128)(2,1)S(1)}, bf16[32,2048]{1,0:T(8,128)(2,1)S(1)}, u32[]{:S(2)}, u32[]{:S(2)}) collective-permute-start(bf16[32,2048]{1,0:T(8,128)(2,1)S(1)} %get-tuple-element.366), channel_id=1, source_target_pairs={{0,1},{1,2},{2,3},{3,0},{4,5},{5,6},{6,7},{7,4},{8,9},{9,10},{10,1... | collective-permute-start | bytes 393224 | tf_op jit(solution)/shard_map/ppermute | solution.py:37
  394.1 21.1 %collective-permute-start.71 = (bf16[2,32,2048]{2,1,0:T(8,128)(2,1)S(1)}, bf16[2,32,2048]{2,1,0:T(8,128)(2,1)S(1)}, u32[]{:S(2)}, u32[]{:S(2)}) collective-permute-start(bf16[2,32,2048]{2,1,0:T(8,128)(2,1)S(1)} %pad_maximum_fusion.28), channel_id=1, source_target_pairs={{0,3},{1,0},{2,1},{3,2},{4,7},{5,4},{6,5},{7,6},{8,11},{9,8},{10,9... | collective-permute-start | bytes 786440 | tf_op jit(solution)/shard_map/ppermute | solution.py:37
  394.3 21.0 %collective-permute-start.70 = (bf16[2,32,2048]{2,1,0:T(8,128)(2,1)S(1)}, bf16[2,32,2048]{2,1,0:T(8,128)(2,1)S(1)}, u32[]{:S(2)}, u32[]{:S(2)}) collective-permute-start(bf16[2,32,2048]{2,1,0:T(8,128)(2,1)S(1)} %pad_maximum_fusion.27), channel_id=1, source_target_pairs={{0,1},{1,2},{2,3},{3,0},{4,5},{5,6},{6,7},{7,4},{8,9},{9,10},{10,1... | collective-permute-start | bytes 786440 | tf_op jit(solution)/shard_map/ppermute | solution.py:37
  396.2 10.0 %collective-permute-start.72 = (f32[1,4096]{1,0:T(1,128)S(1)}, f32[1,4096]{1,0:T(1,128)S(1)}, u32[]{:S(2)}, u32[]{:S(2)}) collective-permute-start(f32[1,4096]{1,0:T(1,128)S(1)} %add.165), channel_id=1, source_target_pairs={{0,8},{4,12},{8,0},{12,4},{1,9},{5,13},{9,1},{13,5},{2,10},{6,14},... | collective-permute-start | bytes 49160 | tf_op jit(solution)/shard_map/ppermute | solution.py:37
  397.0 13.1 %collective-permute-start.77 = (bf16[2,3,32,512]{3,2,1,0:T(8,128)(2,1)S(1)}, bf16[2,3,32,512]{3,2,1,0:T(8,128)(2,1)S(1)}, u32[]{:S(2)}, u32[]{:S(2)}) collective-permute-start(bf16[2,3,32,512]{3,2,1,0:T(8,128)(2,1)S(1)} %collective-permute-done.61.refs_0_), channel_id=1, source_target_pairs={{64,80},{80,96},{96,112},{112,64},{65,81},{81,97},{97,113},{113,65... | collective-permute-start | bytes 589832 | tf_op jit(solution)/shard_map/ppermute | solution.py:37
  401.6 9.4 %collective-permute-start.76 = (bf16[2,3,32,512]{3,2,1,0:T(8,128)(2,1)S(1)}, bf16[2,3,32,512]{3,2,1,0:T(8,128)(2,1)S(1)}, u32[]{:S(2)}, u32[]{:S(2)}) collective-permute-start(bf16[2,3,32,512]{3,2,1,0:T(8,128)(2,1)S(1)} %collective-permute-done.61.refs_0_), channel_id=1, source_target_pairs={{64,96},{80,112},{96,64},{112,80},{65,97},{81,113},{97,65},{113,81... | collective-permute-start | bytes 589832 | tf_op jit(solution)/shard_map/ppermute | solution.py:37
  406.3 7.6 %collective-permute-start.75 = (bf16[2,3,32,512]{3,2,1,0:T(8,128)(2,1)S(1)}, bf16[2,3,32,512]{3,2,1,0:T(8,128)(2,1)S(1)}, u32[]{:S(2)}, u32[]{:S(2)}) collective-permute-start(bf16[2,3,32,512]{3,2,1,0:T(8,128)(2,1)S(1)} %collective-permute-done.61.refs_0_), channel_id=1, source_target_pairs={{64,112},{80,64},{96,80},{112,96},{65,113},{81,65},{97,81},{113,97... | collective-permute-start | bytes 589832 | tf_op jit(solution)/shard_map/ppermute | solution.py:37
  415.4 7.7 %collective-permute-start.73 = (bf16[32,2048]{1,0:T(8,128)(2,1)S(1)}, bf16[32,2048]{1,0:T(8,128)(2,1)S(1)}, u32[]{:S(2)}, u32[]{:S(2)}) collective-permute-start(bf16[32,2048]{1,0:T(8,128)(2,1)S(1)} %get-tuple-element.376), channel_id=1, source_target_pairs={{0,8},{4,12},{8,0},{12,4},{1,9},{5,13},{9,1},{13,5},{2,10},{6,14},... | collective-permute-start | bytes 393224 | tf_op jit(solution)/shard_map/ppermute | solution.py:37
  (48 other events, 457.0 us)

commit v3 on v2

--- a/solution.py
+++ b/solution.py
@@ -35,6 +35,20 @@
         (x,) = self.take(x)
         self.held = x
         return lax.ppermute(x, *route)
+
+    def send_both_ways(self, up, down):
+        same = up is down
+        if same:
+            (up,) = self.take(up)
+            down = up
+        else:
+            up, down = self.take(up, down)
+        self.held = down
+        return lax.ppermute(up, *UP_Y), lax.ppermute(down, *DOWN_Y)
+
+    def tie(self, x):
+        x, self.held = lax.optimization_barrier((x, self.held))
+        return x
 
     def take(self, *xs):
         if self.held is None:
@@ -212,13 +226,12 @@
     def y(self):
         self.got = self.order.take_z(self.got)
         self.mine = jnp.stack(ordered(self.low_z, self.keep, self.got))
-        self.before = self.order.send(self.mine, UP_Y)
-        self.behind = self.order.send(self.mine, DOWN_Y)
+        self.before, self.behind = self.order.send_both_ways(self.mine, self.mine)
 
     def far(self):
         self.before, self.behind = self.order.take(self.before, self.behind)
-        self.far_low = self.order.send(self.before[0], UP_Y)
-        self.far_high = self.order.send(self.behind[1], DOWN_Y)
+        both = self.order.send_both_ways(self.before[0], self.behind[1])
+        self.far_low, self.far_high = both
 
     def core(self):
         self.far_low, self.far_high = self.order.take(self.far_low, self.far_high)
@@ -256,16 +269,15 @@
         half, width = self.kept.shape
         (self.got,) = self.order.take(self.got)
         self.summed = (self.kept + self.got.astype(WIDE)).reshape(4, 2, half // 8, width)
-        self.low = self.order.send(self.summed[2, 0].astype(LOW), UP_Y)
-        self.high = self.order.send(self.summed[2, 1].astype(LOW), DOWN_Y)
+        far = self.summed[2].astype(LOW)
+        self.low, self.high = self.order.send_both_ways(far[0], far[1])
 
     def y(self):
         s = self.summed
         self.low, self.high = self.order.take(self.low, self.high)
         up = jnp.stack([s[1, 0] + self.low.astype(WIDE), s[1, 1]]).astype(LOW)
         down = jnp.stack([s[3, 0], s[3, 1] + self.high.astype(WIDE)]).astype(LOW)
-        self.first = self.order.send(up, UP_Y)
-        self.second = self.order.send(down, DOWN_Y)
+        self.first, self.second = self.order.send_both_ways(up, down)
 
     def z(self):
         self.first, self.second = self.order.take(self.first, self.second)
@@ -292,7 +304,7 @@
 
     def take(self):
         i = self.taken
-        (self.landed[i],) = self.order.take(self.landed[i])
+        self.landed[i] = self.order.tie(self.landed[i])
         self.taken = i + 1
 
     def total(self):
@@ -357,18 +369,18 @@
         args = (where, norm_gain, values, cotangent, *settled.end())
         return call(finish_body, outs, 1, *args)
 
+    first = gather(*heads(where, norm_gain, [grad_in[0], act_in[0]], (False, True)))
+    first.z()
     held = stash_guest[0]
     around = [held] + [order.send(held, round_x(step)) for step in (-1, -2, 1)]
-    first = gather(*heads(where, norm_gain, [grad_in[0], act_in[0]], (False, True)))
-    first.z()
-
+
+    (found,) = call(pick_back_body, [parcel], 2, where, plan, *order.take(*around))
+    guests = order.send(found, TO_EARLY)
+    first.y()
     w_up, w_down = order.take(w_up, w_down)
     half = w_up.shape[2] // 2
     here, there = core * half, (1 - core) * half
     down_got = order.send(lax.dynamic_slice_in_dim(w_down[0], there, half, 0), TO_CORE)
-    (found,) = call(pick_back_body, [parcel], 2, where, plan, *order.take(*around))
-    guests = order.send(found, TO_EARLY)
-    first.y()
     up_got = order.send(lax.dynamic_slice_in_dim(w_up[0], there, half, 1), TO_CORE)
     (down_got,) = order.take(down_got)
     down_own = lax.dynamic_slice_in_dim(w_down[0], here, half, 0)
@@ -401,19 +413,23 @@
     stash_rows = stash.rows()
     pre_zero = Bulk(order, times(stash_rows[0], up), 1)
     pre_zero.z()
-    front_pre_zero = Bulk(order, times(front_rows_zero, up), 2)
+    front_pre_zero = Bulk(order, times(front_rows_zero, up), 4)
     front_pre_zero.z()
     pre_one = Bulk(order, order.done(times(stash_rows[1], up).astype(LOW)), 2)
 
     hidden_zero, d_pre_zero = activations(pre_zero.total(), d_hidden_zero.total())
     back = Settle(order, low_z)
-    back.core(times_transposed(d_pre_zero, up))
+    d_rows = order.done(times_transposed(d_pre_zero, up))
+    front_pre_zero.z()
+    front_pre_zero.take()
+    back.core(d_rows)
     front_pre_zero.z()
     front_pre_zero.take()
     back.far()
+    front_pre_zero.z()
+    front_pre_zero.take()
     back.y()
     back.z()
-    pre_one.z()
     hidden_zero, d_pre_zero = swap_hidden(hidden_zero, d_pre_zero)
     d_input_zero, gain_zero = finished(old[0], grad_in[0], back)
     returned = order.send(d_input_zero, LAST)
@@ -424,6 +440,7 @@
     cot_one = jnp.where(section == 7, grad_last, order.take(returned)[0])
     second = gather(*heads(where, norm_gain, [cot_one], (False,)))
     second.z()
+    pre_one.z()
     pre_one.z()
     front.far()
     second.y()
@@ -451,34 +468,44 @@
         act_in[0],
         input_one,
     )
+    landed = order.send(pulled, TO_LATE)
     third.y()
-    landed = order.send(pulled, TO_LATE)
     grad_down = order.done(over_rows(hidden_zero, my_features(cot_rows_zero)))
     third.far()
+    landed = order.tie(landed)
     third.core()
     (front_rows_one,) = third.rows()
-    (landed,) = order.take(landed)
-    front_pre_one = Bulk(order, order.done(times(front_rows_one, up).astype(LOW)), 1)
+    part = order.done(times(front_rows_one, up).astype(LOW))
+    front_pre_one = Bulk(order, part, 4)
+    front_pre_one.z()
     front_pre_one.z()
 
     hidden_one, d_pre_one = activations(pre_one.total(), d_hidden_one.total())
     back = Settle(order, low_z)
-    back.core(times_transposed(d_pre_one, up))
+    d_rows = order.done(times_transposed(d_pre_one, up))
+    back.core(d_rows)
     hidden_one, d_pre_one = swap_hidden(hidden_one, d_pre_one)
-    back.far()
     around = [landed] + [order.send(landed, round_x(step)) for step in (-1, -2, 1)]
-    back.y()
+    front_pre_one.take()
+    front_pre_one.z()
     hidden_one, d_pre_one = whole_hidden(hidden_one, d_pre_one)
-    back.z()
-    (guest_new,) = call(pick_out_body, [parcel], 2, where, plan, *order.take(*around))
     more = over_rows(my_features(stash_rows[1]), d_pre_one)
     grad_up = order.done((grad_up + more).astype(LOW))
+    front_pre_one.take()
+    front_pre_one.z()
+    back.far()
+    (guest_new,) = call(pick_out_body, [parcel], 2, where, plan, *order.take(*around))
+    guest_new = order.done(guest_new)
     more = over_rows(hidden_one, my_features(cot_rows_one))
     grad_down = order.done((grad_down + more).astype(LOW))
+    front_pre_one.take()
+    back.y()
+    front_pre_one.take()
 
     front = Settle(order, low_z)
     front_hidden = jax.nn.silu(front_pre_one.total()).astype(LOW)
     front.core(times(front_hidden, down))
+    back.z()
     d_input_one, gain_one = finished(old[1], cot_one, back)
     gain = gain_zero + gain_one
     gain = gain + order.send(gain, TO_CORE)

time: 434 us -> 415 us (0.956)
  waiting for transfers between devices: 186 us -> 167 us
  local copies, waits for them, and re-layouts: 28.4 us -> 22.3 us
    ppermute x79 -> x52, waiting for transfers between devices: 186 us -> 116 us  [send(): return lax.ppermute(x, *route)]
    ppermute x0 -> x32, waiting for transfers between devices: none -> 51.3 us  [send_both_ways(): return (lax.ppermute(up, *UP_Y), lax.ppermute(down, *DOWN_Y))]
    ppermute x0 -> x32, starting transfers between devices: none -> 43.8 us  [send_both_ways(): return (lax.ppermute(up, *UP_Y), lax.ppermute(down, *DOWN_Y))]
    ppermute x79 -> x52, starting transfers between devices: 101 us -> 59.8 us  [send(): return lax.ppermute(x, *route)]
    unnamed x76 -> x94, local copies, waits for them, and re-layouts: 11 us -> 10 us
  transfers between devices with their start and end apart: 79 -> 84, of which waited for: 44 -> 38; matrix products, arithmetic and copies ran while one was open for 22% -> 23% of each run, Pallas kernels for 2% -> 2%
where the time goes in v3:
time: 415 us; the launch traced here: 407 us
  waiting for transfers between devices  167 us (40%)
  starting transfers between devices  104 us (25%)
  matrix products  68.2 us (16%)
  other arithmetic  33.1 us (8%)
  local copies, waits for them, and re-layouts  22.3 us (5%)
  Pallas kernels  9.69 us (2%)
    ppermute x52, waiting for transfers between devices, send(): return lax.ppermute(x, *route)  116 us
    ppermute x52, starting transfers between devices, send(): return lax.ppermute(x, *route)  59.8 us
    ppermute x32, waiting for transfers between devices, send_both_ways(): return (lax.ppermute(up, *UP_Y), lax.ppermute(down, *DOWN_Y))  51.3 us
    ppermute x32, starting transfers between devices, send_both_ways(): return (lax.ppermute(up, *UP_Y), lax.ppermute(down, *DOWN_Y))  43.8 us
    dot_general x4, matrix products, over_rows(): lax.dot_general(a, b, (((0,), (0,)), ((), ())), preferred_element_type=WIDE)  28.9 us
    dot_general x6, matrix products, times(): return jnp.dot(a, b, preferred_element_type=WIDE)  25.5 us
    dot_general x4, matrix products, times_transposed(): lax.dot_general(a, b, (((1,), (1,)), ((), ())), preferred_element_type=WIDE)  13.8 us
    unnamed x94, local copies, waits for them, and re-layouts  10 us
  transfers between devices with their start and end apart: 84, of which 38 were waited for; matrix products, arithmetic and copies ran while one was open for 23% of the time, Pallas kernels for 2%

profile of v3, /device:TPU:64, one launch (start us, length us, event | category | flops | bytes accessed | tf_op | source)
XLA Modules:
  0.0 407.2 jit_solution(13686751761092282738)
XLA Ops:
  5.8 3.4 collective-permute-start.3
  9.2 4.6 %collective-permute-start.2 = (bf16[2,3,32,512]{3,2,1,0:T(8,128)(2,1)}, bf16[2,3,32,512]{3,2,1,0:T(8,128)(2,1)S(1)}, u32[]{:S(2)}, u32[]{:S(2)}) collective-permute-start(bf16[2,3,32,512]{3,2,1,0:T(8,128)(2,1)} %bitcast.315), channel_id=1, source_target_pairs={{64,96},{80,112},{96,64},{112,80},{65,97},{81,113},{97,65},{113,81... | collective-permute-start | bytes 589832 | tf_op jit(solution)/shard_map/ppermute | solution.py:37
  13.9 3.3 collective-permute-start.1
  18.0 2.6 collective-permute-done.2.refs_2_
  23.9 3.7 dynamic-slice_bitcast_fusion.1
  28.9 3.1 collective-permute-start.5
  32.0 3.6 dynamic-slice_bitcast_fusion
  36.7 4.3 %bitcast_select_fusion.3 = (bf16[1408,1024]{1,0:T(8,128)(2,1)S(1)}, bf16[1408,1024]{1,0:T(8,128)(2,1)S(1)}) fusion(bf16[1408,1024]{1,0:T(8,128)(2,1)} %collective-permute-done.6, pred[]{:T(512)S(6)} %eq.15, bf16[1,2816,1024]{2,1,0:T(8,128)(2,1)} %param.19, s32[]{:T(128)S(6)} %select_n.214), kind=kLoop, calls=%fused_computation.17 | loop fusion | flops 2883584 | bytes 11534341 | tf_op jit(solution)/shard_map/jit(_where)/select_n | solution.py:216
  41.1 3.5 pad_maximum_fusion
  44.6 6.2 %collective-permute-done.4 = bf16[2,2,32,2048]{3,2,0,1:T(8,128)(2,1)S(1)} collective-permute-done((bf16[2,2,32,2048]{3,2,0,1:T(8,128)(2,1)S(1)}, bf16[2,2,32,2048]{3,2,0,1:T(8,128)(2,1)S(1)}, u32[]{:S(2)}, u32[]{:S(2)}) %collective-permute-start.4) | collective-permute-done | bytes 524320 | tf_op jit(solution)/shard_map/ppermute | solution.py:47
  51.7 3.0 bitcast_select_fusion.1
  54.8 3.0 pad_maximum_fusion.1
  61.3 6.3 %collective-permute-done.7 = bf16[2,32,2048]{2,1,0:T(8,128)(2,1)S(1)} collective-permute-done((bf16[2,32,2048]{2,1,0:T(8,128)(2,1)S(1)}, bf16[2,32,2048]{2,1,0:T(8,128)(2,1)S(1)}, u32[]{:S(2)}, u32[]{:S(2)}) %collective-permute-start.7) | collective-permute-done | bytes 262176 | tf_op jit(solution)/shard_map/ppermute | solution.py:47
  72.4 3.5 convolution_convert_fusion.4
  75.9 8.4 %collective-permute-done.14 = bf16[2,2,32,2048]{3,2,0,1:T(8,128)(2,1)S(1)} collective-permute-done((bf16[2,2,32,2048]{3,2,0,1:T(8,128)(2,1)S(1)}, bf16[2,2,32,2048]{3,2,0,1:T(8,128)(2,1)S(1)}, u32[]{:S(2)}, u32[]{:S(2)}) %collective-permute-start.14) | collective-permute-done | bytes 524320 | tf_op jit(solution)/shard_map/ppermute | solution.py:47
  85.3 2.8 collective-permute-start.17
  88.3 3.4 convolution_convert_fusion.5
  93.8 3.3 collective-permute-done.19
  97.2 3.4 convolution_convert_fusion.3
  103.5 4.5 %convolution_convert_fusion.2 = bf16[512,1408]{1,0:T(8,128)(2,1)} fusion(bf16[512,2048]{1,0:T(8,128)(2,1)S(1)} %bitcast.353, bf16[2048,1408]{1,0:T(8,128)(2,1)S(1)} %bitcast.331), kind=kOutput, calls=%fused_computation.6 | convolution fusion | flops 2953510912 | bytes 9306112 | tf_op jit(solution)/shard_map/dot_general | solution.py:318
  108.0 10.9 %collective-permute-done.21 = bf16[512,1408]{1,0:T(8,128)(2,1)S(1)} collective-permute-done((bf16[512,1408]{1,0:T(8,128)(2,1)S(1)}, bf16[512,1408]{1,0:T(8,128)(2,1)S(1)}, u32[]{:S(2)}, u32[]{:S(2)}) %collective-permute-start.21) | collective-permute-done | bytes 1441824 | tf_op jit(solution)/shard_map/ppermute | solution.py:37
  118.9 28.4 %collective-permute-done.22 = bf16[512,1408]{1,0:T(8,128)(2,1)S(1)} collective-permute-done((bf16[512,1408]{1,0:T(8,128)(2,1)S(1)}, bf16[512,1408]{1,0:T(8,128)(2,1)S(1)}, u32[]{:S(2)}, u32[]{:S(2)}) %collective-permute-start.22) | collective-permute-done | bytes 1441824 | tf_op jit(solution)/shard_map/ppermute | solution.py:37
  147.3 2.8 multiply_convert_fusion.4
  150.1 3.4 fusion.90
  155.9 9.2 %collective-permute-done.23 = bf16[128,1408]{1,0:T(8,128)(2,1)S(1)} collective-permute-done((bf16[128,1408]{1,0:T(8,128)(2,1)S(1)}, bf16[128,1408]{1,0:T(8,128)(2,1)S(1)}, u32[]{:S(2)}, u32[]{:S(2)}) %collective-permute-start.23) | collective-permute-done | bytes 360480 | tf_op jit(solution)/shard_map/ppermute | solution.py:37
  169.7 2.6 collective-permute-done.24
  174.7 2.6 collective-permute-start.29
  179.5 3.7 collective-permute-done.28
  184.7 4.1 %collective-permute-done.20 = bf16[128,1408]{1,0:T(8,128)(2,1)S(1)} collective-permute-done((bf16[128,1408]{1,0:T(8,128)(2,1)}, bf16[128,1408]{1,0:T(8,128)(2,1)S(1)}, u32[]{:S(2)}, u32[]{:S(2)}) %collective-permute-start.20) | collective-permute-done | bytes 360480 | tf_op jit(solution)/shard_map/ppermute | solution.py:37
  188.9 7.0 %collective-permute-done.31 = bf16[128,1408]{1,0:T(8,128)(2,1)S(1)} collective-permute-done((bf16[128,1408]{1,0:T(8,128)(2,1)S(1)}, bf16[128,1408]{1,0:T(8,128)(2,1)S(1)}, u32[]{:S(2)}, u32[]{:S(2)}) %collective-permute-start.31) | collective-permute-done | bytes 360480 | tf_op jit(solution)/shard_map/ppermute | solution.py:37
  200.6 6.2 %fusion = f32[512,2048]{1,0:T(8,128)S(1)} fusion(bf16[1408,2048]{1,0:T(8,128)(2,1)} %pad_maximum_fusion, bf16[512,1408]{1,0:T(8,128)(2,1)S(1)} %copy-done.13, bf16[128,1408]{1,0:T(8,128)(2,1)S(1)} %collective-permute-done.31, bf16[128,1408]{1,0:T(8,128)(2,1)S(1)} %copy-done.29, bf16[128,1408]{1,0:T(8,128)(2,1)S(1)} %copy-done.27, ...), kind=kOutput, calls=%fused_computation.38 | convolution fusion | flops 2963603456 | bytes 12845056 | tf_op jit(solution)/shard_map/dot_general | solution.py:318
  212.7 3.4 collective-permute-done.36
  216.6 5.9 %collective-permute-done.34 = bf16[32,2048]{1,0:T(8,128)(2,1)S(1)} collective-permute-done((bf16[32,2048]{1,0:T(8,128)(2,1)S(1)}, bf16[32,2048]{1,0:T(8,128)(2,1)S(1)}, u32[]{:S(2)}, u32[]{:S(2)}) %collective-permute-start.34) | collective-permute-done | bytes 131104 | tf_op jit(solution)/shard_map/ppermute | solution.py:47
  224.6 5.4 %collective-permute-done.39 = bf16[2,1,32,2048]{3,2,0,1:T(8,128)(2,1)S(1)} collective-permute-done((bf16[2,1,32,2048]{3,2,0,1:T(8,128)(2,1)S(1)}, bf16[2,1,32,2048]{3,2,0,1:T(8,128)(2,1)S(1)}, u32[]{:S(2)}, u32[]{:S(2)}) %collective-permute-start.39) | collective-permute-done | bytes 262176 | tf_op jit(solution)/shard_map/ppermute | solution.py:47
  233.3 4.7 %collective-permute-done.37 = bf16[2,32,2048]{2,1,0:T(8,128)(2,1)S(1)} collective-permute-done((bf16[2,32,2048]{2,1,0:T(8,128)(2,1)S(1)}, bf16[2,32,2048]{2,1,0:T(8,128)(2,1)S(1)}, u32[]{:S(2)}, u32[]{:S(2)}) %collective-permute-start.37) | collective-permute-done | bytes 262176 | tf_op jit(solution)/shard_map/ppermute | solution.py:47
  244.9 2.6 collective-permute-done.44
  250.8 3.5 convolution_convert_fusion.1
  254.9 4.8 %collective-permute-done.45 = bf16[256,1408]{1,0:T(8,128)(2,1)S(1)} collective-permute-done((bf16[256,1408]{1,0:T(8,128)(2,1)S(1)}, bf16[256,1408]{1,0:T(8,128)(2,1)S(1)}, u32[]{:S(2)}, u32[]{:S(2)}) %collective-permute-start.45) | collective-permute-done | bytes 720928 | tf_op jit(solution)/shard_map/ppermute | solution.py:37
  259.6 2.8 collective-permute-done.41.got
  263.1 4.3 %collective-permute-start.47 = (bf16[32,4096]{1,0:T(8,128)(2,1)S(1)}, bf16[32,4096]{1,0:T(8,128)(2,1)S(1)}, u32[]{:S(2)}, u32[]{:S(2)}) collective-permute-start(bf16[32,4096]{1,0:T(8,128)(2,1)S(1)} %shard_map.158), channel_id=1, source_target_pairs={{0,16},{16,32},{32,48},{48,64},{64,80},{80,96},{96,112},{1,17},{17... | collective-permute-start | bytes 786440 | tf_op jit(solution)/shard_map/ppermute | solution.py:37
  270.7 6.0 %fusion.22 = f32[1024,2816]{1,0:T(8,128)} fusion(bf16[512,2816]{1,0:T(8,128)(2,1)S(1)} %pad_maximum_fusion.3, bf16[512,2048]{1,0:T(8,128)(2,1)S(1)} %bitcast.351, pred[]{:T(512)S(6)} %eq.15), kind=kOutput, calls=%fused_computation.77 | convolution fusion | flops 2953314304 | bytes 16515073 | tf_op jit(solution)/shard_map/dot_general | solution.py:326
  279.4 3.2 collective-permute-done.50
  284.7 6.1 %fusion.20 = f32[2816,1024]{1,0:T(8,128)} fusion(bf16[512,2816]{1,0:T(8,128)(2,1)S(1)} %pad_maximum_fusion.2, bf16[512,2048]{1,0:T(8,128)(2,1)S(1)} %bitcast.356, pred[]{:T(512)S(6)} %eq.15), kind=kOutput, calls=%fused_computation.74 | convolution fusion | flops 2953314304 | bytes 16515073 | tf_op jit(solution)/shard_map/dot_general | solution.py:326
  295.9 5.2 %collective-permute-done.56.refs_0_ = bf16[2,3,32,512]{3,2,1,0:T(8,128)(2,1)S(1)} collective-permute-done((bf16[2,3,32,512]{3,2,1,0:T(8,128)(2,1)S(1)}, bf16[2,3,32,512]{3,2,1,0:T(8,128)(2,1)S(1)}, u32[]{:S(2)}, u32[]{:S(2)}) %collective-permute-start.56) | collective-permute-done | bytes 196640 | tf_op jit(solution)/shard_map/ppermute | solution.py:37
  301.7 2.6 collective-permute-done.57
  304.3 3.4 convolution_convert_fusion
  308.7 2.9 multiply_convert_fusion.1
  311.6 3.4 fusion.91
  316.5 4.8 %collective-permute-start.65 = (bf16[2,3,32,512]{3,2,1,0:T(8,128)(2,1)S(1)}, bf16[2,3,32,512]{3,2,1,0:T(8,128)(2,1)S(1)}, u32[]{:S(2)}, u32[]{:S(2)}) collective-permute-start(bf16[2,3,32,512]{3,2,1,0:T(8,128)(2,1)S(1)} %collective-permute-done.56.refs_0_), channel_id=1, source_target_pairs={{64,96},{80,112},{96,64},{112,80},{65,97},{81,113},{97,65},{113,81... | collective-permute-start | bytes 589832 | tf_op jit(solution)/shard_map/ppermute | solution.py:37
  321.3 3.7 collective-permute-start.64
  326.1 4.2 %collective-permute-start.66 = (bf16[2,3,32,512]{3,2,1,0:T(8,128)(2,1)S(1)}, bf16[2,3,32,512]{3,2,1,0:T(8,128)(2,1)S(1)}, u32[]{:S(2)}, u32[]{:S(2)}) collective-permute-start(bf16[2,3,32,512]{3,2,1,0:T(8,128)(2,1)S(1)} %collective-permute-done.56.refs_0_), channel_id=1, source_target_pairs={{64,80},{80,96},{96,112},{112,64},{65,81},{81,97},{97,113},{113,65... | collective-permute-start | bytes 589832 | tf_op jit(solution)/shard_map/ppermute | solution.py:37
  331.7 4.0 collective-permute-done.66.refs_3_
  341.3 8.3 %add_convert_fusion = bf16[2816,1024]{1,0:T(8,128)(2,1)} fusion(f32[2816,1024]{1,0:T(8,128)} %fusion.20, bf16[512,2816]{1,0:T(8,128)(2,1)S(1)} %pad_maximum_fusion.4, bf16[512,2048]{1,0:T(8,128)(2,1)} %bitcast.348, pred[]{:T(512)S(6)} %eq.15), kind=kOutput, calls=%fused_computation | convolution fusion | flops 2959081472 | bytes 22282240 | tf_op jit(solution)/shard_map/dot_general | solution.py:326
  351.7 8.6 %add_convert_fusion.1 = bf16[1024,2816]{1,0:T(8,128)(2,1)} fusion(f32[1024,2816]{1,0:T(8,128)} %fusion.22, bf16[512,2816]{1,0:T(8,128)(2,1)S(1)} %pad_maximum_fusion.5, bf16[512,2048]{1,0:T(8,128)(2,1)} %bitcast.354, pred[]{:T(512)S(6)} %eq.15), kind=kOutput, calls=%fused_computation.1 | convolution fusion | flops 2959081472 | bytes 22282240 | tf_op jit(solution)/shard_map/dot_general | solution.py:326
  360.4 3.2 collective-permute-start.73
  363.7 4.6 %fusion.1 = f32[512,2048]{1,0:T(8,128)S(1)} fusion(bf16[1408,2048]{1,0:T(8,128)(2,1)S(1)} %bitcast.329, bf16[512,1408]{1,0:T(8,128)(2,1)S(1)} %convolution_convert_fusion, bf16[128,1408]{1,0:T(8,128)(2,1)} %collective-permute-done.68, bf16[128,1408]{1,0:T(8,128)(2,1)S(1)} %copy-done.31, bf16[128,1408]{1,0:T(8,128)(2,1)S(1)} %collective-permute-done.60, ...), kind=kOutput, calls=%fused_computation.39 | convolution fusion | flops 2963603456 | bytes 12845056 | tf_op jit(solution)/shard_map/dot_general | solution.py:318
  368.5 3.7 collective-permute-done.72
  373.5 3.8 collective-permute-done.74.got
  380.2 3.2 collective-permute-start.76
  383.6 3.4 collective-permute-done.75
  387.2 3.2 collective-permute-start.79
  391.6 2.6 collective-permute-done.80
  394.3 3.7 collective-permute-done.82
  401.4 3.2 collective-permute-done.83
  (360 shorter events, 105.3 us)
Async XLA Ops:
  4.1 19.6 %collective-permute-start = (bf16[2,32,2048]{2,1,0:T(8,128)(2,1)S(1)}, bf16[2,32,2048]{2,1,0:T(8,128)(2,1)S(1)}, u32[]{:S(2)}, u32[]{:S(2)}) collective-permute-start(bf16[2,32,2048]{2,1,0:T(8,128)(2,1)S(1)} %get-tuple-element.214), channel_id=1, source_target_pairs={{0,8},{4,12},{8,0},{12,4},{1,9},{5,13},{9,1},{13,5},{2,10},{6,14},... | collective-permute-start | bytes 786440 | tf_op jit(solution)/shard_map/ppermute | solution.py:37
  5.8 12.2 %collective-permute-start.3 = (bf16[2,3,32,512]{3,2,1,0:T(8,128)(2,1)}, bf16[2,3,32,512]{3,2,1,0:T(8,128)(2,1)S(1)}, u32[]{:S(2)}, u32[]{:S(2)}) collective-permute-start(bf16[2,3,32,512]{3,2,1,0:T(8,128)(2,1)} %bitcast.314), channel_id=1, source_target_pairs={{64,80},{80,96},{96,112},{112,64},{65,81},{81,97},{97,113},{113,65... | collective-permute-start | bytes 589832 | tf_op jit(solution)/shard_map/ppermute | solution.py:37
  9.2 11.5 %collective-permute-start.2 = (bf16[2,3,32,512]{3,2,1,0:T(8,128)(2,1)}, bf16[2,3,32,512]{3,2,1,0:T(8,128)(2,1)S(1)}, u32[]{:S(2)}, u32[]{:S(2)}) collective-permute-start(bf16[2,3,32,512]{3,2,1,0:T(8,128)(2,1)} %bitcast.315), channel_id=1, source_target_pairs={{64,96},{80,112},{96,64},{112,80},{65,97},{81,113},{97,65},{113,81... | collective-permute-start | bytes 589832 | tf_op jit(solution)/shard_map/ppermute | solution.py:37
  13.9 8.3 %collective-permute-start.1 = (bf16[2,3,32,512]{3,2,1,0:T(8,128)(2,1)}, bf16[2,3,32,512]{3,2,1,0:T(8,128)(2,1)S(1)}, u32[]{:S(2)}, u32[]{:S(2)}) collective-permute-start(bf16[2,3,32,512]{3,2,1,0:T(8,128)(2,1)} %bitcast.316), channel_id=1, source_target_pairs={{64,112},{80,64},{96,80},{112,96},{65,113},{81,65},{97,81},{113,97... | collective-permute-start | bytes 589832 | tf_op jit(solution)/shard_map/ppermute | solution.py:37
  27.5 9.2 %collective-permute-start.6 = (bf16[1408,1024]{1,0:T(8,128)(2,1)}, bf16[1408,1024]{1,0:T(8,128)(2,1)}, u32[]{:S(2)}, u32[]{:S(2)}) collective-permute-start(bf16[1408,1024]{1,0:T(8,128)(2,1)} %dynamic-slice_bitcast_fusion.1), channel_id=1, source_target_pairs={{0,4},{4,0},{8,12},{12,8},{1,5},{5,1},{9,13},{13,9},{2,6},{6,2},{1... | collective-permute-start | bytes 8650760 | tf_op jit(solution)/shard_map/ppermute | solution.py:37
  27.5 30.2 %collective-permute-start.9 = (bf16[2,3,32,512]{3,2,1,0:T(8,128)(2,1)S(1)}, bf16[2,3,32,512]{3,2,1,0:T(8,128)(2,1)S(1)}, u32[]{:S(2)}, u32[]{:S(2)}) collective-permute-start(bf16[2,3,32,512]{3,2,1,0:T(8,128)(2,1)S(1)} %shard_map.154), channel_id=1, source_target_pairs={{64,0},{80,16},{96,32},{112,48},{65,1},{81,17},{97,33},{113,49},{6... | collective-permute-start | bytes 589832 | tf_op jit(solution)/shard_map/ppermute | solution.py:37
  28.9 22.0 %collective-permute-start.5 = (bf16[2,2,32,2048]{3,2,1,0:T(8,128)(2,1)S(1)}, bf16[2,2,32,2048]{3,2,1,0:T(8,128)(2,1)S(1)}, u32[]{:S(2)}, u32[]{:S(2)}) collective-permute-start(bf16[2,2,32,2048]{3,2,1,0:T(8,128)(2,1)S(1)} %pad_maximum_fusion.17), channel_id=1, source_target_pairs={{0,3},{1,0},{2,1},{3,2},{4,7},{5,4},{6,5},{7,6},{8,11},{9,8},{10,9... | collective-permute-start | bytes 1572872 | tf_op jit(solution)/shard_map/ppermute | solution.py:47
  35.6 15.3 %collective-permute-start.4 = (bf16[2,2,32,2048]{3,2,0,1:T(8,128)(2,1)S(1)}, bf16[2,2,32,2048]{3,2,0,1:T(8,128)(2,1)S(1)}, u32[]{:S(2)}, u32[]{:S(2)}) collective-permute-start(bf16[2,2,32,2048]{3,2,0,1:T(8,128)(2,1)S(1)} %copy.18), channel_id=1, source_target_pairs={{0,1},{1,2},{2,3},{3,0},{4,5},{5,6},{6,7},{7,4},{8,9},{9,10},{10,1... | collective-permute-start | bytes 1572872 | tf_op jit(solution)/shard_map/ppermute | solution.py:47
  35.6 16.1 %collective-permute-start.10 = (bf16[1024,1408]{1,0:T(8,128)(2,1)}, bf16[1024,1408]{1,0:T(8,128)(2,1)}, u32[]{:S(2)}, u32[]{:S(2)}) collective-permute-start(bf16[1024,1408]{1,0:T(8,128)(2,1)} %dynamic-slice_bitcast_fusion), channel_id=1, source_target_pairs={{0,4},{4,0},{8,12},{12,8},{1,5},{5,1},{9,13},{13,9},{2,6},{6,2},{1... | collective-permute-start | bytes 8650760 | tf_op jit(solution)/shard_map/ppermute | solution.py:37
  51.6 16.0 %collective-permute-start.8 = (bf16[2,32,2048]{2,1,0:T(8,128)(2,1)S(1)}, bf16[2,32,2048]{2,1,0:T(8,128)(2,1)S(1)}, u32[]{:S(2)}, u32[]{:S(2)}) collective-permute-start(bf16[2,32,2048]{2,1,0:T(8,128)(2,1)S(1)} %get-tuple-element.234), channel_id=1, source_target_pairs={{0,3},{1,0},{2,1},{3,2},{4,7},{5,4},{6,5},{7,6},{8,11},{9,8},{10,9... | collective-permute-start | bytes 786440 | tf_op jit(solution)/shard_map/ppermute | solution.py:47
  58.8 8.8 %collective-permute-start.7 = (bf16[2,32,2048]{2,1,0:T(8,128)(2,1)S(1)}, bf16[2,32,2048]{2,1,0:T(8,128)(2,1)S(1)}, u32[]{:S(2)}, u32[]{:S(2)}) collective-permute-start(bf16[2,32,2048]{2,1,0:T(8,128)(2,1)S(1)} %slice_bitcast_fusion.10), channel_id=1, source_target_pairs={{0,1},{1,2},{2,3},{3,0},{4,5},{5,6},{6,7},{7,4},{8,9},{9,10},{10,1... | collective-permute-start | bytes 786440 | tf_op jit(solution)/shard_map/ppermute | solution.py:47
  60.9 7.7 %collective-permute-start.13 = (bf16[2,32,2048]{2,1,0:T(8,128)(2,1)S(1)}, bf16[2,32,2048]{2,1,0:T(8,128)(2,1)S(1)}, u32[]{:S(2)}, u32[]{:S(2)}) collective-permute-start(bf16[2,32,2048]{2,1,0:T(8,128)(2,1)S(1)} %get-tuple-element.239), channel_id=1, source_target_pairs={{0,8},{4,12},{8,0},{12,4},{1,9},{5,13},{9,1},{13,5},{2,10},{6,14},... | collective-permute-start | bytes 786440 | tf_op jit(solution)/shard_map/ppermute | solution.py:37
  68.8 15.5 %collective-permute-start.15 = (bf16[2,2,32,2048]{3,2,1,0:T(8,128)(2,1)S(1)}, bf16[2,2,32,2048]{3,2,1,0:T(8,128)(2,1)S(1)}, u32[]{:S(2)}, u32[]{:S(2)}) collective-permute-start(bf16[2,2,32,2048]{3,2,1,0:T(8,128)(2,1)S(1)} %pad_maximum_fusion.18), channel_id=1, source_target_pairs={{0,3},{1,0},{2,1},{3,2},{4,7},{5,4},{6,5},{7,6},{8,11},{9,8},{10,9... | collective-permute-start | bytes 1572872 | tf_op jit(solution)/shard_map/ppermute | solution.py:47
  69.6 14.7 %collective-permute-start.14 = (bf16[2,2,32,2048]{3,2,0,1:T(8,128)(2,1)S(1)}, bf16[2,2,32,2048]{3,2,0,1:T(8,128)(2,1)S(1)}, u32[]{:S(2)}, u32[]{:S(2)}) collective-permute-start(bf16[2,2,32,2048]{3,2,0,1:T(8,128)(2,1)S(1)} %copy.23), channel_id=1, source_target_pairs={{0,1},{1,2},{2,3},{3,0},{4,5},{5,6},{6,7},{7,4},{8,9},{9,10},{10,1... | collective-permute-start | bytes 1572872 | tf_op jit(solution)/shard_map/ppermute | solution.py:47
  84.3 34.6 %collective-permute-start.21 = (bf16[512,1408]{1,0:T(8,128)(2,1)S(1)}, bf16[512,1408]{1,0:T(8,128)(2,1)S(1)}, u32[]{:S(2)}, u32[]{:S(2)}) collective-permute-start(bf16[512,1408]{1,0:T(8,128)(2,1)S(1)} %convolution_convert_fusion.4), channel_id=1, source_target_pairs={{0,8},{4,12},{8,0},{12,4},{1,9},{5,13},{9,1},{13,5},{2,10},{6,14},... | collective-permute-start | bytes 4325384 | tf_op jit(solution)/shard_map/ppermute | solution.py:37
  84.8 7.8 %collective-permute-start.16 = (bf16[2,32,2048]{2,1,0:T(8,128)(2,1)S(1)}, bf16[2,32,2048]{2,1,0:T(8,128)(2,1)S(1)}, u32[]{:S(2)}, u32[]{:S(2)}) collective-permute-start(bf16[2,32,2048]{2,1,0:T(8,128)(2,1)S(1)} %slice_bitcast_fusion.8), channel_id=1, source_target_pairs={{0,1},{1,2},{2,3},{3,0},{4,5},{5,6},{6,7},{7,4},{8,9},{9,10},{10,1... | collective-permute-start | bytes 786440 | tf_op jit(solution)/shard_map/ppermute | solution.py:47
  85.3 7.3 %collective-permute-start.17 = (bf16[2,32,2048]{2,1,0:T(8,128)(2,1)S(1)}, bf16[2,32,2048]{2,1,0:T(8,128)(2,1)S(1)}, u32[]{:S(2)}, u32[]{:S(2)}) collective-permute-start(bf16[2,32,2048]{2,1,0:T(8,128)(2,1)S(1)} %get-tuple-element.253), channel_id=1, source_target_pairs={{0,3},{1,0},{2,1},{3,2},{4,7},{5,4},{6,5},{7,6},{8,11},{9,8},{10,9... | collective-permute-start | bytes 786440 | tf_op jit(solution)/shard_map/ppermute | solution.py:47
  100.6 46.7 %collective-permute-start.22 = (bf16[512,1408]{1,0:T(8,128)(2,1)S(1)}, bf16[512,1408]{1,0:T(8,128)(2,1)S(1)}, u32[]{:S(2)}, u32[]{:S(2)}) collective-permute-start(bf16[512,1408]{1,0:T(8,128)(2,1)S(1)} %convolution_convert_fusion.3), channel_id=1, source_target_pairs={{0,8},{4,12},{8,0},{12,4},{1,9},{5,13},{9,1},{13,5},{2,10},{6,14},... | collective-permute-start | bytes 4325384 | tf_op jit(solution)/shard_map/ppermute | solution.py:37
  153.7 12.1 %collective-permute-start.25 = (bf16[256,2048]{1,0:T(8,128)(2,1)S(1)}, bf16[256,2048]{1,0:T(8,128)(2,1)S(1)}, u32[]{:S(2)}, u32[]{:S(2)}) collective-permute-start(bf16[256,2048]{1,0:T(8,128)(2,1)S(1)} %slice.709), channel_id=1, source_target_pairs={{0,4},{4,0},{8,12},{12,8},{1,5},{5,1},{9,13},{13,9},{2,6},{6,2},{1... | collective-permute-start | bytes 3145736 | tf_op jit(solution)/shard_map/ppermute | solution.py:37
  153.8 11.3 %collective-permute-start.23 = (bf16[128,1408]{1,0:T(8,128)(2,1)S(1)}, bf16[128,1408]{1,0:T(8,128)(2,1)S(1)}, u32[]{:S(2)}, u32[]{:S(2)}) collective-permute-start(bf16[128,1408]{1,0:T(8,128)(2,1)S(1)} %get-tuple-element.266), channel_id=1, source_target_pairs={{0,8},{4,12},{8,0},{12,4},{1,9},{5,13},{9,1},{13,5},{2,10},{6,14},... | collective-permute-start | bytes 1081352 | tf_op jit(solution)/shard_map/ppermute | solution.py:37
  154.2 18.1 %collective-permute-start.24 = (bf16[128,1408]{1,0:T(8,128)(2,1)S(1)}, bf16[128,1408]{1,0:T(8,128)(2,1)S(1)}, u32[]{:S(2)}, u32[]{:S(2)}) collective-permute-start(bf16[128,1408]{1,0:T(8,128)(2,1)S(1)} %get-tuple-element.270), channel_id=1, source_target_pairs={{0,8},{4,12},{8,0},{12,4},{1,9},{5,13},{9,1},{13,5},{2,10},{6,14},... | collective-permute-start | bytes 1081352 | tf_op jit(solution)/shard_map/ppermute | solution.py:37
  174.0 9.1 %collective-permute-start.28 = (bf16[2,32,2048]{2,1,0:T(8,128)(2,1)}, bf16[2,32,2048]{2,1,0:T(8,128)(2,1)S(1)}, u32[]{:S(2)}, u32[]{:S(2)}) collective-permute-start(bf16[2,32,2048]{2,1,0:T(8,128)(2,1)} %pad_maximum_fusion.19), channel_id=1, source_target_pairs={{0,1},{1,2},{2,3},{3,0},{4,5},{5,6},{6,7},{7,4},{8,9},{9,10},{10,1... | collective-permute-start | bytes 786440 | tf_op jit(solution)/shard_map/ppermute | solution.py:47
  174.7 8.4 %collective-permute-start.29 = (bf16[2,32,2048]{2,1,0:T(8,128)(2,1)}, bf16[2,32,2048]{2,1,0:T(8,128)(2,1)}, u32[]{:S(2)}, u32[]{:S(2)}) collective-permute-start(bf16[2,32,2048]{2,1,0:T(8,128)(2,1)} %pad_maximum_fusion.20), channel_id=1, source_target_pairs={{0,3},{1,0},{2,1},{3,2},{4,7},{5,4},{6,5},{7,6},{8,11},{9,8},{10,9... | collective-permute-start | bytes 786440 | tf_op jit(solution)/shard_map/ppermute | solution.py:47
  177.3 11.6 %collective-permute-start.20 = (bf16[128,1408]{1,0:T(8,128)(2,1)}, bf16[128,1408]{1,0:T(8,128)(2,1)S(1)}, u32[]{:S(2)}, u32[]{:S(2)}) collective-permute-start(bf16[128,1408]{1,0:T(8,128)(2,1)} %get-tuple-element.260), channel_id=1, source_target_pairs={{0,8},{4,12},{8,0},{12,4},{1,9},{5,13},{9,1},{13,5},{2,10},{6,14},... | collective-permute-start | bytes 1081352 | tf_op jit(solution)/shard_map/ppermute | solution.py:37
  177.8 18.0 %collective-permute-start.31 = (bf16[128,1408]{1,0:T(8,128)(2,1)S(1)}, bf16[128,1408]{1,0:T(8,128)(2,1)S(1)}, u32[]{:S(2)}, u32[]{:S(2)}) collective-permute-start(bf16[128,1408]{1,0:T(8,128)(2,1)S(1)} %get-tuple-element.276), channel_id=1, source_target_pairs={{0,8},{4,12},{8,0},{12,4},{1,9},{5,13},{9,1},{13,5},{2,10},{6,14},... | collective-permute-start | bytes 1081352 | tf_op jit(solution)/shard_map/ppermute | solution.py:37
  184.2 13.0 %collective-permute-start.30 = (bf16[32,2048]{1,0:T(8,128)(2,1)S(1)}, bf16[32,2048]{1,0:T(8,128)(2,1)S(1)}, u32[]{:S(2)}, u32[]{:S(2)}) collective-permute-start(bf16[32,2048]{1,0:T(8,128)(2,1)S(1)} %get-tuple-element.283), channel_id=1, source_target_pairs={{0,8},{4,12},{8,0},{12,4},{1,9},{5,13},{9,1},{13,5},{2,10},{6,14},... | collective-permute-start | bytes 393224 | tf_op jit(solution)/shard_map/ppermute | solution.py:37
  198.3 10.9 %collective-permute-start.33 = (bf16[32,4096]{1,0:T(8,128)(2,1)S(1)}, bf16[32,4096]{1,0:T(8,128)(2,1)S(1)}, u32[]{:S(2)}, u32[]{:S(2)}) collective-permute-start(bf16[32,4096]{1,0:T(8,128)(2,1)S(1)} %get-tuple-element.290), channel_id=1, source_target_pairs={{16,0},{32,16},{48,32},{64,48},{80,64},{96,80},{112,96},{17,1},{33... | collective-permute-start | bytes 786440 | tf_op jit(solution)/shard_map/ppermute | solution.py:37
  208.6 58.8 %collective-permute-start.49 = (bf16[512,1408]{1,0:T(8,128)(2,1)S(1)}, bf16[512,1408]{1,0:T(8,128)(2,1)S(1)}, u32[]{:S(2)}, u32[]{:S(2)}) collective-permute-start(bf16[512,1408]{1,0:T(8,128)(2,1)S(1)} %copy-done.11), channel_id=1, source_target_pairs={{0,4},{4,0},{8,12},{12,8},{1,5},{5,1},{9,13},{13,9},{2,6},{6,2},{1... | collective-permute-start | bytes 4325384 | tf_op jit(solution)/shard_map/ppermute | solution.py:37
  209.1 59.3 %collective-permute-start.48 = (bf16[512,1408]{1,0:T(8,128)(2,1)S(1)}, bf16[512,1408]{1,0:T(8,128)(2,1)S(1)}, u32[]{:S(2)}, u32[]{:S(2)}) collective-permute-start(bf16[512,1408]{1,0:T(8,128)(2,1)S(1)} %copy-done.10), channel_id=1, source_target_pairs={{0,4},{4,0},{8,12},{12,8},{1,5},{5,1},{9,13},{13,9},{2,6},{6,2},{1... | collective-permute-start | bytes 4325384 | tf_op jit(solution)/shard_map/ppermute | solution.py:37
  210.2 44.1 %collective-permute-start.46 = (bf16[256,1408]{1,0:T(8,128)(2,1)S(1)}, bf16[256,1408]{1,0:T(8,128)(2,1)S(1)}, u32[]{:S(2)}, u32[]{:S(2)}) collective-permute-start(bf16[256,1408]{1,0:T(8,128)(2,1)S(1)} %get-tuple-element.300), channel_id=1, source_target_pairs={{0,8},{4,12},{8,0},{12,4},{1,9},{5,13},{9,1},{13,5},{2,10},{6,14},... | collective-permute-start | bytes 2162696 | tf_op jit(solution)/shard_map/ppermute | solution.py:37
  212.4 10.1 %collective-permute-start.35 = (bf16[32,2048]{1,0:T(8,128)(2,1)S(1)}, bf16[32,2048]{1,0:T(8,128)(2,1)S(1)}, u32[]{:S(2)}, u32[]{:S(2)}) collective-permute-start(bf16[32,2048]{1,0:T(8,128)(2,1)S(1)} %get-tuple-element.303), channel_id=1, source_target_pairs={{0,3},{1,0},{2,1},{3,2},{4,7},{5,4},{6,5},{7,6},{8,11},{9,8},{10,9... | collective-permute-start | bytes 393224 | tf_op jit(solution)/shard_map/ppermute | solution.py:47
  222.5 8.8 %collective-permute-start.40 = (bf16[2,1,32,2048]{3,2,1,0:T(8,128)(2,1)S(1)}, bf16[2,1,32,2048]{3,2,1,0:T(8,128)(2,1)S(1)}, u32[]{:S(2)}, u32[]{:S(2)}) collective-permute-start(bf16[2,1,32,2048]{3,2,1,0:T(8,128)(2,1)S(1)} %get-tuple-element.306), channel_id=1, source_target_pairs={{0,3},{1,0},{2,1},{3,2},{4,7},{5,4},{6,5},{7,6},{8,11},{9,8},{10,9... | collective-permute-start | bytes 786440 | tf_op jit(solution)/shard_map/ppermute | solution.py:47
  222.5 7.6 %collective-permute-start.39 = (bf16[2,1,32,2048]{3,2,0,1:T(8,128)(2,1)S(1)}, bf16[2,1,32,2048]{3,2,0,1:T(8,128)(2,1)S(1)}, u32[]{:S(2)}, u32[]{:S(2)}) collective-permute-start(bf16[2,1,32,2048]{3,2,0,1:T(8,128)(2,1)S(1)} %bitcast.344), channel_id=1, source_target_pairs={{0,1},{1,2},{2,3},{3,0},{4,5},{5,6},{6,7},{7,4},{8,9},{9,10},{10,1... | collective-permute-start | bytes 786440 | tf_op jit(solution)/shard_map/ppermute | solution.py:47
  230.1 8.0 %collective-permute-start.37 = (bf16[2,32,2048]{2,1,0:T(8,128)(2,1)S(1)}, bf16[2,32,2048]{2,1,0:T(8,128)(2,1)S(1)}, u32[]{:S(2)}, u32[]{:S(2)}) collective-permute-start(bf16[2,32,2048]{2,1,0:T(8,128)(2,1)S(1)} %pad_maximum_fusion.22), channel_id=1, source_target_pairs={{0,1},{1,2},{2,3},{3,0},{4,5},{5,6},{6,7},{7,4},{8,9},{9,10},{10,1... | collective-permute-start | bytes 786440 | tf_op jit(solution)/shard_map/ppermute | solution.py:47
  231.3 7.8 %collective-permute-start.38 = (bf16[2,32,2048]{2,1,0:T(8,128)(2,1)S(1)}, bf16[2,32,2048]{2,1,0:T(8,128)(2,1)S(1)}, u32[]{:S(2)}, u32[]{:S(2)}) collective-permute-start(bf16[2,32,2048]{2,1,0:T(8,128)(2,1)S(1)} %pad_maximum_fusion.23), channel_id=1, source_target_pairs={{0,3},{1,0},{2,1},{3,2},{4,7},{5,4},{6,5},{7,6},{8,11},{9,8},{10,9... | collective-permute-start | bytes 786440 | tf_op jit(solution)/shard_map/ppermute | solution.py:47
  244.2 15.5 %collective-permute-start.45 = (bf16[256,1408]{1,0:T(8,128)(2,1)S(1)}, bf16[256,1408]{1,0:T(8,128)(2,1)S(1)}, u32[]{:S(2)}, u32[]{:S(2)}) collective-permute-start(bf16[256,1408]{1,0:T(8,128)(2,1)S(1)} %get-tuple-element.299), channel_id=1, source_target_pairs={{0,8},{4,12},{8,0},{12,4},{1,9},{5,13},{9,1},{13,5},{2,10},{6,14},... | collective-permute-start | bytes 2162696 | tf_op jit(solution)/shard_map/ppermute | solution.py:37
  247.5 15.0 %collective-permute-start.41 = (bf16[32,2048]{1,0:T(8,128)(2,1)S(1)}, bf16[32,2048]{1,0:T(8,128)(2,1)S(1)}, u32[]{:S(2)}, u32[]{:S(2)}) collective-permute-start(bf16[32,2048]{1,0:T(8,128)(2,1)S(1)} %get-tuple-element.316), channel_id=1, source_target_pairs={{0,8},{4,12},{8,0},{12,4},{1,9},{5,13},{9,1},{13,5},{2,10},{6,14},... | collective-permute-start | bytes 393224 | tf_op jit(solution)/shard_map/ppermute | solution.py:37
  254.4 28.2 %collective-permute-start.51 = (bf16[256,1408]{1,0:T(8,128)(2,1)S(1)}, bf16[256,1408]{1,0:T(8,128)(2,1)S(1)}, u32[]{:S(2)}, u32[]{:S(2)}) collective-permute-start(bf16[256,1408]{1,0:T(8,128)(2,1)S(1)} %get-tuple-element.322), channel_id=1, source_target_pairs={{0,8},{4,12},{8,0},{12,4},{1,9},{5,13},{9,1},{13,5},{2,10},{6,14},... | collective-permute-start | bytes 2162696 | tf_op jit(solution)/shard_map/ppermute | solution.py:37
  263.1 13.6 %collective-permute-start.47 = (bf16[32,4096]{1,0:T(8,128)(2,1)S(1)}, bf16[32,4096]{1,0:T(8,128)(2,1)S(1)}, u32[]{:S(2)}, u32[]{:S(2)}) collective-permute-start(bf16[32,4096]{1,0:T(8,128)(2,1)S(1)} %shard_map.158), channel_id=1, source_target_pairs={{0,16},{16,32},{32,48},{48,64},{64,80},{80,96},{96,112},{1,17},{17... | collective-permute-start | bytes 786440 | tf_op jit(solution)/shard_map/ppermute | solution.py:37
  282.6 9.9 %collective-permute-start.53 = (bf16[2,1,32,2048]{3,2,1,0:T(8,128)(2,1)S(1)}, bf16[2,1,32,2048]{3,2,1,0:T(8,128)(2,1)S(1)}, u32[]{:S(2)}, u32[]{:S(2)}) collective-permute-start(bf16[2,1,32,2048]{3,2,1,0:T(8,128)(2,1)S(1)} %get-tuple-element.338), channel_id=1, source_target_pairs={{0,3},{1,0},{2,1},{3,2},{4,7},{5,4},{6,5},{7,6},{8,11},{9,8},{10,9... | collective-permute-start | bytes 786440 | tf_op jit(solution)/shard_map/ppermute | solution.py:47
  282.7 9.8 %collective-permute-start.52 = (bf16[2,1,32,2048]{3,2,0,1:T(8,128)(2,1)S(1)}, bf16[2,1,32,2048]{3,2,0,1:T(8,128)(2,1)S(1)}, u32[]{:S(2)}, u32[]{:S(2)}) collective-permute-start(bf16[2,1,32,2048]{3,2,0,1:T(8,128)(2,1)S(1)} %bitcast.345), channel_id=1, source_target_pairs={{0,1},{1,2},{2,3},{3,0},{4,5},{5,6},{6,7},{7,4},{8,9},{9,10},{10,1... | collective-permute-start | bytes 786440 | tf_op jit(solution)/shard_map/ppermute | solution.py:47
  290.8 10.3 %collective-permute-start.56 = (bf16[2,3,32,512]{3,2,1,0:T(8,128)(2,1)S(1)}, bf16[2,3,32,512]{3,2,1,0:T(8,128)(2,1)S(1)}, u32[]{:S(2)}, u32[]{:S(2)}) collective-permute-start(bf16[2,3,32,512]{3,2,1,0:T(8,128)(2,1)S(1)} %get-tuple-element.336), channel_id=1, source_target_pairs={{0,64},{16,80},{32,96},{48,112},{1,65},{17,81},{33,97},{49,113},{2... | collective-permute-start | bytes 589832 | tf_op jit(solution)/shard_map/ppermute | solution.py:37
  292.1 16.7 %collective-permute-start.59 = (bf16[256,1408]{1,0:T(8,128)(2,1)S(1)}, bf16[256,1408]{1,0:T(8,128)(2,1)S(1)}, u32[]{:S(2)}, u32[]{:S(2)}) collective-permute-start(bf16[256,1408]{1,0:T(8,128)(2,1)S(1)} %get-tuple-element.335), channel_id=1, source_target_pairs={{0,8},{4,12},{8,0},{12,4},{1,9},{5,13},{9,1},{13,5},{2,10},{6,14},... | collective-permute-start | bytes 2162696 | tf_op jit(solution)/shard_map/ppermute | solution.py:37
  292.6 8.5 %collective-permute-start.54 = (bf16[1,32,2048]{2,1,0:T(8,128)(2,1)S(1)}, bf16[1,32,2048]{2,1,0:T(8,128)(2,1)S(1)}, u32[]{:S(2)}, u32[]{:S(2)}) collective-permute-start(bf16[1,32,2048]{2,1,0:T(8,128)(2,1)S(1)} %slice_bitcast_fusion.31), channel_id=1, source_target_pairs={{0,1},{1,2},{2,3},{3,0},{4,5},{5,6},{6,7},{7,4},{8,9},{9,10},{10,1... | collective-permute-start | bytes 393224 | tf_op jit(solution)/shard_map/ppermute | solution.py:47
  293.5 7.6 %collective-permute-start.55 = (bf16[1,32,2048]{2,1,0:T(8,128)(2,1)S(1)}, bf16[1,32,2048]{2,1,0:T(8,128)(2,1)S(1)}, u32[]{:S(2)}, u32[]{:S(2)}) collective-permute-start(bf16[1,32,2048]{2,1,0:T(8,128)(2,1)S(1)} %slice_bitcast_fusion.30), channel_id=1, source_target_pairs={{0,3},{1,0},{2,1},{3,2},{4,7},{5,4},{6,5},{7,6},{8,11},{9,8},{10,9... | collective-permute-start | bytes 393224 | tf_op jit(solution)/shard_map/ppermute | solution.py:47
  315.2 15.1 %collective-permute-start.67 = (bf16[256,2048]{1,0:T(8,128)(2,1)S(1)}, bf16[256,2048]{1,0:T(8,128)(2,1)S(1)}, u32[]{:S(2)}, u32[]{:S(2)}) collective-permute-start(bf16[256,2048]{1,0:T(8,128)(2,1)S(1)} %slice.707), channel_id=1, source_target_pairs={{0,4},{4,0},{8,12},{12,8},{1,5},{5,1},{9,13},{13,9},{2,6},{6,2},{1... | collective-permute-start | bytes 3145736 | tf_op jit(solution)/shard_map/ppermute | solution.py:37
  315.4 10.7 %collective-permute-start.58 = (bf16[128,1408]{1,0:T(8,128)(2,1)S(1)}, bf16[128,1408]{1,0:T(8,128)(2,1)S(1)}, u32[]{:S(2)}, u32[]{:S(2)}) collective-permute-start(bf16[128,1408]{1,0:T(8,128)(2,1)S(1)} %get-tuple-element.350), channel_id=1, source_target_pairs={{0,8},{4,12},{8,0},{12,4},{1,9},{5,13},{9,1},{13,5},{2,10},{6,14},... | collective-permute-start | bytes 1081352 | tf_op jit(solution)/shard_map/ppermute | solution.py:37
  316.5 19.1 %collective-permute-start.65 = (bf16[2,3,32,512]{3,2,1,0:T(8,128)(2,1)S(1)}, bf16[2,3,32,512]{3,2,1,0:T(8,128)(2,1)S(1)}, u32[]{:S(2)}, u32[]{:S(2)}) collective-permute-start(bf16[2,3,32,512]{3,2,1,0:T(8,128)(2,1)S(1)} %collective-permute-done.56.refs_0_), channel_id=1, source_target_pairs={{64,96},{80,112},{96,64},{112,80},{65,97},{81,113},{97,65},{113,81... | collective-permute-start | bytes 589832 | tf_op jit(solution)/shard_map/ppermute | solution.py:37
  321.3 15.5 %collective-permute-start.64 = (bf16[2,3,32,512]{3,2,1,0:T(8,128)(2,1)S(1)}, bf16[2,3,32,512]{3,2,1,0:T(8,128)(2,1)S(1)}, u32[]{:S(2)}, u32[]{:S(2)}) collective-permute-start(bf16[2,3,32,512]{3,2,1,0:T(8,128)(2,1)S(1)} %collective-permute-done.56.refs_0_), channel_id=1, source_target_pairs={{64,112},{80,64},{96,80},{112,96},{65,113},{81,65},{97,81},{113,97... | collective-permute-start | bytes 589832 | tf_op jit(solution)/shard_map/ppermute | solution.py:37
  325.0 15.3 %collective-permute-start.62 = (bf16[512,1408]{1,0:T(8,128)(2,1)S(1)}, bf16[512,1408]{1,0:T(8,128)(2,1)S(1)}, u32[]{:S(2)}, u32[]{:S(2)}) collective-permute-start(bf16[512,1408]{1,0:T(8,128)(2,1)S(1)} %get-tuple-element.362), channel_id=1, source_target_pairs={{0,4},{4,0},{8,12},{12,8},{1,5},{5,1},{9,13},{13,9},{2,6},{6,2},{1... | collective-permute-start | bytes 4325384 | tf_op jit(solution)/shard_map/ppermute | solution.py:37
  326.1 9.5 %collective-permute-start.66 = (bf16[2,3,32,512]{3,2,1,0:T(8,128)(2,1)S(1)}, bf16[2,3,32,512]{3,2,1,0:T(8,128)(2,1)S(1)}, u32[]{:S(2)}, u32[]{:S(2)}) collective-permute-start(bf16[2,3,32,512]{3,2,1,0:T(8,128)(2,1)S(1)} %collective-permute-done.56.refs_0_), channel_id=1, source_target_pairs={{64,80},{80,96},{96,112},{112,64},{65,81},{81,97},{97,113},{113,65... | collective-permute-start | bytes 589832 | tf_op jit(solution)/shard_map/ppermute | solution.py:37
  330.3 33.3 %collective-permute-start.68 = (bf16[128,1408]{1,0:T(8,128)(2,1)}, bf16[128,1408]{1,0:T(8,128)(2,1)}, u32[]{:S(2)}, u32[]{:S(2)}) collective-permute-start(bf16[128,1408]{1,0:T(8,128)(2,1)} %get-tuple-element.459), channel_id=1, source_target_pairs={{0,8},{4,12},{8,0},{12,4},{1,9},{5,13},{9,1},{13,5},{2,10},{6,14},... | collective-permute-start | bytes 1081352 | tf_op jit(solution)/shard_map/ppermute | solution.py:37
  335.6 15.2 %collective-permute-start.61 = (bf16[512,1408]{1,0:T(8,128)(2,1)S(1)}, bf16[512,1408]{1,0:T(8,128)(2,1)S(1)}, u32[]{:S(2)}, u32[]{:S(2)}) collective-permute-start(bf16[512,1408]{1,0:T(8,128)(2,1)S(1)} %get-tuple-element.363), channel_id=1, source_target_pairs={{0,4},{4,0},{8,12},{12,8},{1,5},{5,1},{9,13},{13,9},{2,6},{6,2},{1... | collective-permute-start | bytes 4325384 | tf_op jit(solution)/shard_map/ppermute | solution.py:37
  335.6 13.9 %collective-permute-start.63 = (bf16[128,1408]{1,0:T(8,128)(2,1)}, bf16[128,1408]{1,0:T(8,128)(2,1)S(1)}, u32[]{:S(2)}, u32[]{:S(2)}) collective-permute-start(bf16[128,1408]{1,0:T(8,128)(2,1)} %get-tuple-element.460), channel_id=1, source_target_pairs={{0,8},{4,12},{8,0},{12,4},{1,9},{5,13},{9,1},{13,5},{2,10},{6,14},... | collective-permute-start | bytes 1081352 | tf_op jit(solution)/shard_map/ppermute | solution.py:37
  336.8 14.0 %collective-permute-start.70 = (bf16[32,2048]{1,0:T(8,128)(2,1)S(1)}, bf16[32,2048]{1,0:T(8,128)(2,1)S(1)}, u32[]{:S(2)}, u32[]{:S(2)}) collective-permute-start(bf16[32,2048]{1,0:T(8,128)(2,1)S(1)} %get-tuple-element.375), channel_id=1, source_target_pairs={{0,3},{1,0},{2,1},{3,2},{4,7},{5,4},{6,5},{7,6},{8,11},{9,8},{10,9... | collective-permute-start | bytes 393224 | tf_op jit(solution)/shard_map/ppermute | solution.py:47
  340.3 10.5 %collective-permute-start.69 = (bf16[32,2048]{1,0:T(8,128)(2,1)S(1)}, bf16[32,2048]{1,0:T(8,128)(2,1)S(1)}, u32[]{:S(2)}, u32[]{:S(2)}) collective-permute-start(bf16[32,2048]{1,0:T(8,128)(2,1)S(1)} %get-tuple-element.383), channel_id=1, source_target_pairs={{0,1},{1,2},{2,3},{3,0},{4,5},{5,6},{6,7},{7,4},{8,9},{9,10},{10,1... | collective-permute-start | bytes 393224 | tf_op jit(solution)/shard_map/ppermute | solution.py:47
  349.6 14.1 %collective-permute-start.60 = (bf16[128,1408]{1,0:T(8,128)(2,1)S(1)}, bf16[128,1408]{1,0:T(8,128)(2,1)S(1)}, u32[]{:S(2)}, u32[]{:S(2)}) collective-permute-start(bf16[128,1408]{1,0:T(8,128)(2,1)S(1)} %get-tuple-element.353), channel_id=1, source_target_pairs={{0,8},{4,12},{8,0},{12,4},{1,9},{5,13},{9,1},{13,5},{2,10},{6,14},... | collective-permute-start | bytes 1081352 | tf_op jit(solution)/shard_map/ppermute | solution.py:37
  360.4 11.8 %collective-permute-start.73 = (bf16[2,32,2048]{2,1,0:T(8,128)(2,1)S(1)}, bf16[2,32,2048]{2,1,0:T(8,128)(2,1)S(1)}, u32[]{:S(2)}, u32[]{:S(2)}) collective-permute-start(bf16[2,32,2048]{2,1,0:T(8,128)(2,1)S(1)} %pad_maximum_fusion.26), channel_id=1, source_target_pairs={{0,3},{1,0},{2,1},{3,2},{4,7},{5,4},{6,5},{7,6},{8,11},{9,8},{10,9... | collective-permute-start | bytes 786440 | tf_op jit(solution)/shard_map/ppermute | solution.py:47
  363.6 8.5 %collective-permute-start.72 = (bf16[2,32,2048]{2,1,0:T(8,128)(2,1)S(1)}, bf16[2,32,2048]{2,1,0:T(8,128)(2,1)S(1)}, u32[]{:S(2)}, u32[]{:S(2)}) collective-permute-start(bf16[2,32,2048]{2,1,0:T(8,128)(2,1)S(1)} %pad_maximum_fusion.25), channel_id=1, source_target_pairs={{0,1},{1,2},{2,3},{3,0},{4,5},{5,6},{6,7},{7,4},{8,9},{9,10},{10,1... | collective-permute-start | bytes 786440 | tf_op jit(solution)/shard_map/ppermute | solution.py:47
  368.4 11.3 %collective-permute-start.71 = (bf16[256,2048]{1,0:T(8,128)(2,1)S(1)}, bf16[256,2048]{1,0:T(8,128)(2,1)S(1)}, u32[]{:S(2)}, u32[]{:S(2)}) collective-permute-start(bf16[256,2048]{1,0:T(8,128)(2,1)S(1)} %slice.706), channel_id=1, source_target_pairs={{0,4},{4,0},{8,12},{12,8},{1,5},{5,1},{9,13},{13,9},{2,6},{6,2},{1... | collective-permute-start | bytes 3145736 | tf_op jit(solution)/shard_map/ppermute | solution.py:37
  380.2 6.8 %collective-permute-start.75 = (bf16[32,2048]{1,0:T(8,128)(2,1)S(1)}, bf16[32,2048]{1,0:T(8,128)(2,1)S(1)}, u32[]{:S(2)}, u32[]{:S(2)}) collective-permute-start(bf16[32,2048]{1,0:T(8,128)(2,1)S(1)} %get-tuple-element.404), channel_id=1, source_target_pairs={{0,1},{1,2},{2,3},{3,0},{4,5},{5,6},{6,7},{7,4},{8,9},{9,10},{10,1... | collective-permute-start | bytes 393224 | tf_op jit(solution)/shard_map/ppermute | solution.py:47
  387.1 10.9 %collective-permute-start.78 = (bf16[2,32,2048]{2,1,0:T(8,128)(2,1)S(1)}, bf16[2,32,2048]{2,1,0:T(8,128)(2,1)S(1)}, u32[]{:S(2)}, u32[]{:S(2)}) collective-permute-start(bf16[2,32,2048]{2,1,0:T(8,128)(2,1)S(1)} %pad_maximum_fusion.27), channel_id=1, source_target_pairs={{0,1},{1,2},{2,3},{3,0},{4,5},{5,6},{6,7},{7,4},{8,9},{9,10},{10,1... | collective-permute-start | bytes 786440 | tf_op jit(solution)/shard_map/ppermute | solution.py:47
  387.2 10.8 %collective-permute-start.79 = (bf16[2,32,2048]{2,1,0:T(8,128)(2,1)S(1)}, bf16[2,32,2048]{2,1,0:T(8,128)(2,1)S(1)}, u32[]{:S(2)}, u32[]{:S(2)}) collective-permute-start(bf16[2,32,2048]{2,1,0:T(8,128)(2,1)S(1)} %pad_maximum_fusion.28), channel_id=1, source_target_pairs={{0,3},{1,0},{2,1},{3,2},{4,7},{5,4},{6,5},{7,6},{8,11},{9,8},{10,9... | collective-permute-start | bytes 786440 | tf_op jit(solution)/shard_map/ppermute | solution.py:47
  398.2 7.1 %collective-permute-start.81 = (bf16[32,2048]{1,0:T(8,128)(2,1)S(1)}, bf16[32,2048]{1,0:T(8,128)(2,1)S(1)}, u32[]{:S(2)}, u32[]{:S(2)}) collective-permute-start(bf16[32,2048]{1,0:T(8,128)(2,1)S(1)} %get-tuple-element.414), channel_id=1, source_target_pairs={{0,8},{4,12},{8,0},{12,4},{1,9},{5,13},{9,1},{13,5},{2,10},{6,14},... | collective-permute-start | bytes 393224 | tf_op jit(solution)/shard_map/ppermute | solution.py:37
  (62 other events, 439.8 us)

commit v4 on v3

--- a/solution.py
+++ b/solution.py
@@ -512,8 +512,8 @@
     front.far()
     gain = gain + order.send(gain, TO_Z)
     front.y()
+    front.z()
     gain = gain + order.send(gain, ("tensor", [(t, t ^ 1) for t in range(4)]))
-    front.z()
     gain = gain + order.send(gain, ("tensor", [(t, t ^ 2) for t in range(4)]))
     (front_one,) = call(add_body, [whole], 1, where, input_one, *front.end())
 

time: 415 us -> 416 us (level)
  transfers between devices with their start and end apart: 84 -> 84, of which waited for: 38 -> 39; matrix products, arithmetic and copies ran while one was open for 23% -> 23% of each run, Pallas kernels for 2% -> 2%
where the time goes in v4:
time: 416 us; the launch traced here: 408 us
  waiting for transfers between devices  166 us (40%)
  starting transfers between devices  106 us (25%)
  matrix products  68.2 us (16%)
  other arithmetic  33.1 us (8%)
  local copies, waits for them, and re-layouts  22.3 us (5%)
  Pallas kernels  9.69 us (2%)
    ppermute x52, waiting for transfers between devices, send(): return lax.ppermute(x, *route)  113 us
    ppermute x52, starting transfers between devices, send(): return lax.ppermute(x, *route)  62.1 us
    ppermute x32, waiting for transfers between devices, send_both_ways(): return (lax.ppermute(up, *UP_Y), lax.ppermute(down, *DOWN_Y))  53.1 us
    ppermute x32, starting transfers between devices, send_both_ways(): return (lax.ppermute(up, *UP_Y), lax.ppermute(down, *DOWN_Y))  43.8 us
    dot_general x4, matrix products, over_rows(): lax.dot_general(a, b, (((0,), (0,)), ((), ())), preferred_element_type=WIDE)  28.9 us
    dot_general x6, matrix products, times(): return jnp.dot(a, b, preferred_element_type=WIDE)  25.5 us
    dot_general x4, matrix products, times_transposed(): lax.dot_general(a, b, (((1,), (1,)), ((), ())), preferred_element_type=WIDE)  13.8 us
    unnamed x94, local copies, waits for them, and re-layouts  10 us
  transfers between devices with their start and end apart: 84, of which 39 were waited for; matrix products, arithmetic and copies ran while one was open for 23% of the time, Pallas kernels for 2%

profile of v4, /device:TPU:64, one launch (start us, length us, event | category | flops | bytes accessed | tf_op | source)
XLA Modules:
  0.0 407.8 jit_solution(17251569264862738104)
XLA Ops:
  5.8 3.4 collective-permute-start.3
  9.2 4.6 %collective-permute-start.2 = (bf16[2,3,32,512]{3,2,1,0:T(8,128)(2,1)}, bf16[2,3,32,512]{3,2,1,0:T(8,128)(2,1)S(1)}, u32[]{:S(2)}, u32[]{:S(2)}) collective-permute-start(bf16[2,3,32,512]{3,2,1,0:T(8,128)(2,1)} %bitcast.315), channel_id=1, source_target_pairs={{64,96},{80,112},{96,64},{112,80},{65,97},{81,113},{97,65},{113,81... | collective-permute-start | bytes 589832 | tf_op jit(solution)/shard_map/ppermute | solution.py:37
  13.9 3.3 collective-permute-start.1
  18.0 2.6 collective-permute-done.2.refs_2_
  23.9 3.7 dynamic-slice_bitcast_fusion.1
  28.9 3.1 collective-permute-start.5
  32.0 3.6 dynamic-slice_bitcast_fusion
  36.7 4.3 %bitcast_select_fusion.3 = (bf16[1408,1024]{1,0:T(8,128)(2,1)S(1)}, bf16[1408,1024]{1,0:T(8,128)(2,1)S(1)}) fusion(bf16[1408,1024]{1,0:T(8,128)(2,1)} %collective-permute-done.6, pred[]{:T(512)S(6)} %eq.15, bf16[1,2816,1024]{2,1,0:T(8,128)(2,1)} %param.19, s32[]{:T(128)S(6)} %select_n.214), kind=kLoop, calls=%fused_computation.17 | loop fusion | flops 2883584 | bytes 11534341 | tf_op jit(solution)/shard_map/jit(_where)/select_n | solution.py:216
  41.1 3.5 pad_maximum_fusion
  44.6 6.2 %collective-permute-done.4 = bf16[2,2,32,2048]{3,2,0,1:T(8,128)(2,1)S(1)} collective-permute-done((bf16[2,2,32,2048]{3,2,0,1:T(8,128)(2,1)S(1)}, bf16[2,2,32,2048]{3,2,0,1:T(8,128)(2,1)S(1)}, u32[]{:S(2)}, u32[]{:S(2)}) %collective-permute-start.4) | collective-permute-done | bytes 524320 | tf_op jit(solution)/shard_map/ppermute | solution.py:47
  51.7 3.0 bitcast_select_fusion.1
  54.8 3.0 pad_maximum_fusion.1
  61.3 6.3 %collective-permute-done.7 = bf16[2,32,2048]{2,1,0:T(8,128)(2,1)S(1)} collective-permute-done((bf16[2,32,2048]{2,1,0:T(8,128)(2,1)S(1)}, bf16[2,32,2048]{2,1,0:T(8,128)(2,1)S(1)}, u32[]{:S(2)}, u32[]{:S(2)}) %collective-permute-start.7) | collective-permute-done | bytes 262176 | tf_op jit(solution)/shard_map/ppermute | solution.py:47
  72.4 3.5 convolution_convert_fusion.4
  75.9 8.4 %collective-permute-done.14 = bf16[2,2,32,2048]{3,2,0,1:T(8,128)(2,1)S(1)} collective-permute-done((bf16[2,2,32,2048]{3,2,0,1:T(8,128)(2,1)S(1)}, bf16[2,2,32,2048]{3,2,0,1:T(8,128)(2,1)S(1)}, u32[]{:S(2)}, u32[]{:S(2)}) %collective-permute-start.14) | collective-permute-done | bytes 524320 | tf_op jit(solution)/shard_map/ppermute | solution.py:47
  85.3 2.8 collective-permute-start.17
  88.3 3.4 convolution_convert_fusion.5
  93.8 3.3 collective-permute-done.19
  97.2 3.4 convolution_convert_fusion.3
  103.5 4.5 %convolution_convert_fusion.2 = bf16[512,1408]{1,0:T(8,128)(2,1)} fusion(bf16[512,2048]{1,0:T(8,128)(2,1)S(1)} %bitcast.353, bf16[2048,1408]{1,0:T(8,128)(2,1)S(1)} %bitcast.331), kind=kOutput, calls=%fused_computation.6 | convolution fusion | flops 2953510912 | bytes 9306112 | tf_op jit(solution)/shard_map/dot_general | solution.py:318
  108.0 10.9 %collective-permute-done.21 = bf16[512,1408]{1,0:T(8,128)(2,1)S(1)} collective-permute-done((bf16[512,1408]{1,0:T(8,128)(2,1)S(1)}, bf16[512,1408]{1,0:T(8,128)(2,1)S(1)}, u32[]{:S(2)}, u32[]{:S(2)}) %collective-permute-start.21) | collective-permute-done | bytes 1441824 | tf_op jit(solution)/shard_map/ppermute | solution.py:37
  118.9 28.4 %collective-permute-done.22 = bf16[512,1408]{1,0:T(8,128)(2,1)S(1)} collective-permute-done((bf16[512,1408]{1,0:T(8,128)(2,1)S(1)}, bf16[512,1408]{1,0:T(8,128)(2,1)S(1)}, u32[]{:S(2)}, u32[]{:S(2)}) %collective-permute-start.22) | collective-permute-done | bytes 1441824 | tf_op jit(solution)/shard_map/ppermute | solution.py:37
  147.3 2.8 multiply_convert_fusion.4
  150.1 3.4 fusion.90
  155.9 9.2 %collective-permute-done.23 = bf16[128,1408]{1,0:T(8,128)(2,1)S(1)} collective-permute-done((bf16[128,1408]{1,0:T(8,128)(2,1)S(1)}, bf16[128,1408]{1,0:T(8,128)(2,1)S(1)}, u32[]{:S(2)}, u32[]{:S(2)}) %collective-permute-start.23) | collective-permute-done | bytes 360480 | tf_op jit(solution)/shard_map/ppermute | solution.py:37
  169.7 2.6 collective-permute-done.24
  174.7 2.6 collective-permute-start.29
  179.5 3.7 collective-permute-done.28
  184.7 4.1 %collective-permute-done.20 = bf16[128,1408]{1,0:T(8,128)(2,1)S(1)} collective-permute-done((bf16[128,1408]{1,0:T(8,128)(2,1)}, bf16[128,1408]{1,0:T(8,128)(2,1)S(1)}, u32[]{:S(2)}, u32[]{:S(2)}) %collective-permute-start.20) | collective-permute-done | bytes 360480 | tf_op jit(solution)/shard_map/ppermute | solution.py:37
  188.9 7.0 %collective-permute-done.31 = bf16[128,1408]{1,0:T(8,128)(2,1)S(1)} collective-permute-done((bf16[128,1408]{1,0:T(8,128)(2,1)S(1)}, bf16[128,1408]{1,0:T(8,128)(2,1)S(1)}, u32[]{:S(2)}, u32[]{:S(2)}) %collective-permute-start.31) | collective-permute-done | bytes 360480 | tf_op jit(solution)/shard_map/ppermute | solution.py:37
  200.6 6.2 %fusion = f32[512,2048]{1,0:T(8,128)S(1)} fusion(bf16[1408,2048]{1,0:T(8,128)(2,1)} %pad_maximum_fusion, bf16[512,1408]{1,0:T(8,128)(2,1)S(1)} %copy-done.13, bf16[128,1408]{1,0:T(8,128)(2,1)S(1)} %collective-permute-done.31, bf16[128,1408]{1,0:T(8,128)(2,1)S(1)} %copy-done.29, bf16[128,1408]{1,0:T(8,128)(2,1)S(1)} %copy-done.27, ...), kind=kOutput, calls=%fused_computation.38 | convolution fusion | flops 2963603456 | bytes 12845056 | tf_op jit(solution)/shard_map/dot_general | solution.py:318
  212.7 3.4 collective-permute-done.36
  216.6 5.9 %collective-permute-done.34 = bf16[32,2048]{1,0:T(8,128)(2,1)S(1)} collective-permute-done((bf16[32,2048]{1,0:T(8,128)(2,1)S(1)}, bf16[32,2048]{1,0:T(8,128)(2,1)S(1)}, u32[]{:S(2)}, u32[]{:S(2)}) %collective-permute-start.34) | collective-permute-done | bytes 131104 | tf_op jit(solution)/shard_map/ppermute | solution.py:47
  224.6 5.4 %collective-permute-done.39 = bf16[2,1,32,2048]{3,2,0,1:T(8,128)(2,1)S(1)} collective-permute-done((bf16[2,1,32,2048]{3,2,0,1:T(8,128)(2,1)S(1)}, bf16[2,1,32,2048]{3,2,0,1:T(8,128)(2,1)S(1)}, u32[]{:S(2)}, u32[]{:S(2)}) %collective-permute-start.39) | collective-permute-done | bytes 262176 | tf_op jit(solution)/shard_map/ppermute | solution.py:47
  233.3 4.7 %collective-permute-done.37 = bf16[2,32,2048]{2,1,0:T(8,128)(2,1)S(1)} collective-permute-done((bf16[2,32,2048]{2,1,0:T(8,128)(2,1)S(1)}, bf16[2,32,2048]{2,1,0:T(8,128)(2,1)S(1)}, u32[]{:S(2)}, u32[]{:S(2)}) %collective-permute-start.37) | collective-permute-done | bytes 262176 | tf_op jit(solution)/shard_map/ppermute | solution.py:47
  241.7 2.5 collective-permute-done.42
  244.9 2.6 collective-permute-done.44
  250.8 3.5 convolution_convert_fusion.1
  254.9 4.8 %collective-permute-done.45 = bf16[256,1408]{1,0:T(8,128)(2,1)S(1)} collective-permute-done((bf16[256,1408]{1,0:T(8,128)(2,1)S(1)}, bf16[256,1408]{1,0:T(8,128)(2,1)S(1)}, u32[]{:S(2)}, u32[]{:S(2)}) %collective-permute-start.45) | collective-permute-done | bytes 720928 | tf_op jit(solution)/shard_map/ppermute | solution.py:37
  259.6 2.8 collective-permute-done.41.got
  263.1 4.3 %collective-permute-start.47 = (bf16[32,4096]{1,0:T(8,128)(2,1)S(1)}, bf16[32,4096]{1,0:T(8,128)(2,1)S(1)}, u32[]{:S(2)}, u32[]{:S(2)}) collective-permute-start(bf16[32,4096]{1,0:T(8,128)(2,1)S(1)} %shard_map.158), channel_id=1, source_target_pairs={{0,16},{16,32},{32,48},{48,64},{64,80},{80,96},{96,112},{1,17},{17... | collective-permute-start | bytes 786440 | tf_op jit(solution)/shard_map/ppermute | solution.py:37
  270.7 6.0 %fusion.22 = f32[1024,2816]{1,0:T(8,128)} fusion(bf16[512,2816]{1,0:T(8,128)(2,1)S(1)} %pad_maximum_fusion.3, bf16[512,2048]{1,0:T(8,128)(2,1)S(1)} %bitcast.351, pred[]{:T(512)S(6)} %eq.15), kind=kOutput, calls=%fused_computation.77 | convolution fusion | flops 2953314304 | bytes 16515073 | tf_op jit(solution)/shard_map/dot_general | solution.py:326
  279.4 3.2 collective-permute-done.50
  284.7 6.1 %fusion.20 = f32[2816,1024]{1,0:T(8,128)} fusion(bf16[512,2816]{1,0:T(8,128)(2,1)S(1)} %pad_maximum_fusion.2, bf16[512,2048]{1,0:T(8,128)(2,1)S(1)} %bitcast.356, pred[]{:T(512)S(6)} %eq.15), kind=kOutput, calls=%fused_computation.74 | convolution fusion | flops 2953314304 | bytes 16515073 | tf_op jit(solution)/shard_map/dot_general | solution.py:326
  295.9 5.2 %collective-permute-done.56.refs_0_ = bf16[2,3,32,512]{3,2,1,0:T(8,128)(2,1)S(1)} collective-permute-done((bf16[2,3,32,512]{3,2,1,0:T(8,128)(2,1)S(1)}, bf16[2,3,32,512]{3,2,1,0:T(8,128)(2,1)S(1)}, u32[]{:S(2)}, u32[]{:S(2)}) %collective-permute-start.56) | collective-permute-done | bytes 196640 | tf_op jit(solution)/shard_map/ppermute | solution.py:37
  301.7 2.6 collective-permute-done.57
  304.3 3.4 convolution_convert_fusion
  308.7 2.9 multiply_convert_fusion.1
  311.6 3.4 fusion.91
  316.5 4.8 %collective-permute-start.65 = (bf16[2,3,32,512]{3,2,1,0:T(8,128)(2,1)S(1)}, bf16[2,3,32,512]{3,2,1,0:T(8,128)(2,1)S(1)}, u32[]{:S(2)}, u32[]{:S(2)}) collective-permute-start(bf16[2,3,32,512]{3,2,1,0:T(8,128)(2,1)S(1)} %collective-permute-done.56.refs_0_), channel_id=1, source_target_pairs={{64,96},{80,112},{96,64},{112,80},{65,97},{81,113},{97,65},{113,81... | collective-permute-start | bytes 589832 | tf_op jit(solution)/shard_map/ppermute | solution.py:37
  321.3 3.7 collective-permute-start.64
  326.1 4.2 %collective-permute-start.66 = (bf16[2,3,32,512]{3,2,1,0:T(8,128)(2,1)S(1)}, bf16[2,3,32,512]{3,2,1,0:T(8,128)(2,1)S(1)}, u32[]{:S(2)}, u32[]{:S(2)}) collective-permute-start(bf16[2,3,32,512]{3,2,1,0:T(8,128)(2,1)S(1)} %collective-permute-done.56.refs_0_), channel_id=1, source_target_pairs={{64,80},{80,96},{96,112},{112,64},{65,81},{81,97},{97,113},{113,65... | collective-permute-start | bytes 589832 | tf_op jit(solution)/shard_map/ppermute | solution.py:37
  331.7 4.0 collective-permute-done.66.refs_3_
  341.3 8.3 %add_convert_fusion = bf16[2816,1024]{1,0:T(8,128)(2,1)} fusion(f32[2816,1024]{1,0:T(8,128)} %fusion.20, bf16[512,2816]{1,0:T(8,128)(2,1)S(1)} %pad_maximum_fusion.4, bf16[512,2048]{1,0:T(8,128)(2,1)} %bitcast.348, pred[]{:T(512)S(6)} %eq.15), kind=kOutput, calls=%fused_computation | convolution fusion | flops 2959081472 | bytes 22282240 | tf_op jit(solution)/shard_map/dot_general | solution.py:326
  351.7 8.6 %add_convert_fusion.1 = bf16[1024,2816]{1,0:T(8,128)(2,1)} fusion(f32[1024,2816]{1,0:T(8,128)} %fusion.22, bf16[512,2816]{1,0:T(8,128)(2,1)S(1)} %pad_maximum_fusion.5, bf16[512,2048]{1,0:T(8,128)(2,1)} %bitcast.354, pred[]{:T(512)S(6)} %eq.15), kind=kOutput, calls=%fused_computation.1 | convolution fusion | flops 2959081472 | bytes 22282240 | tf_op jit(solution)/shard_map/dot_general | solution.py:326
  360.4 3.2 collective-permute-start.73
  363.7 4.6 %fusion.1 = f32[512,2048]{1,0:T(8,128)S(1)} fusion(bf16[1408,2048]{1,0:T(8,128)(2,1)S(1)} %bitcast.329, bf16[512,1408]{1,0:T(8,128)(2,1)S(1)} %convolution_convert_fusion, bf16[128,1408]{1,0:T(8,128)(2,1)} %collective-permute-done.68, bf16[128,1408]{1,0:T(8,128)(2,1)S(1)} %copy-done.31, bf16[128,1408]{1,0:T(8,128)(2,1)S(1)} %collective-permute-done.60, ...), kind=kOutput, calls=%fused_computation.39 | convolution fusion | flops 2963603456 | bytes 12845056 | tf_op jit(solution)/shard_map/dot_general | solution.py:318
  368.5 3.7 collective-permute-done.72
  373.5 3.8 collective-permute-done.74.got
  380.2 3.2 collective-permute-start.76
  383.6 3.4 collective-permute-done.75
  387.2 3.2 collective-permute-start.79
  391.6 2.5 collective-permute-done.81
  399.9 2.7 collective-permute-start.83
  (360 shorter events, 107.6 us)
Async XLA Ops:
  4.1 19.6 %collective-permute-start = (bf16[2,32,2048]{2,1,0:T(8,128)(2,1)S(1)}, bf16[2,32,2048]{2,1,0:T(8,128)(2,1)S(1)}, u32[]{:S(2)}, u32[]{:S(2)}) collective-permute-start(bf16[2,32,2048]{2,1,0:T(8,128)(2,1)S(1)} %get-tuple-element.214), channel_id=1, source_target_pairs={{0,8},{4,12},{8,0},{12,4},{1,9},{5,13},{9,1},{13,5},{2,10},{6,14},... | collective-permute-start | bytes 786440 | tf_op jit(solution)/shard_map/ppermute | solution.py:37
  5.8 12.2 %collective-permute-start.3 = (bf16[2,3,32,512]{3,2,1,0:T(8,128)(2,1)}, bf16[2,3,32,512]{3,2,1,0:T(8,128)(2,1)S(1)}, u32[]{:S(2)}, u32[]{:S(2)}) collective-permute-start(bf16[2,3,32,512]{3,2,1,0:T(8,128)(2,1)} %bitcast.314), channel_id=1, source_target_pairs={{64,80},{80,96},{96,112},{112,64},{65,81},{81,97},{97,113},{113,65... | collective-permute-start | bytes 589832 | tf_op jit(solution)/shard_map/ppermute | solution.py:37
  9.2 11.5 %collective-permute-start.2 = (bf16[2,3,32,512]{3,2,1,0:T(8,128)(2,1)}, bf16[2,3,32,512]{3,2,1,0:T(8,128)(2,1)S(1)}, u32[]{:S(2)}, u32[]{:S(2)}) collective-permute-start(bf16[2,3,32,512]{3,2,1,0:T(8,128)(2,1)} %bitcast.315), channel_id=1, source_target_pairs={{64,96},{80,112},{96,64},{112,80},{65,97},{81,113},{97,65},{113,81... | collective-permute-start | bytes 589832 | tf_op jit(solution)/shard_map/ppermute | solution.py:37
  13.9 8.3 %collective-permute-start.1 = (bf16[2,3,32,512]{3,2,1,0:T(8,128)(2,1)}, bf16[2,3,32,512]{3,2,1,0:T(8,128)(2,1)S(1)}, u32[]{:S(2)}, u32[]{:S(2)}) collective-permute-start(bf16[2,3,32,512]{3,2,1,0:T(8,128)(2,1)} %bitcast.316), channel_id=1, source_target_pairs={{64,112},{80,64},{96,80},{112,96},{65,113},{81,65},{97,81},{113,97... | collective-permute-start | bytes 589832 | tf_op jit(solution)/shard_map/ppermute | solution.py:37
  27.5 9.2 %collective-permute-start.6 = (bf16[1408,1024]{1,0:T(8,128)(2,1)}, bf16[1408,1024]{1,0:T(8,128)(2,1)}, u32[]{:S(2)}, u32[]{:S(2)}) collective-permute-start(bf16[1408,1024]{1,0:T(8,128)(2,1)} %dynamic-slice_bitcast_fusion.1), channel_id=1, source_target_pairs={{0,4},{4,0},{8,12},{12,8},{1,5},{5,1},{9,13},{13,9},{2,6},{6,2},{1... | collective-permute-start | bytes 8650760 | tf_op jit(solution)/shard_map/ppermute | solution.py:37
  27.5 30.2 %collective-permute-start.9 = (bf16[2,3,32,512]{3,2,1,0:T(8,128)(2,1)S(1)}, bf16[2,3,32,512]{3,2,1,0:T(8,128)(2,1)S(1)}, u32[]{:S(2)}, u32[]{:S(2)}) collective-permute-start(bf16[2,3,32,512]{3,2,1,0:T(8,128)(2,1)S(1)} %shard_map.154), channel_id=1, source_target_pairs={{64,0},{80,16},{96,32},{112,48},{65,1},{81,17},{97,33},{113,49},{6... | collective-permute-start | bytes 589832 | tf_op jit(solution)/shard_map/ppermute | solution.py:37
  28.9 22.0 %collective-permute-start.5 = (bf16[2,2,32,2048]{3,2,1,0:T(8,128)(2,1)S(1)}, bf16[2,2,32,2048]{3,2,1,0:T(8,128)(2,1)S(1)}, u32[]{:S(2)}, u32[]{:S(2)}) collective-permute-start(bf16[2,2,32,2048]{3,2,1,0:T(8,128)(2,1)S(1)} %pad_maximum_fusion.17), channel_id=1, source_target_pairs={{0,3},{1,0},{2,1},{3,2},{4,7},{5,4},{6,5},{7,6},{8,11},{9,8},{10,9... | collective-permute-start | bytes 1572872 | tf_op jit(solution)/shard_map/ppermute | solution.py:47
  35.6 15.3 %collective-permute-start.4 = (bf16[2,2,32,2048]{3,2,0,1:T(8,128)(2,1)S(1)}, bf16[2,2,32,2048]{3,2,0,1:T(8,128)(2,1)S(1)}, u32[]{:S(2)}, u32[]{:S(2)}) collective-permute-start(bf16[2,2,32,2048]{3,2,0,1:T(8,128)(2,1)S(1)} %copy.18), channel_id=1, source_target_pairs={{0,1},{1,2},{2,3},{3,0},{4,5},{5,6},{6,7},{7,4},{8,9},{9,10},{10,1... | collective-permute-start | bytes 1572872 | tf_op jit(solution)/shard_map/ppermute | solution.py:47
  35.6 16.1 %collective-permute-start.10 = (bf16[1024,1408]{1,0:T(8,128)(2,1)}, bf16[1024,1408]{1,0:T(8,128)(2,1)}, u32[]{:S(2)}, u32[]{:S(2)}) collective-permute-start(bf16[1024,1408]{1,0:T(8,128)(2,1)} %dynamic-slice_bitcast_fusion), channel_id=1, source_target_pairs={{0,4},{4,0},{8,12},{12,8},{1,5},{5,1},{9,13},{13,9},{2,6},{6,2},{1... | collective-permute-start | bytes 8650760 | tf_op jit(solution)/shard_map/ppermute | solution.py:37
  51.6 16.0 %collective-permute-start.8 = (bf16[2,32,2048]{2,1,0:T(8,128)(2,1)S(1)}, bf16[2,32,2048]{2,1,0:T(8,128)(2,1)S(1)}, u32[]{:S(2)}, u32[]{:S(2)}) collective-permute-start(bf16[2,32,2048]{2,1,0:T(8,128)(2,1)S(1)} %get-tuple-element.234), channel_id=1, source_target_pairs={{0,3},{1,0},{2,1},{3,2},{4,7},{5,4},{6,5},{7,6},{8,11},{9,8},{10,9... | collective-permute-start | bytes 786440 | tf_op jit(solution)/shard_map/ppermute | solution.py:47
  58.8 8.8 %collective-permute-start.7 = (bf16[2,32,2048]{2,1,0:T(8,128)(2,1)S(1)}, bf16[2,32,2048]{2,1,0:T(8,128)(2,1)S(1)}, u32[]{:S(2)}, u32[]{:S(2)}) collective-permute-start(bf16[2,32,2048]{2,1,0:T(8,128)(2,1)S(1)} %slice_bitcast_fusion.10), channel_id=1, source_target_pairs={{0,1},{1,2},{2,3},{3,0},{4,5},{5,6},{6,7},{7,4},{8,9},{9,10},{10,1... | collective-permute-start | bytes 786440 | tf_op jit(solution)/shard_map/ppermute | solution.py:47
  60.9 7.7 %collective-permute-start.13 = (bf16[2,32,2048]{2,1,0:T(8,128)(2,1)S(1)}, bf16[2,32,2048]{2,1,0:T(8,128)(2,1)S(1)}, u32[]{:S(2)}, u32[]{:S(2)}) collective-permute-start(bf16[2,32,2048]{2,1,0:T(8,128)(2,1)S(1)} %get-tuple-element.239), channel_id=1, source_target_pairs={{0,8},{4,12},{8,0},{12,4},{1,9},{5,13},{9,1},{13,5},{2,10},{6,14},... | collective-permute-start | bytes 786440 | tf_op jit(solution)/shard_map/ppermute | solution.py:37
  68.8 15.5 %collective-permute-start.15 = (bf16[2,2,32,2048]{3,2,1,0:T(8,128)(2,1)S(1)}, bf16[2,2,32,2048]{3,2,1,0:T(8,128)(2,1)S(1)}, u32[]{:S(2)}, u32[]{:S(2)}) collective-permute-start(bf16[2,2,32,2048]{3,2,1,0:T(8,128)(2,1)S(1)} %pad_maximum_fusion.18), channel_id=1, source_target_pairs={{0,3},{1,0},{2,1},{3,2},{4,7},{5,4},{6,5},{7,6},{8,11},{9,8},{10,9... | collective-permute-start | bytes 1572872 | tf_op jit(solution)/shard_map/ppermute | solution.py:47
  69.6 14.7 %collective-permute-start.14 = (bf16[2,2,32,2048]{3,2,0,1:T(8,128)(2,1)S(1)}, bf16[2,2,32,2048]{3,2,0,1:T(8,128)(2,1)S(1)}, u32[]{:S(2)}, u32[]{:S(2)}) collective-permute-start(bf16[2,2,32,2048]{3,2,0,1:T(8,128)(2,1)S(1)} %copy.23), channel_id=1, source_target_pairs={{0,1},{1,2},{2,3},{3,0},{4,5},{5,6},{6,7},{7,4},{8,9},{9,10},{10,1... | collective-permute-start | bytes 1572872 | tf_op jit(solution)/shard_map/ppermute | solution.py:47
  84.3 34.6 %collective-permute-start.21 = (bf16[512,1408]{1,0:T(8,128)(2,1)S(1)}, bf16[512,1408]{1,0:T(8,128)(2,1)S(1)}, u32[]{:S(2)}, u32[]{:S(2)}) collective-permute-start(bf16[512,1408]{1,0:T(8,128)(2,1)S(1)} %convolution_convert_fusion.4), channel_id=1, source_target_pairs={{0,8},{4,12},{8,0},{12,4},{1,9},{5,13},{9,1},{13,5},{2,10},{6,14},... | collective-permute-start | bytes 4325384 | tf_op jit(solution)/shard_map/ppermute | solution.py:37
  84.8 7.8 %collective-permute-start.16 = (bf16[2,32,2048]{2,1,0:T(8,128)(2,1)S(1)}, bf16[2,32,2048]{2,1,0:T(8,128)(2,1)S(1)}, u32[]{:S(2)}, u32[]{:S(2)}) collective-permute-start(bf16[2,32,2048]{2,1,0:T(8,128)(2,1)S(1)} %slice_bitcast_fusion.8), channel_id=1, source_target_pairs={{0,1},{1,2},{2,3},{3,0},{4,5},{5,6},{6,7},{7,4},{8,9},{9,10},{10,1... | collective-permute-start | bytes 786440 | tf_op jit(solution)/shard_map/ppermute | solution.py:47
  85.3 7.3 %collective-permute-start.17 = (bf16[2,32,2048]{2,1,0:T(8,128)(2,1)S(1)}, bf16[2,32,2048]{2,1,0:T(8,128)(2,1)S(1)}, u32[]{:S(2)}, u32[]{:S(2)}) collective-permute-start(bf16[2,32,2048]{2,1,0:T(8,128)(2,1)S(1)} %get-tuple-element.253), channel_id=1, source_target_pairs={{0,3},{1,0},{2,1},{3,2},{4,7},{5,4},{6,5},{7,6},{8,11},{9,8},{10,9... | collective-permute-start | bytes 786440 | tf_op jit(solution)/shard_map/ppermute | solution.py:47
  100.6 46.7 %collective-permute-start.22 = (bf16[512,1408]{1,0:T(8,128)(2,1)S(1)}, bf16[512,1408]{1,0:T(8,128)(2,1)S(1)}, u32[]{:S(2)}, u32[]{:S(2)}) collective-permute-start(bf16[512,1408]{1,0:T(8,128)(2,1)S(1)} %convolution_convert_fusion.3), channel_id=1, source_target_pairs={{0,8},{4,12},{8,0},{12,4},{1,9},{5,13},{9,1},{13,5},{2,10},{6,14},... | collective-permute-start | bytes 4325384 | tf_op jit(solution)/shard_map/ppermute | solution.py:37
  153.7 12.1 %collective-permute-start.25 = (bf16[256,2048]{1,0:T(8,128)(2,1)S(1)}, bf16[256,2048]{1,0:T(8,128)(2,1)S(1)}, u32[]{:S(2)}, u32[]{:S(2)}) collective-permute-start(bf16[256,2048]{1,0:T(8,128)(2,1)S(1)} %slice.709), channel_id=1, source_target_pairs={{0,4},{4,0},{8,12},{12,8},{1,5},{5,1},{9,13},{13,9},{2,6},{6,2},{1... | collective-permute-start | bytes 3145736 | tf_op jit(solution)/shard_map/ppermute | solution.py:37
  153.8 11.3 %collective-permute-start.23 = (bf16[128,1408]{1,0:T(8,128)(2,1)S(1)}, bf16[128,1408]{1,0:T(8,128)(2,1)S(1)}, u32[]{:S(2)}, u32[]{:S(2)}) collective-permute-start(bf16[128,1408]{1,0:T(8,128)(2,1)S(1)} %get-tuple-element.266), channel_id=1, source_target_pairs={{0,8},{4,12},{8,0},{12,4},{1,9},{5,13},{9,1},{13,5},{2,10},{6,14},... | collective-permute-start | bytes 1081352 | tf_op jit(solution)/shard_map/ppermute | solution.py:37
  154.2 18.1 %collective-permute-start.24 = (bf16[128,1408]{1,0:T(8,128)(2,1)S(1)}, bf16[128,1408]{1,0:T(8,128)(2,1)S(1)}, u32[]{:S(2)}, u32[]{:S(2)}) collective-permute-start(bf16[128,1408]{1,0:T(8,128)(2,1)S(1)} %get-tuple-element.270), channel_id=1, source_target_pairs={{0,8},{4,12},{8,0},{12,4},{1,9},{5,13},{9,1},{13,5},{2,10},{6,14},... | collective-permute-start | bytes 1081352 | tf_op jit(solution)/shard_map/ppermute | solution.py:37
  174.0 9.1 %collective-permute-start.28 = (bf16[2,32,2048]{2,1,0:T(8,128)(2,1)}, bf16[2,32,2048]{2,1,0:T(8,128)(2,1)S(1)}, u32[]{:S(2)}, u32[]{:S(2)}) collective-permute-start(bf16[2,32,2048]{2,1,0:T(8,128)(2,1)} %pad_maximum_fusion.19), channel_id=1, source_target_pairs={{0,1},{1,2},{2,3},{3,0},{4,5},{5,6},{6,7},{7,4},{8,9},{9,10},{10,1... | collective-permute-start | bytes 786440 | tf_op jit(solution)/shard_map/ppermute | solution.py:47
  174.7 8.4 %collective-permute-start.29 = (bf16[2,32,2048]{2,1,0:T(8,128)(2,1)}, bf16[2,32,2048]{2,1,0:T(8,128)(2,1)}, u32[]{:S(2)}, u32[]{:S(2)}) collective-permute-start(bf16[2,32,2048]{2,1,0:T(8,128)(2,1)} %pad_maximum_fusion.20), channel_id=1, source_target_pairs={{0,3},{1,0},{2,1},{3,2},{4,7},{5,4},{6,5},{7,6},{8,11},{9,8},{10,9... | collective-permute-start | bytes 786440 | tf_op jit(solution)/shard_map/ppermute | solution.py:47
  177.3 11.6 %collective-permute-start.20 = (bf16[128,1408]{1,0:T(8,128)(2,1)}, bf16[128,1408]{1,0:T(8,128)(2,1)S(1)}, u32[]{:S(2)}, u32[]{:S(2)}) collective-permute-start(bf16[128,1408]{1,0:T(8,128)(2,1)} %get-tuple-element.260), channel_id=1, source_target_pairs={{0,8},{4,12},{8,0},{12,4},{1,9},{5,13},{9,1},{13,5},{2,10},{6,14},... | collective-permute-start | bytes 1081352 | tf_op jit(solution)/shard_map/ppermute | solution.py:37
  177.8 18.0 %collective-permute-start.31 = (bf16[128,1408]{1,0:T(8,128)(2,1)S(1)}, bf16[128,1408]{1,0:T(8,128)(2,1)S(1)}, u32[]{:S(2)}, u32[]{:S(2)}) collective-permute-start(bf16[128,1408]{1,0:T(8,128)(2,1)S(1)} %get-tuple-element.276), channel_id=1, source_target_pairs={{0,8},{4,12},{8,0},{12,4},{1,9},{5,13},{9,1},{13,5},{2,10},{6,14},... | collective-permute-start | bytes 1081352 | tf_op jit(solution)/shard_map/ppermute | solution.py:37
  184.2 13.0 %collective-permute-start.30 = (bf16[32,2048]{1,0:T(8,128)(2,1)S(1)}, bf16[32,2048]{1,0:T(8,128)(2,1)S(1)}, u32[]{:S(2)}, u32[]{:S(2)}) collective-permute-start(bf16[32,2048]{1,0:T(8,128)(2,1)S(1)} %get-tuple-element.283), channel_id=1, source_target_pairs={{0,8},{4,12},{8,0},{12,4},{1,9},{5,13},{9,1},{13,5},{2,10},{6,14},... | collective-permute-start | bytes 393224 | tf_op jit(solution)/shard_map/ppermute | solution.py:37
  198.3 10.9 %collective-permute-start.33 = (bf16[32,4096]{1,0:T(8,128)(2,1)S(1)}, bf16[32,4096]{1,0:T(8,128)(2,1)S(1)}, u32[]{:S(2)}, u32[]{:S(2)}) collective-permute-start(bf16[32,4096]{1,0:T(8,128)(2,1)S(1)} %get-tuple-element.290), channel_id=1, source_target_pairs={{16,0},{32,16},{48,32},{64,48},{80,64},{96,80},{112,96},{17,1},{33... | collective-permute-start | bytes 786440 | tf_op jit(solution)/shard_map/ppermute | solution.py:37
  208.6 58.8 %collective-permute-start.49 = (bf16[512,1408]{1,0:T(8,128)(2,1)S(1)}, bf16[512,1408]{1,0:T(8,128)(2,1)S(1)}, u32[]{:S(2)}, u32[]{:S(2)}) collective-permute-start(bf16[512,1408]{1,0:T(8,128)(2,1)S(1)} %copy-done.11), channel_id=1, source_target_pairs={{0,4},{4,0},{8,12},{12,8},{1,5},{5,1},{9,13},{13,9},{2,6},{6,2},{1... | collective-permute-start | bytes 4325384 | tf_op jit(solution)/shard_map/ppermute | solution.py:37
  209.1 59.3 %collective-permute-start.48 = (bf16[512,1408]{1,0:T(8,128)(2,1)S(1)}, bf16[512,1408]{1,0:T(8,128)(2,1)S(1)}, u32[]{:S(2)}, u32[]{:S(2)}) collective-permute-start(bf16[512,1408]{1,0:T(8,128)(2,1)S(1)} %copy-done.10), channel_id=1, source_target_pairs={{0,4},{4,0},{8,12},{12,8},{1,5},{5,1},{9,13},{13,9},{2,6},{6,2},{1... | collective-permute-start | bytes 4325384 | tf_op jit(solution)/shard_map/ppermute | solution.py:37
  210.2 44.1 %collective-permute-start.46 = (bf16[256,1408]{1,0:T(8,128)(2,1)S(1)}, bf16[256,1408]{1,0:T(8,128)(2,1)S(1)}, u32[]{:S(2)}, u32[]{:S(2)}) collective-permute-start(bf16[256,1408]{1,0:T(8,128)(2,1)S(1)} %get-tuple-element.300), channel_id=1, source_target_pairs={{0,8},{4,12},{8,0},{12,4},{1,9},{5,13},{9,1},{13,5},{2,10},{6,14},... | collective-permute-start | bytes 2162696 | tf_op jit(solution)/shard_map/ppermute | solution.py:37
  212.4 10.1 %collective-permute-start.35 = (bf16[32,2048]{1,0:T(8,128)(2,1)S(1)}, bf16[32,2048]{1,0:T(8,128)(2,1)S(1)}, u32[]{:S(2)}, u32[]{:S(2)}) collective-permute-start(bf16[32,2048]{1,0:T(8,128)(2,1)S(1)} %get-tuple-element.303), channel_id=1, source_target_pairs={{0,3},{1,0},{2,1},{3,2},{4,7},{5,4},{6,5},{7,6},{8,11},{9,8},{10,9... | collective-permute-start | bytes 393224 | tf_op jit(solution)/shard_map/ppermute | solution.py:47
  222.5 8.8 %collective-permute-start.40 = (bf16[2,1,32,2048]{3,2,1,0:T(8,128)(2,1)S(1)}, bf16[2,1,32,2048]{3,2,1,0:T(8,128)(2,1)S(1)}, u32[]{:S(2)}, u32[]{:S(2)}) collective-permute-start(bf16[2,1,32,2048]{3,2,1,0:T(8,128)(2,1)S(1)} %get-tuple-element.306), channel_id=1, source_target_pairs={{0,3},{1,0},{2,1},{3,2},{4,7},{5,4},{6,5},{7,6},{8,11},{9,8},{10,9... | collective-permute-start | bytes 786440 | tf_op jit(solution)/shard_map/ppermute | solution.py:47
  222.5 7.6 %collective-permute-start.39 = (bf16[2,1,32,2048]{3,2,0,1:T(8,128)(2,1)S(1)}, bf16[2,1,32,2048]{3,2,0,1:T(8,128)(2,1)S(1)}, u32[]{:S(2)}, u32[]{:S(2)}) collective-permute-start(bf16[2,1,32,2048]{3,2,0,1:T(8,128)(2,1)S(1)} %bitcast.344), channel_id=1, source_target_pairs={{0,1},{1,2},{2,3},{3,0},{4,5},{5,6},{6,7},{7,4},{8,9},{9,10},{10,1... | collective-permute-start | bytes 786440 | tf_op jit(solution)/shard_map/ppermute | solution.py:47
  230.1 8.0 %collective-permute-start.37 = (bf16[2,32,2048]{2,1,0:T(8,128)(2,1)S(1)}, bf16[2,32,2048]{2,1,0:T(8,128)(2,1)S(1)}, u32[]{:S(2)}, u32[]{:S(2)}) collective-permute-start(bf16[2,32,2048]{2,1,0:T(8,128)(2,1)S(1)} %pad_maximum_fusion.22), channel_id=1, source_target_pairs={{0,1},{1,2},{2,3},{3,0},{4,5},{5,6},{6,7},{7,4},{8,9},{9,10},{10,1... | collective-permute-start | bytes 786440 | tf_op jit(solution)/shard_map/ppermute | solution.py:47
  231.3 7.8 %collective-permute-start.38 = (bf16[2,32,2048]{2,1,0:T(8,128)(2,1)S(1)}, bf16[2,32,2048]{2,1,0:T(8,128)(2,1)S(1)}, u32[]{:S(2)}, u32[]{:S(2)}) collective-permute-start(bf16[2,32,2048]{2,1,0:T(8,128)(2,1)S(1)} %pad_maximum_fusion.23), channel_id=1, source_target_pairs={{0,3},{1,0},{2,1},{3,2},{4,7},{5,4},{6,5},{7,6},{8,11},{9,8},{10,9... | collective-permute-start | bytes 786440 | tf_op jit(solution)/shard_map/ppermute | solution.py:47
  244.2 15.5 %collective-permute-start.45 = (bf16[256,1408]{1,0:T(8,128)(2,1)S(1)}, bf16[256,1408]{1,0:T(8,128)(2,1)S(1)}, u32[]{:S(2)}, u32[]{:S(2)}) collective-permute-start(bf16[256,1408]{1,0:T(8,128)(2,1)S(1)} %get-tuple-element.299), channel_id=1, source_target_pairs={{0,8},{4,12},{8,0},{12,4},{1,9},{5,13},{9,1},{13,5},{2,10},{6,14},... | collective-permute-start | bytes 2162696 | tf_op jit(solution)/shard_map/ppermute | solution.py:37
  247.5 15.0 %collective-permute-start.41 = (bf16[32,2048]{1,0:T(8,128)(2,1)S(1)}, bf16[32,2048]{1,0:T(8,128)(2,1)S(1)}, u32[]{:S(2)}, u32[]{:S(2)}) collective-permute-start(bf16[32,2048]{1,0:T(8,128)(2,1)S(1)} %get-tuple-element.316), channel_id=1, source_target_pairs={{0,8},{4,12},{8,0},{12,4},{1,9},{5,13},{9,1},{13,5},{2,10},{6,14},... | collective-permute-start | bytes 393224 | tf_op jit(solution)/shard_map/ppermute | solution.py:37
  254.4 28.2 %collective-permute-start.51 = (bf16[256,1408]{1,0:T(8,128)(2,1)S(1)}, bf16[256,1408]{1,0:T(8,128)(2,1)S(1)}, u32[]{:S(2)}, u32[]{:S(2)}) collective-permute-start(bf16[256,1408]{1,0:T(8,128)(2,1)S(1)} %get-tuple-element.322), channel_id=1, source_target_pairs={{0,8},{4,12},{8,0},{12,4},{1,9},{5,13},{9,1},{13,5},{2,10},{6,14},... | collective-permute-start | bytes 2162696 | tf_op jit(solution)/shard_map/ppermute | solution.py:37
  263.1 13.6 %collective-permute-start.47 = (bf16[32,4096]{1,0:T(8,128)(2,1)S(1)}, bf16[32,4096]{1,0:T(8,128)(2,1)S(1)}, u32[]{:S(2)}, u32[]{:S(2)}) collective-permute-start(bf16[32,4096]{1,0:T(8,128)(2,1)S(1)} %shard_map.158), channel_id=1, source_target_pairs={{0,16},{16,32},{32,48},{48,64},{64,80},{80,96},{96,112},{1,17},{17... | collective-permute-start | bytes 786440 | tf_op jit(solution)/shard_map/ppermute | solution.py:37
  282.6 9.9 %collective-permute-start.53 = (bf16[2,1,32,2048]{3,2,1,0:T(8,128)(2,1)S(1)}, bf16[2,1,32,2048]{3,2,1,0:T(8,128)(2,1)S(1)}, u32[]{:S(2)}, u32[]{:S(2)}) collective-permute-start(bf16[2,1,32,2048]{3,2,1,0:T(8,128)(2,1)S(1)} %get-tuple-element.338), channel_id=1, source_target_pairs={{0,3},{1,0},{2,1},{3,2},{4,7},{5,4},{6,5},{7,6},{8,11},{9,8},{10,9... | collective-permute-start | bytes 786440 | tf_op jit(solution)/shard_map/ppermute | solution.py:47
  282.7 9.8 %collective-permute-start.52 = (bf16[2,1,32,2048]{3,2,0,1:T(8,128)(2,1)S(1)}, bf16[2,1,32,2048]{3,2,0,1:T(8,128)(2,1)S(1)}, u32[]{:S(2)}, u32[]{:S(2)}) collective-permute-start(bf16[2,1,32,2048]{3,2,0,1:T(8,128)(2,1)S(1)} %bitcast.345), channel_id=1, source_target_pairs={{0,1},{1,2},{2,3},{3,0},{4,5},{5,6},{6,7},{7,4},{8,9},{9,10},{10,1... | collective-permute-start | bytes 786440 | tf_op jit(solution)/shard_map/ppermute | solution.py:47
  290.8 10.3 %collective-permute-start.56 = (bf16[2,3,32,512]{3,2,1,0:T(8,128)(2,1)S(1)}, bf16[2,3,32,512]{3,2,1,0:T(8,128)(2,1)S(1)}, u32[]{:S(2)}, u32[]{:S(2)}) collective-permute-start(bf16[2,3,32,512]{3,2,1,0:T(8,128)(2,1)S(1)} %get-tuple-element.336), channel_id=1, source_target_pairs={{0,64},{16,80},{32,96},{48,112},{1,65},{17,81},{33,97},{49,113},{2... | collective-permute-start | bytes 589832 | tf_op jit(solution)/shard_map/ppermute | solution.py:37
  292.1 16.7 %collective-permute-start.59 = (bf16[256,1408]{1,0:T(8,128)(2,1)S(1)}, bf16[256,1408]{1,0:T(8,128)(2,1)S(1)}, u32[]{:S(2)}, u32[]{:S(2)}) collective-permute-start(bf16[256,1408]{1,0:T(8,128)(2,1)S(1)} %get-tuple-element.335), channel_id=1, source_target_pairs={{0,8},{4,12},{8,0},{12,4},{1,9},{5,13},{9,1},{13,5},{2,10},{6,14},... | collective-permute-start | bytes 2162696 | tf_op jit(solution)/shard_map/ppermute | solution.py:37
  292.6 8.5 %collective-permute-start.54 = (bf16[1,32,2048]{2,1,0:T(8,128)(2,1)S(1)}, bf16[1,32,2048]{2,1,0:T(8,128)(2,1)S(1)}, u32[]{:S(2)}, u32[]{:S(2)}) collective-permute-start(bf16[1,32,2048]{2,1,0:T(8,128)(2,1)S(1)} %slice_bitcast_fusion.31), channel_id=1, source_target_pairs={{0,1},{1,2},{2,3},{3,0},{4,5},{5,6},{6,7},{7,4},{8,9},{9,10},{10,1... | collective-permute-start | bytes 393224 | tf_op jit(solution)/shard_map/ppermute | solution.py:47
  293.5 7.6 %collective-permute-start.55 = (bf16[1,32,2048]{2,1,0:T(8,128)(2,1)S(1)}, bf16[1,32,2048]{2,1,0:T(8,128)(2,1)S(1)}, u32[]{:S(2)}, u32[]{:S(2)}) collective-permute-start(bf16[1,32,2048]{2,1,0:T(8,128)(2,1)S(1)} %slice_bitcast_fusion.30), channel_id=1, source_target_pairs={{0,3},{1,0},{2,1},{3,2},{4,7},{5,4},{6,5},{7,6},{8,11},{9,8},{10,9... | collective-permute-start | bytes 393224 | tf_op jit(solution)/shard_map/ppermute | solution.py:47
  315.2 15.1 %collective-permute-start.67 = (bf16[256,2048]{1,0:T(8,128)(2,1)S(1)}, bf16[256,2048]{1,0:T(8,128)(2,1)S(1)}, u32[]{:S(2)}, u32[]{:S(2)}) collective-permute-start(bf16[256,2048]{1,0:T(8,128)(2,1)S(1)} %slice.707), channel_id=1, source_target_pairs={{0,4},{4,0},{8,12},{12,8},{1,5},{5,1},{9,13},{13,9},{2,6},{6,2},{1... | collective-permute-start | bytes 3145736 | tf_op jit(solution)/shard_map/ppermute | solution.py:37
  315.4 10.7 %collective-permute-start.58 = (bf16[128,1408]{1,0:T(8,128)(2,1)S(1)}, bf16[128,1408]{1,0:T(8,128)(2,1)S(1)}, u32[]{:S(2)}, u32[]{:S(2)}) collective-permute-start(bf16[128,1408]{1,0:T(8,128)(2,1)S(1)} %get-tuple-element.350), channel_id=1, source_target_pairs={{0,8},{4,12},{8,0},{12,4},{1,9},{5,13},{9,1},{13,5},{2,10},{6,14},... | collective-permute-start | bytes 1081352 | tf_op jit(solution)/shard_map/ppermute | solution.py:37
  316.5 19.1 %collective-permute-start.65 = (bf16[2,3,32,512]{3,2,1,0:T(8,128)(2,1)S(1)}, bf16[2,3,32,512]{3,2,1,0:T(8,128)(2,1)S(1)}, u32[]{:S(2)}, u32[]{:S(2)}) collective-permute-start(bf16[2,3,32,512]{3,2,1,0:T(8,128)(2,1)S(1)} %collective-permute-done.56.refs_0_), channel_id=1, source_target_pairs={{64,96},{80,112},{96,64},{112,80},{65,97},{81,113},{97,65},{113,81... | collective-permute-start | bytes 589832 | tf_op jit(solution)/shard_map/ppermute | solution.py:37
  321.3 15.5 %collective-permute-start.64 = (bf16[2,3,32,512]{3,2,1,0:T(8,128)(2,1)S(1)}, bf16[2,3,32,512]{3,2,1,0:T(8,128)(2,1)S(1)}, u32[]{:S(2)}, u32[]{:S(2)}) collective-permute-start(bf16[2,3,32,512]{3,2,1,0:T(8,128)(2,1)S(1)} %collective-permute-done.56.refs_0_), channel_id=1, source_target_pairs={{64,112},{80,64},{96,80},{112,96},{65,113},{81,65},{97,81},{113,97... | collective-permute-start | bytes 589832 | tf_op jit(solution)/shard_map/ppermute | solution.py:37
  325.0 15.3 %collective-permute-start.62 = (bf16[512,1408]{1,0:T(8,128)(2,1)S(1)}, bf16[512,1408]{1,0:T(8,128)(2,1)S(1)}, u32[]{:S(2)}, u32[]{:S(2)}) collective-permute-start(bf16[512,1408]{1,0:T(8,128)(2,1)S(1)} %get-tuple-element.362), channel_id=1, source_target_pairs={{0,4},{4,0},{8,12},{12,8},{1,5},{5,1},{9,13},{13,9},{2,6},{6,2},{1... | collective-permute-start | bytes 4325384 | tf_op jit(solution)/shard_map/ppermute | solution.py:37
  326.1 9.5 %collective-permute-start.66 = (bf16[2,3,32,512]{3,2,1,0:T(8,128)(2,1)S(1)}, bf16[2,3,32,512]{3,2,1,0:T(8,128)(2,1)S(1)}, u32[]{:S(2)}, u32[]{:S(2)}) collective-permute-start(bf16[2,3,32,512]{3,2,1,0:T(8,128)(2,1)S(1)} %collective-permute-done.56.refs_0_), channel_id=1, source_target_pairs={{64,80},{80,96},{96,112},{112,64},{65,81},{81,97},{97,113},{113,65... | collective-permute-start | bytes 589832 | tf_op jit(solution)/shard_map/ppermute | solution.py:37
  330.3 33.3 %collective-permute-start.68 = (bf16[128,1408]{1,0:T(8,128)(2,1)}, bf16[128,1408]{1,0:T(8,128)(2,1)}, u32[]{:S(2)}, u32[]{:S(2)}) collective-permute-start(bf16[128,1408]{1,0:T(8,128)(2,1)} %get-tuple-element.459), channel_id=1, source_target_pairs={{0,8},{4,12},{8,0},{12,4},{1,9},{5,13},{9,1},{13,5},{2,10},{6,14},... | collective-permute-start | bytes 1081352 | tf_op jit(solution)/shard_map/ppermute | solution.py:37
  335.6 15.2 %collective-permute-start.61 = (bf16[512,1408]{1,0:T(8,128)(2,1)S(1)}, bf16[512,1408]{1,0:T(8,128)(2,1)S(1)}, u32[]{:S(2)}, u32[]{:S(2)}) collective-permute-start(bf16[512,1408]{1,0:T(8,128)(2,1)S(1)} %get-tuple-element.363), channel_id=1, source_target_pairs={{0,4},{4,0},{8,12},{12,8},{1,5},{5,1},{9,13},{13,9},{2,6},{6,2},{1... | collective-permute-start | bytes 4325384 | tf_op jit(solution)/shard_map/ppermute | solution.py:37
  335.6 13.9 %collective-permute-start.63 = (bf16[128,1408]{1,0:T(8,128)(2,1)}, bf16[128,1408]{1,0:T(8,128)(2,1)S(1)}, u32[]{:S(2)}, u32[]{:S(2)}) collective-permute-start(bf16[128,1408]{1,0:T(8,128)(2,1)} %get-tuple-element.460), channel_id=1, source_target_pairs={{0,8},{4,12},{8,0},{12,4},{1,9},{5,13},{9,1},{13,5},{2,10},{6,14},... | collective-permute-start | bytes 1081352 | tf_op jit(solution)/shard_map/ppermute | solution.py:37
  336.8 14.0 %collective-permute-start.70 = (bf16[32,2048]{1,0:T(8,128)(2,1)S(1)}, bf16[32,2048]{1,0:T(8,128)(2,1)S(1)}, u32[]{:S(2)}, u32[]{:S(2)}) collective-permute-start(bf16[32,2048]{1,0:T(8,128)(2,1)S(1)} %get-tuple-element.375), channel_id=1, source_target_pairs={{0,3},{1,0},{2,1},{3,2},{4,7},{5,4},{6,5},{7,6},{8,11},{9,8},{10,9... | collective-permute-start | bytes 393224 | tf_op jit(solution)/shard_map/ppermute | solution.py:47
  340.3 10.5 %collective-permute-start.69 = (bf16[32,2048]{1,0:T(8,128)(2,1)S(1)}, bf16[32,2048]{1,0:T(8,128)(2,1)S(1)}, u32[]{:S(2)}, u32[]{:S(2)}) collective-permute-start(bf16[32,2048]{1,0:T(8,128)(2,1)S(1)} %get-tuple-element.383), channel_id=1, source_target_pairs={{0,1},{1,2},{2,3},{3,0},{4,5},{5,6},{6,7},{7,4},{8,9},{9,10},{10,1... | collective-permute-start | bytes 393224 | tf_op jit(solution)/shard_map/ppermute | solution.py:47
  349.6 14.1 %collective-permute-start.60 = (bf16[128,1408]{1,0:T(8,128)(2,1)S(1)}, bf16[128,1408]{1,0:T(8,128)(2,1)S(1)}, u32[]{:S(2)}, u32[]{:S(2)}) collective-permute-start(bf16[128,1408]{1,0:T(8,128)(2,1)S(1)} %get-tuple-element.353), channel_id=1, source_target_pairs={{0,8},{4,12},{8,0},{12,4},{1,9},{5,13},{9,1},{13,5},{2,10},{6,14},... | collective-permute-start | bytes 1081352 | tf_op jit(solution)/shard_map/ppermute | solution.py:37
  360.4 11.8 %collective-permute-start.73 = (bf16[2,32,2048]{2,1,0:T(8,128)(2,1)S(1)}, bf16[2,32,2048]{2,1,0:T(8,128)(2,1)S(1)}, u32[]{:S(2)}, u32[]{:S(2)}) collective-permute-start(bf16[2,32,2048]{2,1,0:T(8,128)(2,1)S(1)} %pad_maximum_fusion.26), channel_id=1, source_target_pairs={{0,3},{1,0},{2,1},{3,2},{4,7},{5,4},{6,5},{7,6},{8,11},{9,8},{10,9... | collective-permute-start | bytes 786440 | tf_op jit(solution)/shard_map/ppermute | solution.py:47
  363.6 8.5 %collective-permute-start.72 = (bf16[2,32,2048]{2,1,0:T(8,128)(2,1)S(1)}, bf16[2,32,2048]{2,1,0:T(8,128)(2,1)S(1)}, u32[]{:S(2)}, u32[]{:S(2)}) collective-permute-start(bf16[2,32,2048]{2,1,0:T(8,128)(2,1)S(1)} %pad_maximum_fusion.25), channel_id=1, source_target_pairs={{0,1},{1,2},{2,3},{3,0},{4,5},{5,6},{6,7},{7,4},{8,9},{9,10},{10,1... | collective-permute-start | bytes 786440 | tf_op jit(solution)/shard_map/ppermute | solution.py:47
  368.4 11.3 %collective-permute-start.71 = (bf16[256,2048]{1,0:T(8,128)(2,1)S(1)}, bf16[256,2048]{1,0:T(8,128)(2,1)S(1)}, u32[]{:S(2)}, u32[]{:S(2)}) collective-permute-start(bf16[256,2048]{1,0:T(8,128)(2,1)S(1)} %slice.706), channel_id=1, source_target_pairs={{0,4},{4,0},{8,12},{12,8},{1,5},{5,1},{9,13},{13,9},{2,6},{6,2},{1... | collective-permute-start | bytes 3145736 | tf_op jit(solution)/shard_map/ppermute | solution.py:37
  380.2 6.8 %collective-permute-start.75 = (bf16[32,2048]{1,0:T(8,128)(2,1)S(1)}, bf16[32,2048]{1,0:T(8,128)(2,1)S(1)}, u32[]{:S(2)}, u32[]{:S(2)}) collective-permute-start(bf16[32,2048]{1,0:T(8,128)(2,1)S(1)} %get-tuple-element.404), channel_id=1, source_target_pairs={{0,1},{1,2},{2,3},{3,0},{4,5},{5,6},{6,7},{7,4},{8,9},{9,10},{10,1... | collective-permute-start | bytes 393224 | tf_op jit(solution)/shard_map/ppermute | solution.py:47
  387.1 8.8 %collective-permute-start.78 = (bf16[2,32,2048]{2,1,0:T(8,128)(2,1)S(1)}, bf16[2,32,2048]{2,1,0:T(8,128)(2,1)S(1)}, u32[]{:S(2)}, u32[]{:S(2)}) collective-permute-start(bf16[2,32,2048]{2,1,0:T(8,128)(2,1)S(1)} %pad_maximum_fusion.27), channel_id=1, source_target_pairs={{0,1},{1,2},{2,3},{3,0},{4,5},{5,6},{6,7},{7,4},{8,9},{9,10},{10,1... | collective-permute-start | bytes 786440 | tf_op jit(solution)/shard_map/ppermute | solution.py:47
  387.2 8.7 %collective-permute-start.79 = (bf16[2,32,2048]{2,1,0:T(8,128)(2,1)S(1)}, bf16[2,32,2048]{2,1,0:T(8,128)(2,1)S(1)}, u32[]{:S(2)}, u32[]{:S(2)}) collective-permute-start(bf16[2,32,2048]{2,1,0:T(8,128)(2,1)S(1)} %pad_maximum_fusion.28), channel_id=1, source_target_pairs={{0,3},{1,0},{2,1},{3,2},{4,7},{5,4},{6,5},{7,6},{8,11},{9,8},{10,9... | collective-permute-start | bytes 786440 | tf_op jit(solution)/shard_map/ppermute | solution.py:47
  397.0 8.9 %collective-permute-start.80 = (bf16[32,2048]{1,0:T(8,128)(2,1)S(1)}, bf16[32,2048]{1,0:T(8,128)(2,1)S(1)}, u32[]{:S(2)}, u32[]{:S(2)}) collective-permute-start(bf16[32,2048]{1,0:T(8,128)(2,1)S(1)} %get-tuple-element.413), channel_id=1, source_target_pairs={{0,8},{4,12},{8,0},{12,4},{1,9},{5,13},{9,1},{13,5},{2,10},{6,14},... | collective-permute-start | bytes 393224 | tf_op jit(solution)/shard_map/ppermute | solution.py:37
  (62 other events, 439.9 us)
